TPU v7x, 512 devices: a whole 4x4x16 slice. The times are simulated.
512 devices in a mesh: rep: 32 (over z, x_lo), gz: 16 (over x_hi, y, core).
Axes of the slice: x: 4 (x_hi: 2, x_lo: 2; x = x_hi * 2 + x_lo), y: 4, z: 16, core: 2. Of those that a mesh axis runs over, the one named last changes fastest.
Arguments:
- lattice_field: float32 [192, 64, 4096], P('rep', 'gz'), may hold values from -4 to 4
- langevin_noise: float32 [2, 192, 64, 4096], P(None, 'rep', 'gz'), may hold values from -5 to 5
- masses: float32 [64, 4096], P('gz'), may hold values from -2 to 2
- counts: int32 [192], replicated, may hold values from 0 to 49, as said below
- dest_slots: int32 [192], replicated, may hold values from 0 to 191, each once
- mode_bins: int32 [64, 64, 33], P('gz'), may hold values from 0 to 15, as said below
Outputs:
- resampled: float32 [192, 64, 4096], P('rep', 'gz')
- propagator: float32 [192, 16], P('rep')
Inputs may be any that keep to these rules, and one draw needn't show every extreme that they name: The counts sum to 192; in each aligned block of 6 replicas (those of one index of rep) at most 3 counts are nonzero, and exactly 3 in some block. `dest_slots`: A permutation of the 192 slots. `mode_bins`: the bin depends only on n_y^2 + n_z^2 + kx^2 with n = min(k, 64 - k), and never falls as that grows; every bin holds at least one mode.
All inputs are finite; a program needn't handle non-finite values.
Results may differ from a plain program's by a relative error of at most 0.00007.
Values sent between devices are 32-bit elements; how exact they have to be, the bound alone decides.
No kernel may reach another device: no remote copies, remote signals or barrier semaphores. Data moves between devices by JAX's collectives and lax.ppermute only.
A program may use at most 64 MiB of HBM per device.

v0:
```python
import jax
import jax.numpy as jnp
from jax import lax
from jax.sharding import PartitionSpec as P

L = 64
SWEEPS = 2
NBINS = 16


step_size = 0.1
quartic = 0.5


def with_halo(block, sides, width):
    for axis, dim in sides:
        count = lax.axis_size(axis)
        forward = [(i, i + 1) for i in range(count - 1)]
        forward.append((count - 1, 0))
        backward = [(target, source) for source, target in forward]
        low = lax.ppermute(
            lax.slice_in_dim(block, block.shape[dim] - width, None, axis=dim), axis, forward
        )
        high = lax.ppermute(lax.slice_in_dim(block, 0, width, axis=dim), axis, backward)
        block = jnp.concatenate([low, block, high], axis=dim)
    return block


def in_plane(center):
    grid = center.reshape(center.shape[0], center.shape[1], L, L)
    across = jnp.roll(grid, 1, axis=3) + jnp.roll(grid, -1, axis=3)
    return jnp.roll(center, L, axis=2) + jnp.roll(center, -L, axis=2) + across.reshape(center.shape)


def update(center, below, above, site_masses, noise_now):
    beside = below + above + in_plane(center)
    drift = 6.0 * center - beside + site_masses[None] * center + quartic * center * center * center
    return center - step_size * drift + jnp.sqrt(2.0 * step_size) * noise_now


def angle_tables(rows, columns):
    product = jnp.arange(rows)[:, None] * jnp.arange(columns)[None, :] % L
    theta = 2.0 * jnp.pi / L * product.astype(jnp.float32)
    return (jnp.cos(theta), jnp.sin(theta))


def make_weights(mode_bins):
    half = L // 2 + 1
    ordered = jnp.transpose(mode_bins, (1, 0, 2))
    wave_x = jnp.arange(half)
    weight_x = jnp.where((wave_x == 0) | (wave_x == L // 2), 1.0, 2.0).astype(jnp.float32)
    onehot = (ordered[..., None] == jnp.arange(NBINS)[None, None, None, :]).astype(jnp.float32)
    return (onehot * weight_x[None, None, :, None]).reshape(-1, NBINS)


def transform(slabs, weights):
    half = L // 2 + 1
    exact = lax.Precision.HIGHEST
    cos_half, sin_half = angle_tables(L, half)
    cos_full, sin_full = angle_tables(L, L)
    along_x = jnp.concatenate([cos_half, -sin_half], axis=1)
    count, depth = (slabs.shape[0], slabs.shape[1])
    grid = slabs.reshape(count, depth, L, L)
    first = jnp.einsum("nzyx,xk->nzyk", grid, along_x, precision=exact)
    real_x, imag_x = (first[..., :half], first[..., half:])
    real_y = jnp.einsum("qy,nzyk->nzqk", cos_full, real_x, precision=exact) + jnp.einsum(
        "qy,nzyk->nzqk", sin_full, imag_x, precision=exact
    )
    imag_y = jnp.einsum("qy,nzyk->nzqk", cos_full, imag_x, precision=exact) - jnp.einsum(
        "qy,nzyk->nzqk", sin_full, real_x, precision=exact
    )
    merged = jnp.concatenate([real_y, imag_y], axis=3).reshape(count, depth, L * 2 * half)
    block = lax.all_to_all(merged, "gz", split_axis=2, concat_axis=1, tiled=True)
    items = block.shape[0]
    pencil = block.reshape(items, L, -1, 2 * half)
    real_p = pencil[..., :half]
    imag_p = pencil[..., half:]
    real_z = jnp.einsum("pz,mzqk->mpqk", cos_full, real_p, precision=exact) + jnp.einsum(
        "pz,mzqk->mpqk", sin_full, imag_p, precision=exact
    )
    imag_z = jnp.einsum("pz,mzqk->mpqk", cos_full, imag_p, precision=exact) - jnp.einsum(
        "pz,mzqk->mpqk", sin_full, real_p, precision=exact
    )
    power = real_z * real_z + imag_z * imag_z
    binned = jnp.dot(power.reshape(items, -1), weights, precision=exact)
    binned_total, weight_total = lax.psum((binned, jnp.sum(weights, axis=0)), "gz")
    return binned_total / (float(L**3) * weight_total)


def local(lattice_field, langevin_noise, masses, counts, dest_slots, mode_bins):
    local_count = lattice_field.shape[0]
    weights = make_weights(mode_bins)
    swept = lattice_field
    for turn in range(SWEEPS):
        padded = with_halo(swept, (("gz", 1),), 1)
        swept = update(padded[:, 1:-1], padded[:, :-2], padded[:, 2:], masses, langevin_noise[turn])
    base = lax.axis_index("rep") * local_count
    ends = jnp.cumsum(counts)
    position = jnp.argsort(dest_slots)
    mine_position = lax.dynamic_slice_in_dim(position, base, local_count)
    mine_source = jnp.sum((ends[None, :] <= mine_position[:, None]).astype(jnp.int32), axis=1)
    empty = jnp.zeros_like(swept)
    piece = lax.all_gather(swept, "rep", axis=0, tiled=True)
    found = (mine_source >= 0) & (mine_source < piece.shape[0])
    chosen = jnp.take(piece, jnp.clip(mine_source, 0, piece.shape[0] - 1), axis=0)
    resampled = jnp.where(found[:, None, None], chosen, empty)
    propagator = transform(resampled, weights)
    return (resampled, propagator)


def solution(mesh):
    in_specs = (
        P("rep", "gz", None),
        P(None, "rep", "gz", None),
        P("gz", None),
        P(),
        P(),
        P("gz", None, None),
    )
    out_specs = (P("rep", "gz", None), P("rep", None))
    return jax.shard_map(local, mesh=mesh, in_specs=in_specs, out_specs=out_specs, check_vma=False)
```

profile of v0, /device:TPU:38, one launch (start us, length us, event | category | flops | bytes accessed | tf_op | source)
XLA Modules:
  0.0 452.3 jit_solution(2166895266252879648)
XLA Ops:
  7.2 1.3 fusion.124
  8.5 1.9 collective-permute-start
  10.4 7.3 %collective-permute-start.1 = (f32[6,1,4096]{2,1,0:T(1,128)S(1)}, f32[6,1,4096]{2,1,0:T(1,128)S(1)}, u32[]{:S(2)}, u32[]{:S(2)}) collective-permute-start(f32[6,1,4096]{2,1,0:T(1,128)S(1)} %get-tuple-element.27), channel_id=1, source_target_pairs={{1,0},{2,1},{3,2},{4,3},{5,4},{6,5},{7,6},{8,7},{9,8},{10,9},{11,1... | collective-permute-start | bytes 294920 | tf_op jit(solution)/shard_map/ppermute | solution.py:24
  17.7 1.4 reshape.93
  19.1 0.3 fusion.117
  19.4 0.3 fusion.118
  19.7 0.7 copy-done
  20.4 0.3 fusion.122
  20.7 0.7 fusion.123
  21.3 0.5 maximum_add_fusion
  21.8 0.3 add.129
  22.2 0.6 copy-done.4
  22.8 0.1 copy-done.1
  23.0 1.8 fusion.23
  24.7 0.4 reshape.94
  25.1 0.3 fusion.116
  25.4 0.3 fusion.115
  25.7 0.3 fusion.119
  26.0 0.8 fusion.121
  26.9 0.1 fusion.120
  26.9 1.9 collective-permute-start.2
  28.8 7.4 %collective-permute-start.3 = (f32[6,1,4096]{2,1,0:T(1,128)}, f32[6,1,4096]{2,1,0:T(1,128)S(1)}, u32[]{:S(2)}, u32[]{:S(2)}) collective-permute-start(f32[6,1,4096]{2,1,0:T(1,128)} %get-tuple-element.21), channel_id=1, source_target_pairs={{1,0},{2,1},{3,2},{4,3},{5,4},{6,5},{7,6},{8,7},{9,8},{10,9},{11,1... | collective-permute-start | bytes 294920 | tf_op jit(solution)/shard_map/ppermute | solution.py:24
  36.3 0.5 maximum_add_fusion.1
  36.8 0.3 add.138
  37.1 1.5 collective-permute-done.3
  38.6 1.6 fusion.27
  40.2 0.1 copy.56
  40.4 0.3 reduce-window.9
  40.9 0.2 mul.221
  41.1 0.2 eq.57
  41.3 3.2 sort.17
  44.6 0.1 slice_reduce_fusion
  44.8 0.2 convert_reduce_fusion
  45.0 0.1 sine_negate_fusion
  45.1 0.2 select_reduce_fusion
  45.3 281.6 %all-gather.2.cloned.1.call-done = f32[192,4,4096]{2,1,0:T(4,128)} async-done(((f32[6,4,4096]{2,1,0:T(4,128)}), f32[192,4,4096]{2,1,0:T(4,128)}) %all-gather.2.cloned.1.call-update) | async-done | bytes 12582928 | tf_op jit(solution)/shard_map/all_gather | solution.py:103
  326.9 5.4 %gather_fusion = f32[6,4,4096]{2,1,0:T(4,128)S(1)} fusion(f32[192,4,4096]{2,1,0:T(4,128)} %all-gather.2.cloned.1.call-done, s32[1024]{0:T(1024)S(1)} %pad_clamp_fusion), kind=kCustom, calls=%fused_computation | custom fusion | bytes 786456 | tf_op jit(solution)/shard_map/jit(_take)/gather | solution.py:105
  332.3 0.4 gather.7
  332.7 0.8 fusion.7
  333.5 1.4 fusion.14
  335.0 1.6 fusion.10
  336.6 1.6 fusion.5
  338.2 1.4 fusion.4
  339.6 0.1 pad_maximum_fusion
  339.7 9.3 %copy.65 = f32[6,4,64,66]{0,1,3,2:T(4,128)} copy(f32[6,4,64,66]{2,3,1,0:T(8,128)S(1)} %pad_maximum_fusion) | data formatting | bytes 811008 | tf_op jit(solution)/shard_map/reshape | solution.py:72
  349.0 12.4 %reshape.110 = f32[16,1,6336]{2,1,0:T(1,128)} reshape(f32[4224,4,6]{2,1,0:T(4,128)} %bitcast.64) | data formatting | bytes 811008
  361.4 7.3 %all-to-all-start = ((f32[16,1,6336]{2,1,0:T(1,128)}), f32[16,1,6336]{2,1,0:T(1,128)S(1)}, u32[]{:S(2)}, u32[]{:S(2)}) async-start(f32[16,1,6336]{2,1,0:T(1,128)} %reshape.110), calls=%async_computation | async-start | bytes 819200 | tf_op jit(solution)/shard_map/all_to_all | solution.py:73
  368.7 0.9 select_select_fusion
  369.6 7.4 %all-to-all-done = f32[16,1,6336]{2,1,0:T(1,128)S(1)} async-done(((f32[16,1,6336]{2,1,0:T(1,128)}), f32[16,1,6336]{2,1,0:T(1,128)S(1)}, u32[]{:S(2)}, u32[]{:S(2)}) %all-to-all-start) | async-done | bytes 405536 | tf_op jit(solution)/shard_map/all_to_all | solution.py:73
  376.9 0.5 broadcast.218
  377.5 1.6 reduce.2
  379.1 15.2 %reshape.111 = f32[4224,4,6]{2,1,0:T(4,128)} reshape(f32[16,6336]{1,0:T(8,128)S(1)} %reduce.2) | data formatting | bytes 811008
  394.3 7.6 %copy.51 = f32[6,4,16,264]{3,1,2,0:T(4,128)S(1)} copy(f32[6,4,16,264]{0,1,3,2:T(4,128)} %bitcast.65) | data formatting | bytes 811008 | tf_op jit(solution)/shard_map/all_to_all | solution.py:73
  401.9 0.6 reshape.96
  402.5 0.5 fusion.114
  402.9 0.3 copy.67
  403.3 0.7 fusion.56
  404.0 0.3 copy.68
  404.3 0.7 fusion.54
  405.0 0.7 fusion.3
  405.7 0.7 fusion.2
  406.4 1.6 convolution_bitcast_fusion
  407.9 36.9 %all-reduce.1 = (f32[6,16]{1,0:T(8,128)S(1)}, f32[16]{0:T(128)S(1)}) all-reduce(f32[6,16]{1,0:T(8,128)S(1)} %convolution_bitcast_fusion, f32[16]{0:T(128)S(1)} %select_reduce_fusion), channel_id=1, replica_groups=mesh['rep'=32,'gz'=16] {'gz'}, use_global_device_ids=true, to_apply=%region_4.5 | all-reduce | flops 112 | bytes 896 | tf_op jit(solution)/shard_map/psum | solution.py:86
  444.9 0.6 broadcast_divide_fusion
  (31 shorter events, 0.5 us)
Async XLA Ops:
  7.2 319.8 %all-gather.2.cloned.1.call-start = ((), (), s32[]{:S(2)}) async-start(), calls=%async_computation.1 | async-start | bytes 12976128 | tf_op jit(solution)/shard_map/all_gather | solution.py:103
  8.5 13.6 %collective-permute-start = (f32[6,1,4096]{2,1,0:T(1,128)S(1)}, f32[6,1,4096]{2,1,0:T(1,128)S(1)}, u32[]{:S(2)}, u32[]{:S(2)}) collective-permute-start(f32[6,1,4096]{2,1,0:T(1,128)S(1)} %get-tuple-element.26), channel_id=1, source_target_pairs={{0,1},{1,2},{2,3},{3,4},{4,5},{5,6},{6,7},{7,8},{8,9},{9,10},{10,1... | collective-permute-start | bytes 294920 | tf_op jit(solution)/shard_map/ppermute | solution.py:21
  10.4 11.7 %collective-permute-start.1 = (f32[6,1,4096]{2,1,0:T(1,128)S(1)}, f32[6,1,4096]{2,1,0:T(1,128)S(1)}, u32[]{:S(2)}, u32[]{:S(2)}) collective-permute-start(f32[6,1,4096]{2,1,0:T(1,128)S(1)} %get-tuple-element.27), channel_id=1, source_target_pairs={{1,0},{2,1},{3,2},{4,3},{5,4},{6,5},{7,6},{8,7},{9,8},{10,9},{11,1... | collective-permute-start | bytes 294920 | tf_op jit(solution)/shard_map/ppermute | solution.py:24
  19.4 1.0 copy-start
  21.8 1.1 copy-start.1
  22.2 0.6 copy-start.4
  22.2 0.7 copy-start.5
  26.9 10.2 %collective-permute-start.2 = (f32[6,1,4096]{2,1,0:T(1,128)}, f32[6,1,4096]{2,1,0:T(1,128)S(1)}, u32[]{:S(2)}, u32[]{:S(2)}) collective-permute-start(f32[6,1,4096]{2,1,0:T(1,128)} %get-tuple-element.20), channel_id=1, source_target_pairs={{0,1},{1,2},{2,3},{3,4},{4,5},{5,6},{6,7},{7,8},{8,9},{9,10},{10,1... | collective-permute-start | bytes 294920 | tf_op jit(solution)/shard_map/ppermute | solution.py:21
  28.8 9.8 %collective-permute-start.3 = (f32[6,1,4096]{2,1,0:T(1,128)}, f32[6,1,4096]{2,1,0:T(1,128)S(1)}, u32[]{:S(2)}, u32[]{:S(2)}) collective-permute-start(f32[6,1,4096]{2,1,0:T(1,128)} %get-tuple-element.21), channel_id=1, source_target_pairs={{1,0},{2,1},{3,2},{4,3},{5,4},{6,5},{7,6},{8,7},{9,8},{10,9},{11,1... | collective-permute-start | bytes 294920 | tf_op jit(solution)/shard_map/ppermute | solution.py:24
  36.8 1.9 copy-start.3
  38.6 1.6 copy-start.2
  38.6 1.8 copy-start.6
  40.2 1.1 copy-start.7
  361.4 15.5 %all-to-all-start = ((f32[16,1,6336]{2,1,0:T(1,128)}), f32[16,1,6336]{2,1,0:T(1,128)S(1)}, u32[]{:S(2)}, u32[]{:S(2)}) async-start(f32[16,1,6336]{2,1,0:T(1,128)} %reshape.110), calls=%async_computation | async-start | bytes 819200 | tf_op jit(solution)/shard_map/all_to_all | solution.py:73
Sparse Core Ops, SparseCore 0:
  40.3 286.5 all-gather.1
where the time goes:
time: 453 us; the launch traced here: 452 us
  waiting for transfers between devices  290 us (64%)
  local copies, waits for them, and re-layouts  61.9 us (14%)
  blocking collectives  36.9 us (8%)
  starting transfers between devices  25.8 us (6%)
  between operations  14.4 us (3%)
  other arithmetic  11.6 us (3%)
  matrix products  11.2 us (2%)
    all_gather x1, waiting for transfers between devices, local(): piece = lax.all_gather(swept, 'rep', axis=0, tiled=True)  282 us
    psum x1, blocking collectives, transform(): lax.psum((binned, jnp.sum(weights, axis=0)), 'gz')  36.9 us
    unnamed x20, local copies, waits for them, and re-layouts  29.8 us
    ppermute x2, starting transfers between devices, with_halo(): lax.ppermute(lax.slice_in_dim(block, 0, width, axis=dim), axis, backward)  14.7 us
    reshape x1, local copies, waits for them, and re-layouts, transform(): jnp.concatenate([real_y, imag_y], axis=3)  9.27 us
  transfers between devices with their start and end apart: 6, of which 3 were waited for; matrix products, arithmetic and copies ran while one was open for 2% of the time, Pallas kernels for 0%

commit v1 on v0

v1 whole, which is shorter than its diff:
```python
import jax
import jax.numpy as jnp
import ml_dtypes
import numpy as np
from jax import lax
from jax.experimental import pallas as pl
from jax.experimental.pallas import tpu as pltpu
from jax.sharding import PartitionSpec as P

L = 64
NBINS = 16
LIVE = 3
DEPTH = 4
ROWS = 32
PER = 6

VMEM = pltpu.VMEM
SMEM = pltpu.SMEM


def split_constant(table):
    table = table.astype(np.float32)
    high = table.astype(ml_dtypes.bfloat16)
    low = (table - high.astype(np.float32)).astype(ml_dtypes.bfloat16)
    return np.stack([high, low])


def real_basis(sine_wave):
    slot = np.arange(L)[:, None]
    site = np.arange(L)[None, :]
    wave = np.where(slot <= L // 2, slot, sine_wave(slot))
    angle = 2.0 * np.pi / L * (wave * site % L)
    basis = np.where(slot <= L // 2, np.cos(angle), np.sin(angle)) * np.sqrt(2.0)
    basis[0] = 1.0
    basis[L // 2] = np.cos(np.pi * np.arange(L))
    return basis / np.sqrt(L)


def tables():
    basis_x = real_basis(lambda slot: slot - L // 2)
    basis_k = real_basis(lambda slot: L - slot)
    along_x = np.einsum("ab,cd,mx->acxdbm", np.eye(2), np.eye(2), basis_x).reshape(256, 256)
    along_y = basis_k.reshape(16, 2, 2, 32, 2).transpose(2, 1, 0, 4, 3).reshape(64, 64)
    along_z = np.einsum("ab,kz->akzb", np.eye(2), basis_k).reshape(128, 128)
    return split_constant(along_x), split_constant(along_y), split_constant(along_z)


def split(value):
    high = value.astype(jnp.bfloat16)
    return high, (value - high.astype(jnp.float32)).astype(jnp.bfloat16)


def dot(a, b):
    return jnp.dot(a, b, preferred_element_type=jnp.float32)


def live_of(counts_ref, base):
    seen = jnp.int32(0)
    live = [jnp.int32(0)] * LIVE
    for j in range(PER):
        alive = counts_ref[base + j] > 0
        for k in range(LIVE):
            live[k] = jnp.where(alive & (seen == k), j, live[k])
        seen = seen + alive.astype(jnp.int32)
    return live


def edges_kernel(base_ref, counts_ref, field, noise, masses, up, down, fbuf, nbuf, mbuf, sems):
    live = live_of(counts_ref, base_ref[0])
    copies = [pltpu.make_async_copy(masses, mbuf, sems.at[2 * LIVE])]
    for k in range(LIVE):
        copies.append(pltpu.make_async_copy(field.at[live[k]], fbuf.at[k], sems.at[2 * k]))
        copies.append(pltpu.make_async_copy(noise.at[0, live[k]], nbuf.at[k], sems.at[2 * k + 1]))
    for copy in copies:
        copy.start()
    for copy in copies:
        copy.wait()
    for k in range(LIVE):
        up[2 * k] = fbuf[k, pl.ds(2, ROWS, stride=DEPTH), :]
        up[2 * k + 1] = fbuf[k, pl.ds(3, ROWS, stride=DEPTH), :]
        down[2 * k] = fbuf[k, pl.ds(0, ROWS, stride=DEPTH), :]
        down[2 * k + 1] = fbuf[k, pl.ds(1, ROWS, stride=DEPTH), :]
        up[2 * LIVE + k] = nbuf[k, pl.ds(3, ROWS, stride=DEPTH), :]
        down[2 * LIVE + k] = nbuf[k, pl.ds(0, ROWS, stride=DEPTH), :]
    up[3 * LIVE] = mbuf[pl.ds(3, ROWS, stride=DEPTH), :]
    down[3 * LIVE] = mbuf[pl.ds(0, ROWS, stride=DEPTH), :]


def floor_div(value, by):
    return jnp.floor((value.astype(jnp.float32) + 0.5) * (1.0 / by)).astype(jnp.int32)


def plan_kernel(counts_ref, slots_ref, bins_ref, item_ref, wide_ref, map_ref):
    total = counts_ref.shape[1]
    row = lax.broadcasted_iota(jnp.int32, (total, total), 0)
    col = lax.broadcasted_iota(jnp.int32, (total, total), 1)
    number = jnp.broadcast_to(counts_ref[...].astype(jnp.float32), (total, total))
    slot = jnp.broadcast_to(slots_ref[...].astype(jnp.float32), (total, total))

    def along(mask, value):
        return jnp.sum(jnp.where(mask, value, 0.0), axis=1, keepdims=True)

    own = along(row == col, number)
    ends = along(col <= row, number)
    slot_column = along(row == col, slot)
    block_row = floor_div(row, PER)
    block_col = floor_div(col, PER)
    rank = along((block_row == block_col) & (col < row) & (number > 0.0), jnp.ones_like(number))
    name = rank + LIVE * block_row[:, :1].astype(jnp.float32)
    position = jnp.sum(
        jnp.where(slot_column == col.astype(jnp.float32), row.astype(jnp.float32), 0.0), axis=0, keepdims=True
    )
    held = (position >= ends - own) & (position < ends)
    item = jnp.sum(jnp.where(held, name, 0.0), axis=0, keepdims=True)
    item_ref[...] = item.astype(jnp.int32)
    devices = total // PER
    to = lax.broadcasted_iota(jnp.int32, (devices, total), 0)
    s = lax.broadcasted_iota(jnp.int32, (devices, total), 1)
    lane = lax.broadcasted_iota(jnp.int32, (devices, 128), 1)
    wide = jnp.full((devices, 128), -1.0, jnp.float32)
    items = jnp.broadcast_to(item, (devices, total))
    for q in range(PER):
        column = jnp.sum(jnp.where(s == to * PER + q, items, 0.0), axis=1, keepdims=True)
        wide = jnp.where((lane >= NBINS * q) & (lane < NBINS * (q + 1)), column, wide)
    wide_ref[...] = wide.astype(jnp.int32)
    lane = lax.broadcasted_iota(jnp.int32, (L, 128), 1)
    for pair in range(2):
        halves = []
        for odd in range(2):
            bins = bins_ref[2 * pair + odd]
            halves.append(jnp.where(lane <= L // 2, bins, pltpu.roll(bins, L // 2, axis=1)))
        map_ref[pair * L : (pair + 1) * L, :] = jnp.where(lane < L, halves[0], pltpu.roll(halves[1], L, axis=1))


def beside(v, lane):
    swapped = pltpu.roll(v, L, axis=1)
    rows = v.shape[0]
    y = swapped + jnp.where(lane < L, pltpu.roll(swapped, 1, axis=0), pltpu.roll(swapped, rows - 1, axis=0))
    inner = lane & (L - 1)
    low = pltpu.roll(jnp.where(inner == L - 1, swapped, v), 1, axis=1)
    high = pltpu.roll(jnp.where(inner == 0, swapped, v), 127, axis=1)
    return y + (low + high)


def sweep_kernel(
    base_ref, counts_ref, field, noise, masses, lo, hi, along_x, along_y, pieces, chunks, fbuf, nbuf, mbuf, sems
):
    live = live_of(counts_ref, base_ref[0])
    first = pltpu.make_async_copy(masses, mbuf, sems.at[3 * LIVE])
    first.start()
    copies = []
    for k in range(LIVE):
        copies.append(
            [
                pltpu.make_async_copy(field.at[live[k]], fbuf.at[k], sems.at[3 * k]),
                pltpu.make_async_copy(noise.at[0, live[k]], nbuf.at[0, k], sems.at[3 * k + 1]),
                pltpu.make_async_copy(noise.at[1, live[k]], nbuf.at[1, k], sems.at[3 * k + 2]),
            ]
        )
        for copy in copies[-1]:
            copy.start()
    first.wait()
    lane = lax.broadcasted_iota(jnp.int32, (ROWS, 128), 1)
    kick = float(np.sqrt(np.float32(0.2)))

    def update(center, below, above, mass, noise_now):
        near = below + above + beside(center, lane)
        return center * (0.4 - 0.1 * mass - 0.05 * (center * center)) + 0.1 * near + kick * noise_now

    def planes(ref, *at):
        return [ref[(*at, pl.ds(z, ROWS, stride=DEPTH), slice(None))] for z in range(DEPTH)]

    mass = [lo[3 * LIVE]] + planes(mbuf) + [hi[3 * LIVE]]
    left = []
    for k in range(LIVE):
        for copy in copies[k]:
            copy.wait()
        old = [lo[2 * k], lo[2 * k + 1]] + planes(fbuf, k) + [hi[2 * k], hi[2 * k + 1]]
        kicks = [lo[2 * LIVE + k]] + planes(nbuf, 0, k) + [hi[2 * LIVE + k]]
        mid = [update(old[p + 1], old[p], old[p + 2], mass[p], kicks[p]) for p in range(DEPTH + 2)]
        kicks = planes(nbuf, 1, k)
        new = [update(mid[p + 1], mid[p], mid[p + 2], mass[p + 1], kicks[p]) for p in range(DEPTH)]
        for z in range(DEPTH):
            pieces[pl.ds(k * DEPTH + z, ROWS, stride=LIVE * DEPTH), :] = new[z]
        left += [jnp.concatenate(new[0:2], axis=1), jnp.concatenate(new[2:4], axis=1)]
    high, low = split(jnp.concatenate(left, axis=0))
    across = dot(high, along_x[0]) + (dot(low, along_x[0]) + dot(high, along_x[1]))
    parts = [across[i * ROWS : (i + 1) * ROWS] for i in range(2 * LIVE)]
    right = jnp.concatenate([jnp.concatenate([p[:, :128], p[:, 128:]], axis=0) for p in parts], axis=1)
    high, low = split(right)
    turned = dot(along_y[0], high) + (dot(along_y[0], low) + dot(along_y[1], high))
    for i in range(2 * LIVE):
        even = turned[:ROWS, 128 * i : 128 * (i + 1)]
        odd = turned[ROWS:, 128 * i : 128 * (i + 1)]
        ready = (
            jnp.where(lane < L, even, pltpu.roll(odd, L, axis=1)),
            jnp.where(lane < L, pltpu.roll(even, L, axis=1), odd),
        )
        for side in range(2):
            for pair in range(2):
                chunks[pl.ds(i * 4 + side * 2 + pair, 16, stride=8 * LIVE), :] = ready[side][16 * pair : 16 * pair + 16]


def bins_kernel(chunks, map_ref, along_z, out, rows):
    place = map_ref[...]
    power = []
    for k in range(LIVE):
        high, low = split(chunks[:, 8 * k : 8 * k + 8, :].reshape(128, 128))
        mode = dot(along_z[0], high) + (dot(along_z[0], low) + dot(along_z[1], high))
        power.append(mode * mode)
    power.append(jnp.ones_like(power[0]))
    for b in range(NBINS):
        here = place == b
        for k in range(LIVE + 1):
            rows[k * NBINS + b : k * NBINS + b + 1, :] = jnp.sum(
                jnp.where(here, power[k], 0.0), axis=0, keepdims=True
            )
    rows[(LIVE + 1) * NBINS :, :] = jnp.zeros((128 - (LIVE + 1) * NBINS, 128), jnp.float32)
    sums = lax.dot_general(
        jnp.ones((8, 128), jnp.float32),
        rows[...],
        (((1,), (1,)), ((), ())),
        precision=lax.Precision.HIGHEST,
        preferred_element_type=jnp.float32,
    )
    for g in range(out.shape[0]):
        out[g] = sums[0:1]


def pick_kernel(item_ref, me_ref, pieces, sums, wide, out):
    total = item_ref.shape[0]
    devices = total // PER
    lane = lax.broadcasted_iota(jnp.int32, (1, 128), 1)
    summed = jnp.sum(sums[...].reshape(sums.shape[0], 128), axis=0, keepdims=True)

    def spread(k):
        v = jnp.where((lane >= NBINS * k) & (lane < NBINS * (k + 1)), summed, 0.0)
        for shift in (16, 32, 64):
            v = v + pltpu.roll(v, shift, axis=1)
        return v

    weight = spread(LIVE)
    mine = jnp.zeros((devices, 128), jnp.float32)
    for k in range(LIVE):
        mine = jnp.where(wide[...] == me_ref[0] * LIVE + k, spread(k) / weight, mine)
    for d in range(devices):
        for q in range(PER):
            out[d * (PER + 1) + q] = pieces[item_ref[d * PER + q]]
        out[d * (PER + 1) + PER] = jnp.broadcast_to(mine[d : d + 1], (DEPTH, 128))


def finish_kernel(got, resampled, propagator):
    devices = got.shape[0] // (PER + 1)
    sums = got[PER]
    for d in range(1, devices):
        sums = sums + got[d * (PER + 1) + PER]
    for q in range(PER):
        for d in range(devices):
            resampled[q, :, 128 * d : 128 * (d + 1)] = got[d * (PER + 1) + q]
    for q in range(PER):
        turned = sums if q == 0 else pltpu.roll(sums, 128 - NBINS * q, axis=1)
        propagator[q : q + 1, :] = turned[0:1, :NBINS]


def spec(space):
    return pl.BlockSpec(memory_space=space)


def shape(*dims, dtype=jnp.float32):
    return jax.ShapeDtypeStruct(dims, dtype)


def rows_view(slabs):
    lead = slabs.shape[:-2]
    parts = slabs.reshape(*lead, DEPTH, ROWS, 128)
    return jnp.swapaxes(parts, -3, -2).reshape(*lead, DEPTH * ROWS, 128)


def edges(base, counts, field, noise, masses):
    return pl.pallas_call(
        edges_kernel,
        out_shape=[shape(3 * LIVE + 1, ROWS, 128)] * 2,
        in_specs=[spec(SMEM)] * 2 + [spec(pl.ANY)] * 3,
        out_specs=[spec(VMEM)] * 2,
        scratch_shapes=[
            VMEM((LIVE, 128, 128), jnp.float32),
            VMEM((LIVE, 128, 128), jnp.float32),
            VMEM((128, 128), jnp.float32),
            pltpu.SemaphoreType.DMA((2 * LIVE + 1,)),
        ],
        name="edges",
    )(base, counts, field, noise, masses)


def plan(counts, dest_slots, mode_bins):
    total = counts.shape[0]
    padded = jnp.pad(mode_bins, ((0, 0), (0, 0), (0, 128 - mode_bins.shape[2])))
    return pl.pallas_call(
        plan_kernel,
        out_shape=[
            shape(1, total, dtype=jnp.int32),
            shape(total // PER, 128, dtype=jnp.int32),
            shape(128, 128, dtype=jnp.int32),
        ],
        in_specs=[spec(VMEM)] * 3,
        out_specs=[spec(VMEM)] * 3,
        name="plan",
    )(counts.reshape(1, total), dest_slots.reshape(1, total), padded)


def sweeps(base, counts, field, noise, masses, lo, hi, along_x, along_y):
    return pl.pallas_call(
        sweep_kernel,
        out_shape=[shape(ROWS * LIVE * DEPTH, 128), shape(16 * 8 * LIVE, 128)],
        in_specs=[spec(SMEM)] * 2 + [spec(pl.ANY)] * 3 + [spec(VMEM)] * 4,
        out_specs=[spec(VMEM)] * 2,
        scratch_shapes=[
            VMEM((LIVE, 128, 128), jnp.float32),
            VMEM((2, LIVE, 128, 128), jnp.float32),
            VMEM((128, 128), jnp.float32),
            pltpu.SemaphoreType.DMA((3 * LIVE + 1,)),
        ],
        name="sweeps",
    )(base, counts, field, noise, masses, lo, hi, along_x, along_y)


def bins(chunks, place, along_z):
    return pl.pallas_call(
        bins_kernel,
        out_shape=shape(16, 1, 128),
        in_specs=[spec(VMEM)] * 3,
        out_specs=spec(VMEM),
        scratch_shapes=[VMEM((128, 128), jnp.float32)],
        name="bins",
    )(chunks, place, along_z)


def pick(item, me, pieces, sums, wide):
    devices = item.shape[0] // PER
    return pl.pallas_call(
        pick_kernel,
        out_shape=shape(devices * (PER + 1), DEPTH, 128),
        in_specs=[spec(SMEM)] * 2 + [spec(VMEM)] * 3,
        out_specs=spec(VMEM),
        name="pick",
    )(item, me, pieces, sums, wide)


def finish(got):
    return pl.pallas_call(
        finish_kernel,
        out_shape=[shape(PER, DEPTH, L * L), shape(PER, NBINS)],
        in_specs=[spec(VMEM)],
        out_specs=[spec(VMEM)] * 2,
        name="finish",
    )(got)


def local(lattice_field, langevin_noise, masses, counts, dest_slots, mode_bins):
    along_x, along_y, along_z = (jnp.asarray(t) for t in tables())
    me = lax.axis_index("rep").astype(jnp.int32).reshape(1)
    base = me * PER
    field, noise, mass = rows_view(lattice_field), rows_view(langevin_noise), rows_view(masses)
    up, down = edges(base, counts, field, noise, mass)
    ring = lax.axis_size("gz")
    forward = [(i, (i + 1) % ring) for i in range(ring)]
    lo = lax.ppermute(up, "gz", forward)
    hi = lax.ppermute(down, "gz", [(b, a) for a, b in forward])
    item, wide, place = plan(counts, dest_slots, mode_bins)
    pieces, chunks = sweeps(base, counts, field, noise, mass, lo, hi, along_x, along_y)
    reps = lax.axis_size("rep")
    chunks = lax.all_to_all(chunks.reshape(ring, 8 * LIVE, 128), "gz", 0, 0, tiled=True)
    pieces = lax.all_to_all(pieces.reshape(reps, LIVE, DEPTH, 128), "rep", 0, 0, tiled=True)
    sums = lax.all_to_all(bins(chunks, place, along_z), "gz", 0, 0, tiled=True)
    out = pick(item.reshape(-1), me, pieces.reshape(reps * LIVE, DEPTH, 128), sums, wide)
    got = lax.all_to_all(out.reshape(reps, PER + 1, DEPTH, 128), "rep", 0, 0, tiled=True)
    resampled, propagator = finish(got.reshape(reps * (PER + 1), DEPTH, 128))
    return resampled, propagator


def solution(mesh):
    in_specs = (
        P("rep", "gz", None),
        P(None, "rep", "gz", None),
        P("gz", None),
        P(),
        P(),
        P("gz", None, None),
    )
    out_specs = (P("rep", "gz", None), P("rep", None))
    return jax.shard_map(local, mesh=mesh, in_specs=in_specs, out_specs=out_specs, check_vma=False)
```

time: 453 us -> 125 us (0.28)
  the two profiles are of different devices: /device:TPU:38 before, /device:TPU:2 now
where the time goes in v1:
time: 125 us; the launch traced here: 124 us
  blocking collectives  81 us (65%)
  starting transfers between devices  16.1 us (13%)
  Pallas kernels  15.2 us (12%)
  waiting for transfers between devices  9.32 us (7%)
  local copies, waits for them, and re-layouts  2.13 us (2%)
    all_to_all x1, blocking collectives, local(): lax.all_to_all(pieces.reshape(reps, LIVE, DEPTH, 128), 'rep', 0, 0, tiled...  35.6 us
    all_to_all x1, blocking collectives, local(): lax.all_to_all(out.reshape(reps, PER + 1, DEPTH, 128), 'rep', 0, 0, tiled...  34 us
    all_to_all x1, blocking collectives, local(): sums = lax.all_to_all(bins(chunks, place, along_z), 'gz', 0, 0, tiled=True)  11.4 us
    ppermute x1, starting transfers between devices, local(): hi = lax.ppermute(down, 'gz', [(b, a) for a, b in forward])  7.26 us
    all_to_all x1, starting transfers between devices, local(): lax.all_to_all(chunks.reshape(ring, 8 * LIVE, 128), 'gz', 0, 0, tiled=True)  6.94 us
    all_to_all x1, waiting for transfers between devices, local(): lax.all_to_all(chunks.reshape(ring, 8 * LIVE, 128), 'gz', 0, 0, tiled=True)  6.19 us
    pallas_call x1, Pallas kernels, sweeps(): pl.pallas_call(sweep_kernel, out_shape=[shape(ROWS * LIVE * DEPTH, 128),...  4.46 us
    pallas_call x1, Pallas kernels, edges(): pl.pallas_call(edges_kernel, out_shape=[shape(3 * LIVE + 1, ROWS, 128)] *...  2.52 us
  transfers between devices with their start and end apart: 3, of which 3 were waited for; matrix products, arithmetic and copies ran while one was open for 1% of the time, Pallas kernels for 2%

profile of v1, /device:TPU:2, one launch (start us, length us, event | category | flops | bytes accessed | tf_op | source)
XLA Modules:
  0.0 124.4 jit_solution(696349431641826987)
XLA Ops:
  0.6 2.5 %edges.1 = (f32[10,32,128]{2,1,0:T(8,128)}, f32[10,32,128]{2,1,0:T(8,128)}) custom-call(s32[1]{0:T(128)S(6)} %mul.3.base_ref, s32[192]{0:T(256)} %counts_ref.3, f32[6,128,128]{2,1,0:T(8,128)} %bitcast.28, f32[2,6,128,128]{3,2,1,0:T(8,128)} %bitcast.24, f32[128,128]{1,0:T(8,128)} %bitcast.31), custom_call_target="tpu_custom_call" | custom-call | tf_op jit(solution)/shard_map/edges/pallas_call | solution.py:280
  3.2 1.9 %collective-permute-start = (f32[10,32,128]{2,1,0:T(8,128)}, f32[10,32,128]{2,1,0:T(8,128)S(1)}, u32[]{:S(2)}, u32[]{:S(2)}) collective-permute-start(f32[10,32,128]{2,1,0:T(8,128)} %get-tuple-element.10), channel_id=1, source_target_pairs={{0,1},{1,2},{2,3},{3,4},{4,5},{5,6},{6,7},{7,8},{8,9},{9,10},{10,1... | collective-permute-start | bytes 491528 | tf_op jit(solution)/shard_map/ppermute | solution.py:367
  5.1 7.3 %collective-permute-start.1 = (f32[10,32,128]{2,1,0:T(8,128)}, f32[10,32,128]{2,1,0:T(8,128)S(1)}, u32[]{:S(2)}, u32[]{:S(2)}) collective-permute-start(f32[10,32,128]{2,1,0:T(8,128)} %get-tuple-element.11), channel_id=1, source_target_pairs={{1,0},{2,1},{3,2},{4,3},{5,4},{6,5},{7,6},{8,7},{9,8},{10,9},{11,1... | collective-permute-start | bytes 491528 | tf_op jit(solution)/shard_map/ppermute | solution.py:368
  12.4 1.3 %collective-permute-done.lo = f32[10,32,128]{2,1,0:T(8,128)S(1)} collective-permute-done((f32[10,32,128]{2,1,0:T(8,128)}, f32[10,32,128]{2,1,0:T(8,128)S(1)}, u32[]{:S(2)}, u32[]{:S(2)}) %collective-permute-start) | collective-permute-done | bytes 163872 | tf_op jit(solution)/shard_map/ppermute | solution.py:367
  13.6 0.0 copy-start.2
  13.6 1.9 %collective-permute-done.1.hi = f32[10,32,128]{2,1,0:T(8,128)S(1)} collective-permute-done((f32[10,32,128]{2,1,0:T(8,128)}, f32[10,32,128]{2,1,0:T(8,128)S(1)}, u32[]{:S(2)}, u32[]{:S(2)}) %collective-permute-start.1) | collective-permute-done | bytes 163872 | tf_op jit(solution)/shard_map/ppermute | solution.py:368
  15.5 0.0 copy-done.2
  15.5 0.0 copy-start.3
  15.5 0.7 copy-done.3
  16.1 4.5 %sweeps.1 = (f32[384,128]{1,0:T(8,128)}, f32[384,128]{1,0:T(8,128)}) custom-call(s32[1]{0:T(128)S(6)} %mul.3.base_ref, s32[192]{0:T(256)} %counts_ref.3, f32[6,128,128]{2,1,0:T(8,128)} %bitcast.29, f32[2,6,128,128]{3,2,1,0:T(8,128)} %bitcast.25, f32[128,128]{1,0:T(8,128)} %bitcast.32, f32[10,32,128]{2,1,0:T(8,128)} %copy-done.2, f32[10,32,128]{2,1,0:T(8,128)} %copy-done.3, ...), custom_call_target="tpu_custom_call" | custom-call | tf_op jit(solution)/shard_map/sweeps/pallas_call | solution.py:312
  20.6 0.0 copy-start.4
  20.6 6.9 %all-to-all-start.1 = ((f32[16,24,128]{2,1,0:T(8,128)}), f32[16,24,128]{2,1,0:T(8,128)S(1)}, u32[]{:S(2)}, u32[]{:S(2)}) async-start(f32[16,24,128]{2,1,0:T(8,128)} %bitcast.34), calls=%async_computation.1 | async-start | bytes 393216 | tf_op jit(solution)/shard_map/all_to_all | solution.py:372
  27.6 0.0 copy-done.4
  27.6 0.1 copy.11
  27.7 0.7 pad.4.bins_ref
  28.4 1.9 %plan.1 = (s32[1,192]{1,0:T(1,128)}, s32[32,128]{1,0:T(8,128)}, s32[128,128]{1,0:T(8,128)}) custom-call(s32[1,192]{1,0:T(1,128)} %bitcast.35, s32[1,192]{1,0:T(1,128)} %bitcast.36, s32[4,64,128]{2,1,0:T(8,128)} %pad.4.bins_ref), custom_call_target="tpu_custom_call" | custom-call | tf_op jit(solution)/shard_map/plan/pallas_call | solution.py:298
  30.3 0.0 copy-start.1
  30.3 6.2 %all-to-all-done.1.chunks = f32[16,24,128]{2,1,0:T(8,128)S(1)} async-done(((f32[16,24,128]{2,1,0:T(8,128)}), f32[16,24,128]{2,1,0:T(8,128)S(1)}, u32[]{:S(2)}, u32[]{:S(2)}) %all-to-all-start.1) | async-done | bytes 196640 | tf_op jit(solution)/shard_map/all_to_all | solution.py:372
  36.5 0.0 copy-start
  36.5 0.7 copy-done
  37.1 2.5 %bins.1 = f32[16,1,128]{2,1,0:T(1,128)} custom-call(f32[16,24,128]{2,1,0:T(8,128)} %copy-done, s32[128,128]{1,0:T(8,128)} %get-tuple-element.14.map_ref, bf16[2,128,128]{2,1,0:T(8,128)(2,1)} %constant.18.clone.along_z), custom_call_target="tpu_custom_call" | custom-call | tf_op jit(solution)/shard_map/bins/pallas_call | solution.py:328
  39.6 11.4 %all_to_all.20.sums = f32[16,1,128]{2,1,0:T(1,128)} all-to-all(f32[16,1,128]{2,1,0:T(1,128)} %bins.1), channel_id=1, replica_groups=mesh['rep'=32,'gz'=16] {'gz'}, dimensions={0} | all-to-all | bytes 16384 | tf_op jit(solution)/shard_map/all_to_all | solution.py:374
  51.0 0.0 copy-done.1
  51.0 35.6 %all_to_all.21 = f32[32,3,4,128]{3,2,1,0:T(4,128)} all-to-all(f32[32,3,4,128]{3,2,1,0:T(4,128)S(1)} %bitcast.33), channel_id=1, replica_groups=mesh['rep'=32,'gz'=16] {'rep'}, dimensions={0} | all-to-all | bytes 393216 | tf_op jit(solution)/shard_map/all_to_all | solution.py:373
  86.6 2.0 %pick.1 = f32[224,4,128]{2,1,0:T(4,128)} custom-call(s32[192]{0:T(256)} %bitcast.37, s32[1]{0:T(128)} %bitcast.3.me_ref, f32[96,4,128]{2,1,0:T(4,128)} %bitcast.30, f32[16,1,128]{2,1,0:T(1,128)} %all_to_all.20.sums, s32[32,128]{1,0:T(8,128)} %get-tuple-element.15.wide), custom_call_target="tpu_custom_call" | custom-call | tf_op jit(solution)/shard_map/pick/pallas_call | solution.py:340
  88.6 34.0 %all_to_all.22 = f32[32,7,4,128]{3,2,1,0:T(4,128)} all-to-all(f32[32,7,4,128]{3,2,1,0:T(4,128)} %bitcast.27), channel_id=1, replica_groups=mesh['rep'=32,'gz'=16] {'rep'}, dimensions={0} | all-to-all | bytes 917504 | tf_op jit(solution)/shard_map/all_to_all | solution.py:376
  122.6 1.8 %finish.1 = (f32[6,4,4096]{2,1,0:T(4,128)}, f32[6,16]{1,0:T(8,128)}) custom-call(f32[224,4,128]{2,1,0:T(4,128)} %bitcast.26), custom_call_target="tpu_custom_call" | custom-call | tf_op jit(solution)/shard_map/finish/pallas_call | solution.py:350
Async XLA Ops:
  3.2 10.5 %collective-permute-start = (f32[10,32,128]{2,1,0:T(8,128)}, f32[10,32,128]{2,1,0:T(8,128)S(1)}, u32[]{:S(2)}, u32[]{:S(2)}) collective-permute-start(f32[10,32,128]{2,1,0:T(8,128)} %get-tuple-element.10), channel_id=1, source_target_pairs={{0,1},{1,2},{2,3},{3,4},{4,5},{5,6},{6,7},{7,8},{8,9},{9,10},{10,1... | collective-permute-start | bytes 491528 | tf_op jit(solution)/shard_map/ppermute | solution.py:367
  5.1 10.4 %collective-permute-start.1 = (f32[10,32,128]{2,1,0:T(8,128)}, f32[10,32,128]{2,1,0:T(8,128)S(1)}, u32[]{:S(2)}, u32[]{:S(2)}) collective-permute-start(f32[10,32,128]{2,1,0:T(8,128)} %get-tuple-element.11), channel_id=1, source_target_pairs={{1,0},{2,1},{3,2},{4,3},{5,4},{6,5},{7,6},{8,7},{9,8},{10,9},{11,1... | collective-permute-start | bytes 491528 | tf_op jit(solution)/shard_map/ppermute | solution.py:368
  13.6 1.9 %copy-start.2 = (f32[10,32,128]{2,1,0:T(8,128)}, f32[10,32,128]{2,1,0:T(8,128)S(1)}, u32[]{:S(2)}) copy-start(f32[10,32,128]{2,1,0:T(8,128)S(1)} %collective-permute-done.lo) | copy-start | bytes 491524
  15.5 0.7 copy-start.3
  20.6 7.0 %copy-start.4 = (s32[4,64,33]{1,0,2:T(4,128)S(1)}, s32[4,64,33]{1,0,2:T(4,128)}, u32[]{:S(2)}) copy-start(s32[4,64,33]{1,0,2:T(4,128)} %param.14) | copy-start | bytes 101380
  20.6 15.8 %all-to-all-start.1 = ((f32[16,24,128]{2,1,0:T(8,128)}), f32[16,24,128]{2,1,0:T(8,128)S(1)}, u32[]{:S(2)}, u32[]{:S(2)}) async-start(f32[16,24,128]{2,1,0:T(8,128)} %bitcast.34), calls=%async_computation.1 | async-start | bytes 393216 | tf_op jit(solution)/shard_map/all_to_all | solution.py:372
  30.3 20.7 %copy-start.1 = (f32[384,128]{1,0:T(8,128)S(1)}, f32[384,128]{1,0:T(8,128)}, u32[]{:S(2)}) copy-start(f32[384,128]{1,0:T(8,128)} %get-tuple-element.12) | copy-start | bytes 589828
  36.5 0.7 copy-start

commit v2 on v1

--- a/solution.py
+++ b/solution.py
@@ -223,15 +223,14 @@
         precision=lax.Precision.HIGHEST,
         preferred_element_type=jnp.float32,
     )
-    for g in range(out.shape[0]):
-        out[g] = sums[0:1]
+    out[...] = sums[0:1]
 
 
 def pick_kernel(item_ref, me_ref, pieces, sums, wide, out):
     total = item_ref.shape[0]
     devices = total // PER
     lane = lax.broadcasted_iota(jnp.int32, (1, 128), 1)
-    summed = jnp.sum(sums[...].reshape(sums.shape[0], 128), axis=0, keepdims=True)
+    summed = sums[...]
 
     def spread(k):
         v = jnp.where((lane >= NBINS * k) & (lane < NBINS * (k + 1)), summed, 0.0)
@@ -327,7 +326,7 @@
 def bins(chunks, place, along_z):
     return pl.pallas_call(
         bins_kernel,
-        out_shape=shape(16, 1, 128),
+        out_shape=shape(1, 128),
         in_specs=[spec(VMEM)] * 3,
         out_specs=spec(VMEM),
         scratch_shapes=[VMEM((128, 128), jnp.float32)],
@@ -366,12 +365,16 @@
     forward = [(i, (i + 1) % ring) for i in range(ring)]
     lo = lax.ppermute(up, "gz", forward)
     hi = lax.ppermute(down, "gz", [(b, a) for a, b in forward])
-    item, wide, place = plan(counts, dest_slots, mode_bins)
+    lo, hi, item, wide, place = lax.optimization_barrier((lo, hi, *plan(counts, dest_slots, mode_bins)))
     pieces, chunks = sweeps(base, counts, field, noise, mass, lo, hi, along_x, along_y)
     reps = lax.axis_size("rep")
     chunks = lax.all_to_all(chunks.reshape(ring, 8 * LIVE, 128), "gz", 0, 0, tiled=True)
+    pieces, sums = lax.optimization_barrier((pieces, bins(chunks, place, along_z)))
     pieces = lax.all_to_all(pieces.reshape(reps, LIVE, DEPTH, 128), "rep", 0, 0, tiled=True)
-    sums = lax.all_to_all(bins(chunks, place, along_z), "gz", 0, 0, tiled=True)
+    step = 1
+    while step < ring:
+        sums = sums + lax.ppermute(sums, "gz", [(i, i ^ step) for i in range(ring)])
+        step *= 2
     out = pick(item.reshape(-1), me, pieces.reshape(reps * LIVE, DEPTH, 128), sums, wide)
     got = lax.all_to_all(out.reshape(reps, PER + 1, DEPTH, 128), "rep", 0, 0, tiled=True)
     resampled, propagator = finish(got.reshape(reps * (PER + 1), DEPTH, 128))

time: 125 us -> 124 us (level)
  blocking collectives: 81 us -> 56.1 us
  starting transfers between devices: 16.1 us -> 34.7 us
  waiting for transfers between devices: 9.32 us -> 14 us
    all_to_all x2 -> x1, blocking collectives: 47 us -> 15.8 us  [local(): lax.all_to_all(chunks.reshape(ring, 8 * LIVE, 128), 'gz', 0, 0, tiled=True)]
    ppermute x0 -> x4, waiting for transfers between devices: none -> 13.5 us  [local(): sums = sums + lax.ppermute(sums, 'gz', [(i, i ^ step) for i in range(ring)])]
    all_to_all x1, starting transfers between devices: 6.94 us -> 16.8 us  [local(): lax.all_to_all(pieces.reshape(reps, LIVE, DEPTH, 128), 'rep', 0, 0, tiled...]
    ppermute x0 -> x4, starting transfers between devices: none -> 8.71 us  [local(): sums = sums + lax.ppermute(sums, 'gz', [(i, i ^ step) for i in range(ring)])]
    all_to_all x1, blocking collectives: 34 us -> 40.3 us  [local(): lax.all_to_all(out.reshape(reps, PER + 1, DEPTH, 128), 'rep', 0, 0, tiled...]
    all_to_all x1, waiting for transfers between devices: 6.19 us -> 0.01 us  [local(): lax.all_to_all(pieces.reshape(reps, LIVE, DEPTH, 128), 'rep', 0, 0, tiled...]
    ppermute x1, waiting for transfers between devices: 1.86 us -> 0.46 us  [local(): hi = lax.ppermute(down, 'gz', [(b, a) for a, b in forward])]
    ppermute x1, waiting for transfers between devices: 1.27 us -> 0.01 us  [local(): lo = lax.ppermute(up, 'gz', forward)]
  transfers between devices with their start and end apart: 3 -> 7, of which waited for: 3 -> 5; matrix products, arithmetic and copies ran while one was open for 1% -> 1% of each run, Pallas kernels for 2% -> 2%
where the time goes in v2:
time: 124 us; the launch traced here: 123 us
  blocking collectives  56.1 us (45%)
  starting transfers between devices  34.7 us (28%)
  Pallas kernels  15.2 us (12%)
  waiting for transfers between devices  14 us (11%)
  local copies, waits for them, and re-layouts  2.1 us (2%)
    all_to_all x1, blocking collectives, local(): lax.all_to_all(out.reshape(reps, PER + 1, DEPTH, 128), 'rep', 0, 0, tiled...  40.3 us
    all_to_all x1, starting transfers between devices, local(): lax.all_to_all(pieces.reshape(reps, LIVE, DEPTH, 128), 'rep', 0, 0, tiled...  16.8 us
    all_to_all x1, blocking collectives, local(): lax.all_to_all(chunks.reshape(ring, 8 * LIVE, 128), 'gz', 0, 0, tiled=True)  15.8 us
    ppermute x4, waiting for transfers between devices, local(): sums = sums + lax.ppermute(sums, 'gz', [(i, i ^ step) for i in range(ring)])  13.5 us
    ppermute x4, starting transfers between devices, local(): sums = sums + lax.ppermute(sums, 'gz', [(i, i ^ step) for i in range(ring)])  8.71 us
    ppermute x1, starting transfers between devices, local(): hi = lax.ppermute(down, 'gz', [(b, a) for a, b in forward])  7.26 us
    pallas_call x1, Pallas kernels, sweeps(): pl.pallas_call(sweep_kernel, out_shape=[shape(ROWS * LIVE * DEPTH, 128),...  4.46 us
    pallas_call x1, Pallas kernels, edges(): pl.pallas_call(edges_kernel, out_shape=[shape(3 * LIVE + 1, ROWS, 128)] *...  2.65 us
  transfers between devices with their start and end apart: 7, of which 5 were waited for; matrix products, arithmetic and copies ran while one was open for 1% of the time, Pallas kernels for 2%

profile of v2, /device:TPU:2, one launch (start us, length us, event | category | flops | bytes accessed | tf_op | source)
XLA Modules:
  0.0 123.5 jit_solution(3069165348065076036)
XLA Ops:
  0.6 0.0 copy-start.3
  0.6 2.7 %edges.1 = (f32[10,32,128]{2,1,0:T(8,128)}, f32[10,32,128]{2,1,0:T(8,128)}) custom-call(s32[1]{0:T(128)S(6)} %mul.3.base_ref, s32[192]{0:T(256)} %counts_ref.3, f32[6,128,128]{2,1,0:T(8,128)} %bitcast.28, f32[2,6,128,128]{3,2,1,0:T(8,128)} %bitcast.24, f32[128,128]{1,0:T(8,128)} %bitcast.31), custom_call_target="tpu_custom_call" | custom-call | tf_op jit(solution)/shard_map/edges/pallas_call | solution.py:279
  3.3 1.9 %collective-permute-start = (f32[10,32,128]{2,1,0:T(8,128)}, f32[10,32,128]{2,1,0:T(8,128)S(1)}, u32[]{:S(2)}, u32[]{:S(2)}) collective-permute-start(f32[10,32,128]{2,1,0:T(8,128)} %get-tuple-element.16), channel_id=1, source_target_pairs={{0,1},{1,2},{2,3},{3,4},{4,5},{5,6},{6,7},{7,8},{8,9},{9,10},{10,1... | collective-permute-start | bytes 491528 | tf_op jit(solution)/shard_map/ppermute | solution.py:366
  5.2 7.3 %collective-permute-start.1 = (f32[10,32,128]{2,1,0:T(8,128)}, f32[10,32,128]{2,1,0:T(8,128)S(1)}, u32[]{:S(2)}, u32[]{:S(2)}) collective-permute-start(f32[10,32,128]{2,1,0:T(8,128)} %get-tuple-element.17), channel_id=1, source_target_pairs={{1,0},{2,1},{3,2},{4,3},{5,4},{6,5},{7,6},{8,7},{9,8},{10,9},{11,1... | collective-permute-start | bytes 491528 | tf_op jit(solution)/shard_map/ppermute | solution.py:367
  12.5 0.0 copy-done.3
  12.5 0.1 copy.14
  12.6 0.7 pad.4.bins_ref
  13.3 1.9 %plan.1 = (s32[1,192]{1,0:T(1,128)}, s32[32,128]{1,0:T(8,128)}, s32[128,128]{1,0:T(8,128)}) custom-call(s32[1,192]{1,0:T(1,128)} %bitcast.34, s32[1,192]{1,0:T(1,128)} %bitcast.35, s32[4,64,128]{2,1,0:T(8,128)} %pad.4.bins_ref), custom_call_target="tpu_custom_call" | custom-call | tf_op jit(solution)/shard_map/plan/pallas_call | solution.py:297
  15.2 0.0 collective-permute-done.lo
  15.2 0.0 copy-start.1
  15.2 0.5 collective-permute-done.1.hi
  15.6 0.0 copy-start.2
  15.6 0.2 copy-done.1
  15.8 0.4 copy-done.2
  16.3 4.5 %sweeps.1 = (f32[384,128]{1,0:T(8,128)}, f32[384,128]{1,0:T(8,128)}) custom-call(s32[1]{0:T(128)S(6)} %mul.3.base_ref, s32[192]{0:T(256)} %counts_ref.3, f32[6,128,128]{2,1,0:T(8,128)} %bitcast.29, f32[2,6,128,128]{3,2,1,0:T(8,128)} %bitcast.25, f32[128,128]{1,0:T(8,128)} %bitcast.32, f32[10,32,128]{2,1,0:T(8,128)} %copy-done.1, f32[10,32,128]{2,1,0:T(8,128)} %copy-done.2, ...), custom_call_target="tpu_custom_call" | custom-call | tf_op jit(solution)/shard_map/sweeps/pallas_call | solution.py:311
  20.8 15.8 %all_to_all.15.chunks = f32[16,24,128]{2,1,0:T(8,128)} all-to-all(f32[16,24,128]{2,1,0:T(8,128)} %bitcast.33), channel_id=1, replica_groups=mesh['rep'=32,'gz'=16] {'gz'}, dimensions={0} | all-to-all | bytes 393216 | tf_op jit(solution)/shard_map/all_to_all | solution.py:371
  36.5 2.4 %bins.1 = f32[1,128]{1,0:T(1,128)} custom-call(f32[16,24,128]{2,1,0:T(8,128)} %all_to_all.15.chunks, s32[128,128]{1,0:T(8,128)} %get-tuple-element.26.map_ref, bf16[2,128,128]{2,1,0:T(8,128)(2,1)} %constant.18.clone.along_z), custom_call_target="tpu_custom_call" | custom-call | tf_op jit(solution)/shard_map/bins/pallas_call | solution.py:327
  38.9 0.0 copy-start.4
  38.9 16.8 %all-to-all-start.1 = ((f32[32,3,4,128]{3,2,1,0:T(4,128)}), f32[32,3,4,128]{3,2,1,0:T(4,128)S(1)}, u32[]{:S(2)}, u32[]{:S(2)}) async-start(f32[32,3,4,128]{3,2,1,0:T(4,128)} %bitcast.20), calls=%async_computation.1 | async-start | bytes 393216 | tf_op jit(solution)/shard_map/all_to_all | solution.py:373
  55.8 0.0 copy-done.4
  55.8 1.9 %collective-permute-start.2 = (f32[1,128]{1,0:T(1,128)S(1)}, f32[1,128]{1,0:T(1,128)S(1)}, u32[]{:S(2)}, u32[]{:S(2)}) collective-permute-start(f32[1,128]{1,0:T(1,128)S(1)} %copy-done.4), channel_id=1, source_target_pairs={{0,1},{1,0},{2,3},{3,2},{4,5},{5,4},{6,7},{7,6},{8,9},{9,8},{10,11... | collective-permute-start | bytes 1544 | tf_op jit(solution)/shard_map/ppermute | solution.py:376
  57.7 1.1 collective-permute-done.2
  58.8 1.9 %collective-permute-start.3 = (f32[1,128]{1,0:T(1,128)S(1)}, f32[1,128]{1,0:T(1,128)S(1)}, u32[]{:S(2)}, u32[]{:S(2)}) collective-permute-start(f32[1,128]{1,0:T(1,128)S(1)} %add.14), channel_id=1, source_target_pairs={{0,2},{1,3},{2,0},{3,1},{4,6},{5,7},{6,4},{7,5},{8,10},{9,11},{10,... | collective-permute-start | bytes 1544 | tf_op jit(solution)/shard_map/ppermute | solution.py:376
  60.7 3.5 %collective-permute-done.3 = f32[1,128]{1,0:T(1,128)S(1)} collective-permute-done((f32[1,128]{1,0:T(1,128)S(1)}, f32[1,128]{1,0:T(1,128)S(1)}, u32[]{:S(2)}, u32[]{:S(2)}) %collective-permute-start.3) | collective-permute-done | bytes 544 | tf_op jit(solution)/shard_map/ppermute | solution.py:376
  64.2 2.3 %collective-permute-start.4 = (f32[1,128]{1,0:T(1,128)S(1)}, f32[1,128]{1,0:T(1,128)S(1)}, u32[]{:S(2)}, u32[]{:S(2)}) collective-permute-start(f32[1,128]{1,0:T(1,128)S(1)} %add.15), channel_id=1, source_target_pairs={{0,4},{1,5},{2,6},{3,7},{4,0},{5,1},{6,2},{7,3},{8,12},{9,13},{10,... | collective-permute-start | bytes 1544 | tf_op jit(solution)/shard_map/ppermute | solution.py:376
  66.6 4.6 %collective-permute-done.4 = f32[1,128]{1,0:T(1,128)S(1)} collective-permute-done((f32[1,128]{1,0:T(1,128)S(1)}, f32[1,128]{1,0:T(1,128)S(1)}, u32[]{:S(2)}, u32[]{:S(2)}) %collective-permute-start.4) | collective-permute-done | bytes 544 | tf_op jit(solution)/shard_map/ppermute | solution.py:376
  71.2 2.6 %collective-permute-start.5 = (f32[1,128]{1,0:T(1,128)S(1)}, f32[1,128]{1,0:T(1,128)S(1)}, u32[]{:S(2)}, u32[]{:S(2)}) collective-permute-start(f32[1,128]{1,0:T(1,128)S(1)} %add.16), channel_id=1, source_target_pairs={{0,8},{1,9},{2,10},{3,11},{4,12},{5,13},{6,14},{7,15},{8,0},{9,1},... | collective-permute-start | bytes 1544 | tf_op jit(solution)/shard_map/ppermute | solution.py:376
  73.7 4.4 %collective-permute-done.5 = f32[1,128]{1,0:T(1,128)S(1)} collective-permute-done((f32[1,128]{1,0:T(1,128)S(1)}, f32[1,128]{1,0:T(1,128)S(1)}, u32[]{:S(2)}, u32[]{:S(2)}) %collective-permute-start.5) | collective-permute-done | bytes 544 | tf_op jit(solution)/shard_map/ppermute | solution.py:376
  78.1 0.5 add.17.sums
  78.6 0.0 all-to-all-done.1
  78.6 0.0 copy-start
  78.6 0.7 copy-done
  79.3 2.0 %pick.1 = f32[224,4,128]{2,1,0:T(4,128)} custom-call(s32[192]{0:T(256)} %bitcast.36, s32[1]{0:T(128)} %bitcast.me_ref, f32[96,4,128]{2,1,0:T(4,128)} %bitcast.30, f32[1,128]{1,0:T(1,128)} %add.17.sums, s32[32,128]{1,0:T(8,128)} %get-tuple-element.29.wide), custom_call_target="tpu_custom_call" | custom-call | tf_op jit(solution)/shard_map/pick/pallas_call | solution.py:339
  81.3 40.3 %all_to_all.16 = f32[32,7,4,128]{3,2,1,0:T(4,128)} all-to-all(f32[32,7,4,128]{3,2,1,0:T(4,128)} %bitcast.27), channel_id=1, replica_groups=mesh['rep'=32,'gz'=16] {'rep'}, dimensions={0} | all-to-all | bytes 917504 | tf_op jit(solution)/shard_map/all_to_all | solution.py:379
  121.6 1.8 %finish.1 = (f32[6,4,4096]{2,1,0:T(4,128)}, f32[6,16]{1,0:T(8,128)}) custom-call(f32[224,4,128]{2,1,0:T(4,128)} %bitcast.26), custom_call_target="tpu_custom_call" | custom-call | tf_op jit(solution)/shard_map/finish/pallas_call | solution.py:349
  (3 shorter events, 0.0 us)
Async XLA Ops:
  0.6 11.9 %copy-start.3 = (s32[4,64,33]{1,0,2:T(4,128)S(1)}, s32[4,64,33]{1,0,2:T(4,128)}, u32[]{:S(2)}) copy-start(s32[4,64,33]{1,0,2:T(4,128)} %param.14) | copy-start | bytes 101380
  3.3 11.9 %collective-permute-start = (f32[10,32,128]{2,1,0:T(8,128)}, f32[10,32,128]{2,1,0:T(8,128)S(1)}, u32[]{:S(2)}, u32[]{:S(2)}) collective-permute-start(f32[10,32,128]{2,1,0:T(8,128)} %get-tuple-element.16), channel_id=1, source_target_pairs={{0,1},{1,2},{2,3},{3,4},{4,5},{5,6},{6,7},{7,8},{8,9},{9,10},{10,1... | collective-permute-start | bytes 491528 | tf_op jit(solution)/shard_map/ppermute | solution.py:366
  5.2 10.4 %collective-permute-start.1 = (f32[10,32,128]{2,1,0:T(8,128)}, f32[10,32,128]{2,1,0:T(8,128)S(1)}, u32[]{:S(2)}, u32[]{:S(2)}) collective-permute-start(f32[10,32,128]{2,1,0:T(8,128)} %get-tuple-element.17), channel_id=1, source_target_pairs={{1,0},{2,1},{3,2},{4,3},{5,4},{6,5},{7,6},{8,7},{9,8},{10,9},{11,1... | collective-permute-start | bytes 491528 | tf_op jit(solution)/shard_map/ppermute | solution.py:367
  15.2 0.7 copy-start.1
  15.6 0.7 copy-start.2
  38.9 16.9 %copy-start.4 = (f32[1,128]{1,0:T(1,128)S(1)}, f32[1,128]{1,0:T(1,128)}, u32[]{:S(2)}) copy-start(f32[1,128]{1,0:T(1,128)} %bins.1) | copy-start | bytes 1540
  38.9 39.7 %all-to-all-start.1 = ((f32[32,3,4,128]{3,2,1,0:T(4,128)}), f32[32,3,4,128]{3,2,1,0:T(4,128)S(1)}, u32[]{:S(2)}, u32[]{:S(2)}) async-start(f32[32,3,4,128]{3,2,1,0:T(4,128)} %bitcast.20), calls=%async_computation.1 | async-start | bytes 393216 | tf_op jit(solution)/shard_map/all_to_all | solution.py:373
  55.8 3.0 %collective-permute-start.2 = (f32[1,128]{1,0:T(1,128)S(1)}, f32[1,128]{1,0:T(1,128)S(1)}, u32[]{:S(2)}, u32[]{:S(2)}) collective-permute-start(f32[1,128]{1,0:T(1,128)S(1)} %copy-done.4), channel_id=1, source_target_pairs={{0,1},{1,0},{2,3},{3,2},{4,5},{5,4},{6,7},{7,6},{8,9},{9,8},{10,11... | collective-permute-start | bytes 1544 | tf_op jit(solution)/shard_map/ppermute | solution.py:376
  58.8 5.4 %collective-permute-start.3 = (f32[1,128]{1,0:T(1,128)S(1)}, f32[1,128]{1,0:T(1,128)S(1)}, u32[]{:S(2)}, u32[]{:S(2)}) collective-permute-start(f32[1,128]{1,0:T(1,128)S(1)} %add.14), channel_id=1, source_target_pairs={{0,2},{1,3},{2,0},{3,1},{4,6},{5,7},{6,4},{7,5},{8,10},{9,11},{10,... | collective-permute-start | bytes 1544 | tf_op jit(solution)/shard_map/ppermute | solution.py:376
  64.2 6.9 %collective-permute-start.4 = (f32[1,128]{1,0:T(1,128)S(1)}, f32[1,128]{1,0:T(1,128)S(1)}, u32[]{:S(2)}, u32[]{:S(2)}) collective-permute-start(f32[1,128]{1,0:T(1,128)S(1)} %add.15), channel_id=1, source_target_pairs={{0,4},{1,5},{2,6},{3,7},{4,0},{5,1},{6,2},{7,3},{8,12},{9,13},{10,... | collective-permute-start | bytes 1544 | tf_op jit(solution)/shard_map/ppermute | solution.py:376
  71.2 6.9 %collective-permute-start.5 = (f32[1,128]{1,0:T(1,128)S(1)}, f32[1,128]{1,0:T(1,128)S(1)}, u32[]{:S(2)}, u32[]{:S(2)}) collective-permute-start(f32[1,128]{1,0:T(1,128)S(1)} %add.16), channel_id=1, source_target_pairs={{0,8},{1,9},{2,10},{3,11},{4,12},{5,13},{6,14},{7,15},{8,0},{9,1},... | collective-permute-start | bytes 1544 | tf_op jit(solution)/shard_map/ppermute | solution.py:376
  78.6 0.7 copy-start

commit v3 on v2

--- a/solution.py
+++ b/solution.py
@@ -13,6 +13,7 @@
 DEPTH = 4
 ROWS = 32
 PER = 6
+BLOCKS = LIVE + 1
 
 VMEM = pltpu.VMEM
 SMEM = pltpu.SMEM
@@ -106,7 +107,7 @@
     block_row = floor_div(row, PER)
     block_col = floor_div(col, PER)
     rank = along((block_row == block_col) & (col < row) & (number > 0.0), jnp.ones_like(number))
-    name = rank + LIVE * block_row[:, :1].astype(jnp.float32)
+    name = rank + BLOCKS * block_row[:, :1].astype(jnp.float32)
     position = jnp.sum(
         jnp.where(slot_column == col.astype(jnp.float32), row.astype(jnp.float32), 0.0), axis=0, keepdims=True
     )
@@ -181,7 +182,7 @@
         kicks = planes(nbuf, 1, k)
         new = [update(mid[p + 1], mid[p], mid[p + 2], mass[p + 1], kicks[p]) for p in range(DEPTH)]
         for z in range(DEPTH):
-            pieces[pl.ds(k * DEPTH + z, ROWS, stride=LIVE * DEPTH), :] = new[z]
+            pieces[pl.ds(k * DEPTH + z, ROWS, stride=BLOCKS * DEPTH), :] = new[z]
         left += [jnp.concatenate(new[0:2], axis=1), jnp.concatenate(new[2:4], axis=1)]
     high, low = split(jnp.concatenate(left, axis=0))
     across = dot(high, along_x[0]) + (dot(low, along_x[0]) + dot(high, along_x[1]))
@@ -201,7 +202,8 @@
                 chunks[pl.ds(i * 4 + side * 2 + pair, 16, stride=8 * LIVE), :] = ready[side][16 * pair : 16 * pair + 16]
 
 
-def bins_kernel(chunks, map_ref, along_z, out, rows):
+def bins_kernel(me_ref, chunks, map_ref, wide, along_z, _, pieces, rows, block, sem):
+    devices = wide.shape[0]
     place = map_ref[...]
     power = []
     for k in range(LIVE):
@@ -211,54 +213,57 @@
     power.append(jnp.ones_like(power[0]))
     for b in range(NBINS):
         here = place == b
-        for k in range(LIVE + 1):
+        for k in range(BLOCKS):
             rows[k * NBINS + b : k * NBINS + b + 1, :] = jnp.sum(
                 jnp.where(here, power[k], 0.0), axis=0, keepdims=True
             )
-    rows[(LIVE + 1) * NBINS :, :] = jnp.zeros((128 - (LIVE + 1) * NBINS, 128), jnp.float32)
+    rows[BLOCKS * NBINS :, :] = jnp.zeros((128 - BLOCKS * NBINS, 128), jnp.float32)
     sums = lax.dot_general(
         jnp.ones((8, 128), jnp.float32),
         rows[...],
         (((1,), (1,)), ((), ())),
         precision=lax.Precision.HIGHEST,
         preferred_element_type=jnp.float32,
-    )
-    out[...] = sums[0:1]
-
-
-def pick_kernel(item_ref, me_ref, pieces, sums, wide, out):
-    total = item_ref.shape[0]
-    devices = total // PER
+    )[0:1]
     lane = lax.broadcasted_iota(jnp.int32, (1, 128), 1)
-    summed = sums[...]
-
-    def spread(k):
-        v = jnp.where((lane >= NBINS * k) & (lane < NBINS * (k + 1)), summed, 0.0)
-        for shift in (16, 32, 64):
-            v = v + pltpu.roll(v, shift, axis=1)
-        return v
-
-    weight = spread(LIVE)
-    mine = jnp.zeros((devices, 128), jnp.float32)
-    for k in range(LIVE):
-        mine = jnp.where(wide[...] == me_ref[0] * LIVE + k, spread(k) / weight, mine)
+    mine = jnp.where(lane >= NBINS * PER, spread(sums, LIVE, lane) * (1.0 / devices), 0.0)
+    mine = jnp.broadcast_to(mine, (devices, 128))
+    for k in range(LIVE):
+        mine = jnp.where(wide[...] == me_ref[0] * BLOCKS + k, spread(sums, k, lane), mine)
     for d in range(devices):
-        for q in range(PER):
-            out[d * (PER + 1) + q] = pieces[item_ref[d * PER + q]]
-        out[d * (PER + 1) + PER] = jnp.broadcast_to(mine[d : d + 1], (DEPTH, 128))
-
-
-def finish_kernel(got, resampled, propagator):
-    devices = got.shape[0] // (PER + 1)
-    sums = got[PER]
+        block[d] = jnp.broadcast_to(mine[d : d + 1], (DEPTH, 128))
+    copy = pltpu.make_async_copy(block, pieces.at[:, LIVE], sem)
+    copy.start()
+    copy.wait()
+
+
+def spread(row, k, lane):
+    row = jnp.where((lane >= NBINS * k) & (lane < NBINS * (k + 1)), row, 0.0)
+    for shift in (16, 32, 64):
+        row = row + pltpu.roll(row, shift, axis=1)
+    return row
+
+
+def pick_kernel(item_ref, pieces, out, part):
+    devices = pieces.shape[0] // BLOCKS
+    for s in range(devices * PER):
+        out[s] = pieces[item_ref[s]]
+    sums = pieces[LIVE]
     for d in range(1, devices):
-        sums = sums + got[d * (PER + 1) + PER]
+        sums = sums + pieces[d * BLOCKS + LIVE]
+    part[...] = sums[0:1]
+
+
+def finish_kernel(got, sums_ref, resampled, propagator):
+    devices = got.shape[0] // PER
     for q in range(PER):
         for d in range(devices):
-            resampled[q, :, 128 * d : 128 * (d + 1)] = got[d * (PER + 1) + q]
+            resampled[q, :, 128 * d : 128 * (d + 1)] = got[d * PER + q]
+    lane = lax.broadcasted_iota(jnp.int32, (1, 128), 1)
+    ratio = sums_ref[...] / spread(sums_ref[...], PER, lane)
     for q in range(PER):
-        turned = sums if q == 0 else pltpu.roll(sums, 128 - NBINS * q, axis=1)
-        propagator[q : q + 1, :] = turned[0:1, :NBINS]
+        turned = ratio if q == 0 else pltpu.roll(ratio, 128 - NBINS * q, axis=1)
+        propagator[q : q + 1, :] = turned[:, :NBINS]
 
 
 def spec(space):
@@ -310,7 +315,7 @@
 def sweeps(base, counts, field, noise, masses, lo, hi, along_x, along_y):
     return pl.pallas_call(
         sweep_kernel,
-        out_shape=[shape(ROWS * LIVE * DEPTH, 128), shape(16 * 8 * LIVE, 128)],
+        out_shape=[shape(ROWS * BLOCKS * DEPTH, 128), shape(16 * 8 * LIVE, 128)],
         in_specs=[spec(SMEM)] * 2 + [spec(pl.ANY)] * 3 + [spec(VMEM)] * 4,
         out_specs=[spec(VMEM)] * 2,
         scratch_shapes=[
@@ -323,36 +328,41 @@
     )(base, counts, field, noise, masses, lo, hi, along_x, along_y)
 
 
-def bins(chunks, place, along_z):
+def bins(me, chunks, place, wide, along_z, pieces):
+    devices = wide.shape[0]
     return pl.pallas_call(
         bins_kernel,
-        out_shape=shape(1, 128),
-        in_specs=[spec(VMEM)] * 3,
-        out_specs=spec(VMEM),
-        scratch_shapes=[VMEM((128, 128), jnp.float32)],
+        out_shape=shape(devices, BLOCKS, DEPTH, 128),
+        in_specs=[spec(SMEM)] + [spec(VMEM)] * 4 + [spec(pl.ANY)],
+        out_specs=spec(pl.ANY),
+        scratch_shapes=[
+            VMEM((128, 128), jnp.float32),
+            VMEM((devices, DEPTH, 128), jnp.float32),
+            pltpu.SemaphoreType.DMA,
+        ],
+        input_output_aliases={5: 0},
         name="bins",
-    )(chunks, place, along_z)
-
-
-def pick(item, me, pieces, sums, wide):
-    devices = item.shape[0] // PER
+    )(me, chunks, place, wide, along_z, pieces)
+
+
+def pick(item, pieces):
     return pl.pallas_call(
         pick_kernel,
-        out_shape=shape(devices * (PER + 1), DEPTH, 128),
-        in_specs=[spec(SMEM)] * 2 + [spec(VMEM)] * 3,
-        out_specs=spec(VMEM),
+        out_shape=[shape(item.shape[0], DEPTH, 128), shape(1, 128)],
+        in_specs=[spec(SMEM), spec(VMEM)],
+        out_specs=[spec(VMEM)] * 2,
         name="pick",
-    )(item, me, pieces, sums, wide)
-
-
-def finish(got):
+    )(item, pieces)
+
+
+def finish(got, sums):
     return pl.pallas_call(
         finish_kernel,
         out_shape=[shape(PER, DEPTH, L * L), shape(PER, NBINS)],
-        in_specs=[spec(VMEM)],
+        in_specs=[spec(VMEM)] * 2,
         out_specs=[spec(VMEM)] * 2,
         name="finish",
-    )(got)
+    )(got, sums)
 
 
 def local(lattice_field, langevin_noise, masses, counts, dest_slots, mode_bins):
@@ -369,15 +379,15 @@
     pieces, chunks = sweeps(base, counts, field, noise, mass, lo, hi, along_x, along_y)
     reps = lax.axis_size("rep")
     chunks = lax.all_to_all(chunks.reshape(ring, 8 * LIVE, 128), "gz", 0, 0, tiled=True)
-    pieces, sums = lax.optimization_barrier((pieces, bins(chunks, place, along_z)))
-    pieces = lax.all_to_all(pieces.reshape(reps, LIVE, DEPTH, 128), "rep", 0, 0, tiled=True)
+    pieces = bins(me, chunks, place, wide, along_z, pieces.reshape(reps, BLOCKS, DEPTH, 128))
+    pieces = lax.all_to_all(pieces, "rep", 0, 0, tiled=True)
+    out, sums = pick(item.reshape(-1), pieces.reshape(reps * BLOCKS, DEPTH, 128))
+    got = lax.all_to_all(out.reshape(reps, PER, DEPTH, 128), "rep", 0, 0, tiled=True)
     step = 1
     while step < ring:
         sums = sums + lax.ppermute(sums, "gz", [(i, i ^ step) for i in range(ring)])
         step *= 2
-    out = pick(item.reshape(-1), me, pieces.reshape(reps * LIVE, DEPTH, 128), sums, wide)
-    got = lax.all_to_all(out.reshape(reps, PER + 1, DEPTH, 128), "rep", 0, 0, tiled=True)
-    resampled, propagator = finish(got.reshape(reps * (PER + 1), DEPTH, 128))
+    resampled, propagator = finish(got.reshape(reps * PER, DEPTH, 128), sums)
     return resampled, propagator
 
 

time: 124 us -> 113 us (0.911)
  starting transfers between devices: 34.7 us -> 23.7 us
  blocking collectives: 56.1 us -> 54 us
    all_to_all x1, starting transfers between devices: 16.8 us -> 4.1 us  [local(): lax.all_to_all(out.reshape(reps, PER, DEPTH, 128), 'rep', 0, 0, tiled=True)]
    all_to_all x1, waiting for transfers between devices: 0.01 us -> 2.48 us  [local(): lax.all_to_all(out.reshape(reps, PER, DEPTH, 128), 'rep', 0, 0, tiled=True)]
    all_to_all x1, blocking collectives: 40.3 us -> 38.3 us  [local(): pieces = lax.all_to_all(pieces, 'rep', 0, 0, tiled=True)]
    ppermute x4, waiting for transfers between devices: 13.5 us -> 11.8 us  [local(): sums = sums + lax.ppermute(sums, 'gz', [(i, i ^ step) for i in range(ring)])]
    ppermute x4, starting transfers between devices: 8.71 us -> 10.4 us  [local(): sums = sums + lax.ppermute(sums, 'gz', [(i, i ^ step) for i in range(ring)])]
  transfers between devices with their start and end apart: 7 -> 7, of which waited for: 5 -> 6; matrix products, arithmetic and copies ran while one was open for 1% -> 1% of each run, Pallas kernels for 2% -> 2%
where the time goes in v3:
time: 113 us; the launch traced here: 112 us
  blocking collectives  54 us (48%)
  starting transfers between devices  23.7 us (21%)
  Pallas kernels  15.7 us (14%)
  waiting for transfers between devices  14.7 us (13%)
  local copies, waits for them, and re-layouts  2.81 us (2%)
    all_to_all x1, blocking collectives, local(): pieces = lax.all_to_all(pieces, 'rep', 0, 0, tiled=True)  38.3 us
    all_to_all x1, blocking collectives, local(): lax.all_to_all(chunks.reshape(ring, 8 * LIVE, 128), 'gz', 0, 0, tiled=True)  15.8 us
    ppermute x4, waiting for transfers between devices, local(): sums = sums + lax.ppermute(sums, 'gz', [(i, i ^ step) for i in range(ring)])  11.8 us
    ppermute x4, starting transfers between devices, local(): sums = sums + lax.ppermute(sums, 'gz', [(i, i ^ step) for i in range(ring)])  10.4 us
    ppermute x1, starting transfers between devices, local(): hi = lax.ppermute(down, 'gz', [(b, a) for a, b in forward])  7.26 us
    pallas_call x1, Pallas kernels, sweeps(): pl.pallas_call(sweep_kernel, out_shape=[shape(ROWS * BLOCKS * DEPTH, 128)...  4.52 us
    all_to_all x1, starting transfers between devices, local(): lax.all_to_all(out.reshape(reps, PER, DEPTH, 128), 'rep', 0, 0, tiled=True)  4.1 us
    pallas_call x1, Pallas kernels, bins(): pl.pallas_call(bins_kernel, out_shape=shape(devices, BLOCKS, DEPTH, 128),...  2.73 us
  transfers between devices with their start and end apart: 7, of which 6 were waited for; matrix products, arithmetic and copies ran while one was open for 1% of the time, Pallas kernels for 2%

profile of v3, /device:TPU:2, one launch (start us, length us, event | category | flops | bytes accessed | tf_op | source)
XLA Modules:
  0.0 112.3 jit_solution(6186369195956976967)
XLA Ops:
  0.6 0.0 copy-start.3
  0.6 2.7 %edges.1 = (f32[10,32,128]{2,1,0:T(8,128)}, f32[10,32,128]{2,1,0:T(8,128)}) custom-call(s32[1]{0:T(128)S(6)} %mul.3.base_ref, s32[192]{0:T(256)} %counts_ref.3, f32[6,128,128]{2,1,0:T(8,128)} %bitcast.27, f32[2,6,128,128]{3,2,1,0:T(8,128)} %bitcast.24, f32[128,128]{1,0:T(8,128)} %bitcast.32), custom_call_target="tpu_custom_call" | custom-call | tf_op jit(solution)/shard_map/edges/pallas_call | solution.py:284
  3.3 1.9 %collective-permute-start = (f32[10,32,128]{2,1,0:T(8,128)}, f32[10,32,128]{2,1,0:T(8,128)S(1)}, u32[]{:S(2)}, u32[]{:S(2)}) collective-permute-start(f32[10,32,128]{2,1,0:T(8,128)} %get-tuple-element.16), channel_id=1, source_target_pairs={{0,1},{1,2},{2,3},{3,4},{4,5},{5,6},{6,7},{7,8},{8,9},{9,10},{10,1... | collective-permute-start | bytes 491528 | tf_op jit(solution)/shard_map/ppermute | solution.py:376
  5.2 7.3 %collective-permute-start.1 = (f32[10,32,128]{2,1,0:T(8,128)}, f32[10,32,128]{2,1,0:T(8,128)S(1)}, u32[]{:S(2)}, u32[]{:S(2)}) collective-permute-start(f32[10,32,128]{2,1,0:T(8,128)} %get-tuple-element.17), channel_id=1, source_target_pairs={{1,0},{2,1},{3,2},{4,3},{5,4},{6,5},{7,6},{8,7},{9,8},{10,9},{11,1... | collective-permute-start | bytes 491528 | tf_op jit(solution)/shard_map/ppermute | solution.py:377
  12.5 0.0 copy-done.3
  12.5 0.1 copy.15
  12.6 0.7 pad.4.bins_ref
  13.3 1.9 %plan.1 = (s32[1,192]{1,0:T(1,128)}, s32[32,128]{1,0:T(8,128)}, s32[128,128]{1,0:T(8,128)}) custom-call(s32[1,192]{1,0:T(1,128)} %bitcast.35, s32[1,192]{1,0:T(1,128)} %bitcast.36, s32[4,64,128]{2,1,0:T(8,128)} %pad.4.bins_ref), custom_call_target="tpu_custom_call" | custom-call | tf_op jit(solution)/shard_map/plan/pallas_call | solution.py:302
  15.2 0.0 collective-permute-done.lo
  15.2 0.0 copy-start.1
  15.2 0.4 collective-permute-done.1.hi
  15.6 0.0 copy-start.2
  15.6 0.2 copy-done.1
  15.9 0.4 copy-done.2
  16.3 4.5 %sweeps.1 = (f32[512,128]{1,0:T(8,128)}, f32[384,128]{1,0:T(8,128)}) custom-call(s32[1]{0:T(128)S(6)} %mul.3.base_ref, s32[192]{0:T(256)} %counts_ref.3, f32[6,128,128]{2,1,0:T(8,128)} %bitcast.28, f32[2,6,128,128]{3,2,1,0:T(8,128)} %bitcast.25, f32[128,128]{1,0:T(8,128)} %bitcast.33, f32[10,32,128]{2,1,0:T(8,128)} %copy-done.1, f32[10,32,128]{2,1,0:T(8,128)} %copy-done.2, ...), custom_call_target="tpu_custom_call" | custom-call | tf_op jit(solution)/shard_map/sweeps/pallas_call | solution.py:316
  20.8 15.8 %all_to_all.15.chunks = f32[16,24,128]{2,1,0:T(8,128)} all-to-all(f32[16,24,128]{2,1,0:T(8,128)} %bitcast.34), channel_id=1, replica_groups=mesh['rep'=32,'gz'=16] {'gz'}, dimensions={0} | all-to-all | bytes 393216 | tf_op jit(solution)/shard_map/all_to_all | solution.py:381
  36.6 2.7 %bins.1 = f32[32,4,4,128]{3,2,1,0:T(4,128)} custom-call(s32[1]{0:T(128)} %bitcast.me_ref, f32[16,24,128]{2,1,0:T(8,128)} %all_to_all.15.chunks, s32[128,128]{1,0:T(8,128)} %get-tuple-element.25.map_ref, s32[32,128]{1,0:T(8,128)} %get-tuple-element.26.wide, bf16[2,128,128]{2,1,0:T(8,128)(2,1)} %constant.18.clone.along_z, ...), custom_call_target="tpu_custom_call", output_to_operand_aliasing={{}: (5, {})} | custom-call | tf_op jit(solution)/shard_map/bins/pallas_call | solution.py:333
  39.4 38.3 %all_to_all.16 = f32[32,4,4,128]{3,2,1,0:T(4,128)} all-to-all(f32[32,4,4,128]{3,2,1,0:T(4,128)} %bins.1), channel_id=1, replica_groups=mesh['rep'=32,'gz'=16] {'rep'}, dimensions={0} | all-to-all | bytes 524288 | tf_op jit(solution)/shard_map/all_to_all | solution.py:383
  77.6 1.9 %pick.1 = (f32[192,4,128]{2,1,0:T(4,128)}, f32[1,128]{1,0:T(1,128)}) custom-call(s32[192]{0:T(256)} %bitcast.37, f32[128,4,128]{2,1,0:T(4,128)} %bitcast.30), custom_call_target="tpu_custom_call" | custom-call | tf_op jit(solution)/shard_map/pick/pallas_call | solution.py:349
  79.5 4.1 %all-to-all-start.2 = ((f32[32,6,4,128]{3,2,1,0:T(4,128)}), f32[32,6,4,128]{3,2,1,0:T(4,128)S(1)}, u32[]{:S(2)}, u32[]{:S(2)}) async-start(f32[32,6,4,128]{3,2,1,0:T(4,128)} %bitcast.31), calls=%async_computation.2 | async-start | bytes 786432 | tf_op jit(solution)/shard_map/all_to_all | solution.py:385
  83.6 0.0 copy-start.4
  83.6 0.6 copy-done.4
  84.2 1.9 %collective-permute-start.2 = (f32[1,128]{1,0:T(1,128)S(1)}, f32[1,128]{1,0:T(1,128)S(1)}, u32[]{:S(2)}, u32[]{:S(2)}) collective-permute-start(f32[1,128]{1,0:T(1,128)S(1)} %copy-done.4), channel_id=1, source_target_pairs={{0,1},{1,0},{2,3},{3,2},{4,5},{5,4},{6,7},{7,6},{8,9},{9,8},{10,11... | collective-permute-start | bytes 1544 | tf_op jit(solution)/shard_map/ppermute | solution.py:388
  86.1 1.1 collective-permute-done.2
  87.2 2.5 %collective-permute-start.3 = (f32[1,128]{1,0:T(1,128)S(1)}, f32[1,128]{1,0:T(1,128)S(1)}, u32[]{:S(2)}, u32[]{:S(2)}) collective-permute-start(f32[1,128]{1,0:T(1,128)S(1)} %add.14), channel_id=1, source_target_pairs={{0,2},{1,3},{2,0},{3,1},{4,6},{5,7},{6,4},{7,5},{8,10},{9,11},{10,... | collective-permute-start | bytes 1544 | tf_op jit(solution)/shard_map/ppermute | solution.py:388
  89.8 2.9 %collective-permute-done.3 = f32[1,128]{1,0:T(1,128)S(1)} collective-permute-done((f32[1,128]{1,0:T(1,128)S(1)}, f32[1,128]{1,0:T(1,128)S(1)}, u32[]{:S(2)}, u32[]{:S(2)}) %collective-permute-start.3) | collective-permute-done | bytes 544 | tf_op jit(solution)/shard_map/ppermute | solution.py:388
  92.6 3.2 %collective-permute-start.4 = (f32[1,128]{1,0:T(1,128)S(1)}, f32[1,128]{1,0:T(1,128)S(1)}, u32[]{:S(2)}, u32[]{:S(2)}) collective-permute-start(f32[1,128]{1,0:T(1,128)S(1)} %add.15), channel_id=1, source_target_pairs={{0,4},{1,5},{2,6},{3,7},{4,0},{5,1},{6,2},{7,3},{8,12},{9,13},{10,... | collective-permute-start | bytes 1544 | tf_op jit(solution)/shard_map/ppermute | solution.py:388
  95.8 3.7 %collective-permute-done.4 = f32[1,128]{1,0:T(1,128)S(1)} collective-permute-done((f32[1,128]{1,0:T(1,128)S(1)}, f32[1,128]{1,0:T(1,128)S(1)}, u32[]{:S(2)}, u32[]{:S(2)}) %collective-permute-start.4) | collective-permute-done | bytes 544 | tf_op jit(solution)/shard_map/ppermute | solution.py:388
  99.6 2.8 %collective-permute-start.5 = (f32[1,128]{1,0:T(1,128)S(1)}, f32[1,128]{1,0:T(1,128)S(1)}, u32[]{:S(2)}, u32[]{:S(2)}) collective-permute-start(f32[1,128]{1,0:T(1,128)S(1)} %add.16), channel_id=1, source_target_pairs={{0,8},{1,9},{2,10},{3,11},{4,12},{5,13},{6,14},{7,15},{8,0},{9,1},... | collective-permute-start | bytes 1544 | tf_op jit(solution)/shard_map/ppermute | solution.py:388
  102.4 4.1 %collective-permute-done.5 = f32[1,128]{1,0:T(1,128)S(1)} collective-permute-done((f32[1,128]{1,0:T(1,128)S(1)}, f32[1,128]{1,0:T(1,128)S(1)}, u32[]{:S(2)}, u32[]{:S(2)}) %collective-permute-start.5) | collective-permute-done | bytes 544 | tf_op jit(solution)/shard_map/ppermute | solution.py:388
  106.5 0.6 add.17.sums_ref
  107.1 2.5 %all-to-all-done.2 = f32[32,6,4,128]{3,2,1,0:T(4,128)S(1)} async-done(((f32[32,6,4,128]{3,2,1,0:T(4,128)}), f32[32,6,4,128]{3,2,1,0:T(4,128)S(1)}, u32[]{:S(2)}, u32[]{:S(2)}) %all-to-all-start.2) | async-done | bytes 393248 | tf_op jit(solution)/shard_map/all_to_all | solution.py:385
  109.5 0.0 copy-start
  109.5 0.8 copy-done
  110.3 2.0 %finish.1 = (f32[6,4,4096]{2,1,0:T(4,128)}, f32[6,16]{1,0:T(8,128)}) custom-call(f32[192,4,128]{2,1,0:T(4,128)} %bitcast.26, f32[1,128]{1,0:T(1,128)} %add.17.sums_ref), custom_call_target="tpu_custom_call" | custom-call | tf_op jit(solution)/shard_map/finish/pallas_call | solution.py:359
  (3 shorter events, 0.0 us)
Async XLA Ops:
  0.6 11.9 %copy-start.3 = (s32[4,64,33]{1,0,2:T(4,128)S(1)}, s32[4,64,33]{1,0,2:T(4,128)}, u32[]{:S(2)}) copy-start(s32[4,64,33]{1,0,2:T(4,128)} %param.14) | copy-start | bytes 101380
  3.3 11.9 %collective-permute-start = (f32[10,32,128]{2,1,0:T(8,128)}, f32[10,32,128]{2,1,0:T(8,128)S(1)}, u32[]{:S(2)}, u32[]{:S(2)}) collective-permute-start(f32[10,32,128]{2,1,0:T(8,128)} %get-tuple-element.16), channel_id=1, source_target_pairs={{0,1},{1,2},{2,3},{3,4},{4,5},{5,6},{6,7},{7,8},{8,9},{9,10},{10,1... | collective-permute-start | bytes 491528 | tf_op jit(solution)/shard_map/ppermute | solution.py:376
  5.2 10.4 %collective-permute-start.1 = (f32[10,32,128]{2,1,0:T(8,128)}, f32[10,32,128]{2,1,0:T(8,128)S(1)}, u32[]{:S(2)}, u32[]{:S(2)}) collective-permute-start(f32[10,32,128]{2,1,0:T(8,128)} %get-tuple-element.17), channel_id=1, source_target_pairs={{1,0},{2,1},{3,2},{4,3},{5,4},{6,5},{7,6},{8,7},{9,8},{10,9},{11,1... | collective-permute-start | bytes 491528 | tf_op jit(solution)/shard_map/ppermute | solution.py:377
  15.2 0.7 copy-start.1
  15.6 0.7 copy-start.2
  79.5 30.0 %all-to-all-start.2 = ((f32[32,6,4,128]{3,2,1,0:T(4,128)}), f32[32,6,4,128]{3,2,1,0:T(4,128)S(1)}, u32[]{:S(2)}, u32[]{:S(2)}) async-start(f32[32,6,4,128]{3,2,1,0:T(4,128)} %bitcast.31), calls=%async_computation.2 | async-start | bytes 786432 | tf_op jit(solution)/shard_map/all_to_all | solution.py:385
  83.6 0.6 copy-start.4
  84.2 3.0 %collective-permute-start.2 = (f32[1,128]{1,0:T(1,128)S(1)}, f32[1,128]{1,0:T(1,128)S(1)}, u32[]{:S(2)}, u32[]{:S(2)}) collective-permute-start(f32[1,128]{1,0:T(1,128)S(1)} %copy-done.4), channel_id=1, source_target_pairs={{0,1},{1,0},{2,3},{3,2},{4,5},{5,4},{6,7},{7,6},{8,9},{9,8},{10,11... | collective-permute-start | bytes 1544 | tf_op jit(solution)/shard_map/ppermute | solution.py:388
  87.2 5.4 %collective-permute-start.3 = (f32[1,128]{1,0:T(1,128)S(1)}, f32[1,128]{1,0:T(1,128)S(1)}, u32[]{:S(2)}, u32[]{:S(2)}) collective-permute-start(f32[1,128]{1,0:T(1,128)S(1)} %add.14), channel_id=1, source_target_pairs={{0,2},{1,3},{2,0},{3,1},{4,6},{5,7},{6,4},{7,5},{8,10},{9,11},{10,... | collective-permute-start | bytes 1544 | tf_op jit(solution)/shard_map/ppermute | solution.py:388
  92.6 6.9 %collective-permute-start.4 = (f32[1,128]{1,0:T(1,128)S(1)}, f32[1,128]{1,0:T(1,128)S(1)}, u32[]{:S(2)}, u32[]{:S(2)}) collective-permute-start(f32[1,128]{1,0:T(1,128)S(1)} %add.15), channel_id=1, source_target_pairs={{0,4},{1,5},{2,6},{3,7},{4,0},{5,1},{6,2},{7,3},{8,12},{9,13},{10,... | collective-permute-start | bytes 1544 | tf_op jit(solution)/shard_map/ppermute | solution.py:388
  99.6 6.9 %collective-permute-start.5 = (f32[1,128]{1,0:T(1,128)S(1)}, f32[1,128]{1,0:T(1,128)S(1)}, u32[]{:S(2)}, u32[]{:S(2)}) collective-permute-start(f32[1,128]{1,0:T(1,128)S(1)} %add.16), channel_id=1, source_target_pairs={{0,8},{1,9},{2,10},{3,11},{4,12},{5,13},{6,14},{7,15},{8,0},{9,1},... | collective-permute-start | bytes 1544 | tf_op jit(solution)/shard_map/ppermute | solution.py:388
  109.5 0.8 copy-start

commit v4 on v3

--- a/solution.py
+++ b/solution.py
@@ -66,25 +66,58 @@
     return live
 
 
-def edges_kernel(base_ref, counts_ref, field, noise, masses, up, down, fbuf, nbuf, mbuf, sems):
+def planes(ref, *at):
+    return [ref[(*at, pl.ds(z, ROWS, stride=DEPTH), slice(None))] for z in range(DEPTH)]
+
+
+def beside(v, lane):
+    swapped = pltpu.roll(v, L, axis=1)
+    rows = v.shape[0]
+    y = swapped + jnp.where(lane < L, pltpu.roll(swapped, 1, axis=0), pltpu.roll(swapped, rows - 1, axis=0))
+    inner = lane & (L - 1)
+    low = pltpu.roll(jnp.where(inner == L - 1, swapped, v), 1, axis=1)
+    high = pltpu.roll(jnp.where(inner == 0, swapped, v), 127, axis=1)
+    return y + (low + high)
+
+
+KICK = float(np.sqrt(np.float32(0.2)))
+
+
+def update(center, near, mass, noise_now, lane):
+    near = near + beside(center, lane)
+    return center * (0.4 - 0.1 * mass - 0.05 * (center * center)) + 0.1 * near + KICK * noise_now
+
+
+def edges_kernel(base_ref, counts_ref, field, noise, masses, up, down, mid, fbuf, nbuf, mbuf, sems):
     live = live_of(counts_ref, base_ref[0])
-    copies = [pltpu.make_async_copy(masses, mbuf, sems.at[2 * LIVE])]
+    first = pltpu.make_async_copy(masses, mbuf, sems.at[2 * LIVE])
+    first.start()
+    copies = []
     for k in range(LIVE):
-        copies.append(pltpu.make_async_copy(field.at[live[k]], fbuf.at[k], sems.at[2 * k]))
-        copies.append(pltpu.make_async_copy(noise.at[0, live[k]], nbuf.at[k], sems.at[2 * k + 1]))
-    for copy in copies:
-        copy.start()
-    for copy in copies:
-        copy.wait()
+        copies.append(
+            [
+                pltpu.make_async_copy(field.at[live[k]], fbuf.at[k], sems.at[2 * k]),
+                pltpu.make_async_copy(noise.at[0, live[k]], nbuf.at[k], sems.at[2 * k + 1]),
+            ]
+        )
+        for copy in copies[-1]:
+            copy.start()
+    first.wait()
+    lane = lax.broadcasted_iota(jnp.int32, (ROWS, 128), 1)
+    mass = planes(mbuf)
     for k in range(LIVE):
-        up[2 * k] = fbuf[k, pl.ds(2, ROWS, stride=DEPTH), :]
-        up[2 * k + 1] = fbuf[k, pl.ds(3, ROWS, stride=DEPTH), :]
-        down[2 * k] = fbuf[k, pl.ds(0, ROWS, stride=DEPTH), :]
-        down[2 * k + 1] = fbuf[k, pl.ds(1, ROWS, stride=DEPTH), :]
-        up[2 * LIVE + k] = nbuf[k, pl.ds(3, ROWS, stride=DEPTH), :]
-        down[2 * LIVE + k] = nbuf[k, pl.ds(0, ROWS, stride=DEPTH), :]
-    up[3 * LIVE] = mbuf[pl.ds(3, ROWS, stride=DEPTH), :]
-    down[3 * LIVE] = mbuf[pl.ds(0, ROWS, stride=DEPTH), :]
+        for copy in copies[k]:
+            copy.wait()
+        old = planes(fbuf, k)
+        kicks = planes(nbuf, k)
+        near = (old[1], old[0] + old[2], old[1] + old[3], old[2])
+        new = [update(old[z], near[z], mass[z], kicks[z], lane) for z in range(DEPTH)]
+        down[2 * k] = old[0]
+        down[2 * k + 1] = new[0]
+        up[2 * k] = old[3]
+        up[2 * k + 1] = new[3]
+        mid[2 * k] = new[1]
+        mid[2 * k + 1] = new[2]
 
 
 def floor_div(value, by):
@@ -133,54 +166,31 @@
         map_ref[pair * L : (pair + 1) * L, :] = jnp.where(lane < L, halves[0], pltpu.roll(halves[1], L, axis=1))
 
 
-def beside(v, lane):
-    swapped = pltpu.roll(v, L, axis=1)
-    rows = v.shape[0]
-    y = swapped + jnp.where(lane < L, pltpu.roll(swapped, 1, axis=0), pltpu.roll(swapped, rows - 1, axis=0))
-    inner = lane & (L - 1)
-    low = pltpu.roll(jnp.where(inner == L - 1, swapped, v), 1, axis=1)
-    high = pltpu.roll(jnp.where(inner == 0, swapped, v), 127, axis=1)
-    return y + (low + high)
-
-
 def sweep_kernel(
-    base_ref, counts_ref, field, noise, masses, lo, hi, along_x, along_y, pieces, chunks, fbuf, nbuf, mbuf, sems
+    base_ref, counts_ref, noise, masses, lo, hi, up, down, mid, along_x, along_y, pieces, chunks, nbuf, mbuf, sems
 ):
     live = live_of(counts_ref, base_ref[0])
-    first = pltpu.make_async_copy(masses, mbuf, sems.at[3 * LIVE])
+    first = pltpu.make_async_copy(masses, mbuf, sems.at[LIVE])
     first.start()
-    copies = []
-    for k in range(LIVE):
-        copies.append(
-            [
-                pltpu.make_async_copy(field.at[live[k]], fbuf.at[k], sems.at[3 * k]),
-                pltpu.make_async_copy(noise.at[0, live[k]], nbuf.at[0, k], sems.at[3 * k + 1]),
-                pltpu.make_async_copy(noise.at[1, live[k]], nbuf.at[1, k], sems.at[3 * k + 2]),
-            ]
-        )
-        for copy in copies[-1]:
-            copy.start()
+    copies = [pltpu.make_async_copy(noise.at[1, live[k]], nbuf.at[k], sems.at[k]) for k in range(LIVE)]
+    for copy in copies:
+        copy.start()
     first.wait()
     lane = lax.broadcasted_iota(jnp.int32, (ROWS, 128), 1)
-    kick = float(np.sqrt(np.float32(0.2)))
-
-    def update(center, below, above, mass, noise_now):
-        near = below + above + beside(center, lane)
-        return center * (0.4 - 0.1 * mass - 0.05 * (center * center)) + 0.1 * near + kick * noise_now
-
-    def planes(ref, *at):
-        return [ref[(*at, pl.ds(z, ROWS, stride=DEPTH), slice(None))] for z in range(DEPTH)]
-
-    mass = [lo[3 * LIVE]] + planes(mbuf) + [hi[3 * LIVE]]
+    mass = planes(mbuf)
     left = []
     for k in range(LIVE):
-        for copy in copies[k]:
-            copy.wait()
-        old = [lo[2 * k], lo[2 * k + 1]] + planes(fbuf, k) + [hi[2 * k], hi[2 * k + 1]]
-        kicks = [lo[2 * LIVE + k]] + planes(nbuf, 0, k) + [hi[2 * LIVE + k]]
-        mid = [update(old[p + 1], old[p], old[p + 2], mass[p], kicks[p]) for p in range(DEPTH + 2)]
-        kicks = planes(nbuf, 1, k)
-        new = [update(mid[p + 1], mid[p], mid[p + 2], mass[p + 1], kicks[p]) for p in range(DEPTH)]
+        copies[k].wait()
+        now = [
+            lo[2 * k + 1] + 0.1 * down[2 * k],
+            down[2 * k + 1] + 0.1 * lo[2 * k],
+            mid[2 * k],
+            mid[2 * k + 1],
+            up[2 * k + 1] + 0.1 * hi[2 * k],
+            hi[2 * k + 1] + 0.1 * up[2 * k],
+        ]
+        kicks = planes(nbuf, k)
+        new = [update(now[p + 1], now[p] + now[p + 2], mass[p], kicks[p], lane) for p in range(DEPTH)]
         for z in range(DEPTH):
             pieces[pl.ds(k * DEPTH + z, ROWS, stride=BLOCKS * DEPTH), :] = new[z]
         left += [jnp.concatenate(new[0:2], axis=1), jnp.concatenate(new[2:4], axis=1)]
@@ -283,9 +293,9 @@
 def edges(base, counts, field, noise, masses):
     return pl.pallas_call(
         edges_kernel,
-        out_shape=[shape(3 * LIVE + 1, ROWS, 128)] * 2,
+        out_shape=[shape(2 * LIVE, ROWS, 128)] * 3,
         in_specs=[spec(SMEM)] * 2 + [spec(pl.ANY)] * 3,
-        out_specs=[spec(VMEM)] * 2,
+        out_specs=[spec(VMEM)] * 3,
         scratch_shapes=[
             VMEM((LIVE, 128, 128), jnp.float32),
             VMEM((LIVE, 128, 128), jnp.float32),
@@ -312,20 +322,19 @@
     )(counts.reshape(1, total), dest_slots.reshape(1, total), padded)
 
 
-def sweeps(base, counts, field, noise, masses, lo, hi, along_x, along_y):
+def sweeps(base, counts, noise, masses, *blocks):
     return pl.pallas_call(
         sweep_kernel,
         out_shape=[shape(ROWS * BLOCKS * DEPTH, 128), shape(16 * 8 * LIVE, 128)],
-        in_specs=[spec(SMEM)] * 2 + [spec(pl.ANY)] * 3 + [spec(VMEM)] * 4,
+        in_specs=[spec(SMEM)] * 2 + [spec(pl.ANY)] * 2 + [spec(VMEM)] * 7,
         out_specs=[spec(VMEM)] * 2,
         scratch_shapes=[
             VMEM((LIVE, 128, 128), jnp.float32),
-            VMEM((2, LIVE, 128, 128), jnp.float32),
             VMEM((128, 128), jnp.float32),
-            pltpu.SemaphoreType.DMA((3 * LIVE + 1,)),
+            pltpu.SemaphoreType.DMA((LIVE + 1,)),
         ],
         name="sweeps",
-    )(base, counts, field, noise, masses, lo, hi, along_x, along_y)
+    )(base, counts, noise, masses, *blocks)
 
 
 def bins(me, chunks, place, wide, along_z, pieces):
@@ -370,13 +379,13 @@
     me = lax.axis_index("rep").astype(jnp.int32).reshape(1)
     base = me * PER
     field, noise, mass = rows_view(lattice_field), rows_view(langevin_noise), rows_view(masses)
-    up, down = edges(base, counts, field, noise, mass)
+    up, down, mid = edges(base, counts, field, noise, mass)
     ring = lax.axis_size("gz")
     forward = [(i, (i + 1) % ring) for i in range(ring)]
     lo = lax.ppermute(up, "gz", forward)
     hi = lax.ppermute(down, "gz", [(b, a) for a, b in forward])
     lo, hi, item, wide, place = lax.optimization_barrier((lo, hi, *plan(counts, dest_slots, mode_bins)))
-    pieces, chunks = sweeps(base, counts, field, noise, mass, lo, hi, along_x, along_y)
+    pieces, chunks = sweeps(base, counts, noise, mass, lo, hi, up, down, mid, along_x, along_y)
     reps = lax.axis_size("rep")
     chunks = lax.all_to_all(chunks.reshape(ring, 8 * LIVE, 128), "gz", 0, 0, tiled=True)
     pieces = bins(me, chunks, place, wide, along_z, pieces.reshape(reps, BLOCKS, DEPTH, 128))

time: 113 us -> 112 us (level)
  transfers between devices with their start and end apart: 7 -> 7, of which waited for: 6 -> 5; matrix products, arithmetic and copies ran while one was open for 1% -> 1% of each run, Pallas kernels for 2% -> 2%
where the time goes in v4:
time: 112 us; the launch traced here: 111 us
  blocking collectives  53.7 us (48%)
  starting transfers between devices  23.7 us (21%)
  Pallas kernels  15.3 us (14%)
  waiting for transfers between devices  14.3 us (13%)
  local copies, waits for them, and re-layouts  2.79 us (2%)
    all_to_all x1, blocking collectives, local(): pieces = lax.all_to_all(pieces, 'rep', 0, 0, tiled=True)  38.3 us
    all_to_all x1, blocking collectives, local(): lax.all_to_all(chunks.reshape(ring, 8 * LIVE, 128), 'gz', 0, 0, tiled=True)  15.5 us
    ppermute x4, waiting for transfers between devices, local(): sums = sums + lax.ppermute(sums, 'gz', [(i, i ^ step) for i in range(ring)])  11.8 us
    ppermute x4, starting transfers between devices, local(): sums = sums + lax.ppermute(sums, 'gz', [(i, i ^ step) for i in range(ring)])  10.4 us
    ppermute x1, starting transfers between devices, local(): hi = lax.ppermute(down, 'gz', [(b, a) for a, b in forward])  7.26 us
    all_to_all x1, starting transfers between devices, local(): lax.all_to_all(out.reshape(reps, PER, DEPTH, 128), 'rep', 0, 0, tiled=True)  4.1 us
    pallas_call x1, Pallas kernels, sweeps(): pl.pallas_call(sweep_kernel, out_shape=[shape(ROWS * BLOCKS * DEPTH, 128)...  3.85 us
    pallas_call x1, Pallas kernels, edges(): pl.pallas_call(edges_kernel, out_shape=[shape(2 * LIVE, ROWS, 128)] * 3,...  3.01 us
  transfers between devices with their start and end apart: 7, of which 5 were waited for; matrix products, arithmetic and copies ran while one was open for 1% of the time, Pallas kernels for 2%

profile of v4, /device:TPU:2, one launch (start us, length us, event | category | flops | bytes accessed | tf_op | source)
XLA Modules:
  0.0 111.2 jit_solution(5896770517792167604)
XLA Ops:
  0.6 0.0 copy-start.3
  0.6 3.0 %edges.1 = (f32[6,32,128]{2,1,0:T(8,128)}, f32[6,32,128]{2,1,0:T(8,128)}, f32[6,32,128]{2,1,0:T(8,128)}) custom-call(s32[1]{0:T(128)S(6)} %mul.3.base_ref, s32[192]{0:T(256)} %counts_ref.3, f32[6,128,128]{2,1,0:T(8,128)} %bitcast.30, f32[2,6,128,128]{3,2,1,0:T(8,128)} %bitcast.24, f32[128,128]{1,0:T(8,128)} %bitcast.31), custom_call_target="tpu_custom_call" | custom-call | tf_op jit(solution)/shard_map/edges/pallas_call | solution.py:294
  3.7 1.9 %collective-permute-start = (f32[6,32,128]{2,1,0:T(8,128)}, f32[6,32,128]{2,1,0:T(8,128)S(1)}, u32[]{:S(2)}, u32[]{:S(2)}) collective-permute-start(f32[6,32,128]{2,1,0:T(8,128)} %get-tuple-element.17.up), channel_id=1, source_target_pairs={{0,1},{1,2},{2,3},{3,4},{4,5},{5,6},{6,7},{7,8},{8,9},{9,10},{10,1... | collective-permute-start | bytes 294920 | tf_op jit(solution)/shard_map/ppermute | solution.py:385
  5.6 7.3 %collective-permute-start.1 = (f32[6,32,128]{2,1,0:T(8,128)}, f32[6,32,128]{2,1,0:T(8,128)S(1)}, u32[]{:S(2)}, u32[]{:S(2)}) collective-permute-start(f32[6,32,128]{2,1,0:T(8,128)} %get-tuple-element.18.down), channel_id=1, source_target_pairs={{1,0},{2,1},{3,2},{4,3},{5,4},{6,5},{7,6},{8,7},{9,8},{10,9},{11,1... | collective-permute-start | bytes 294920 | tf_op jit(solution)/shard_map/ppermute | solution.py:386
  12.9 0.0 copy-done.3
  12.9 0.1 copy.15
  13.0 0.7 pad.4.bins_ref
  13.7 1.9 %plan.1 = (s32[1,192]{1,0:T(1,128)}, s32[32,128]{1,0:T(8,128)}, s32[128,128]{1,0:T(8,128)}) custom-call(s32[1,192]{1,0:T(1,128)} %bitcast.34, s32[1,192]{1,0:T(1,128)} %bitcast.35, s32[4,64,128]{2,1,0:T(8,128)} %pad.4.bins_ref), custom_call_target="tpu_custom_call" | custom-call | tf_op jit(solution)/shard_map/plan/pallas_call | solution.py:312
  15.6 0.0 collective-permute-done.lo
  15.6 0.0 copy-start.1
  15.6 0.0 collective-permute-done.1.hi
  15.6 0.0 copy-start.2
  15.6 0.6 copy-done.1
  16.2 0.0 copy-done.2
  16.2 3.8 %sweeps.1 = (f32[512,128]{1,0:T(8,128)}, f32[384,128]{1,0:T(8,128)}) custom-call(s32[1]{0:T(128)S(6)} %mul.3.base_ref, s32[192]{0:T(256)} %counts_ref.3, f32[2,6,128,128]{3,2,1,0:T(8,128)} %bitcast.25, f32[128,128]{1,0:T(8,128)} %bitcast.32, f32[6,32,128]{2,1,0:T(8,128)} %copy-done.1, f32[6,32,128]{2,1,0:T(8,128)} %copy-done.2, ...), custom_call_target="tpu_custom_call" | custom-call | tf_op jit(solution)/shard_map/sweeps/pallas_call | solution.py:326
  20.1 15.5 %all_to_all.15.chunks = f32[16,24,128]{2,1,0:T(8,128)} all-to-all(f32[16,24,128]{2,1,0:T(8,128)} %bitcast.33), channel_id=1, replica_groups=mesh['rep'=32,'gz'=16] {'gz'}, dimensions={0} | all-to-all | bytes 393216 | tf_op jit(solution)/shard_map/all_to_all | solution.py:390
  35.6 2.7 %bins.1 = f32[32,4,4,128]{3,2,1,0:T(4,128)} custom-call(s32[1]{0:T(128)} %bitcast.me_ref, f32[16,24,128]{2,1,0:T(8,128)} %all_to_all.15.chunks, s32[128,128]{1,0:T(8,128)} %get-tuple-element.27.map_ref, s32[32,128]{1,0:T(8,128)} %get-tuple-element.28.wide, bf16[2,128,128]{2,1,0:T(8,128)(2,1)} %constant.18.clone.along_z, ...), custom_call_target="tpu_custom_call", output_to_operand_aliasing={{}: (5, {})} | custom-call | tf_op jit(solution)/shard_map/bins/pallas_call | solution.py:342
  38.3 38.3 %all_to_all.16 = f32[32,4,4,128]{3,2,1,0:T(4,128)} all-to-all(f32[32,4,4,128]{3,2,1,0:T(4,128)} %bins.1), channel_id=1, replica_groups=mesh['rep'=32,'gz'=16] {'rep'}, dimensions={0} | all-to-all | bytes 524288 | tf_op jit(solution)/shard_map/all_to_all | solution.py:392
  76.6 1.9 %pick.1 = (f32[192,4,128]{2,1,0:T(4,128)}, f32[1,128]{1,0:T(1,128)}) custom-call(s32[192]{0:T(256)} %bitcast.36, f32[128,4,128]{2,1,0:T(4,128)} %bitcast.28), custom_call_target="tpu_custom_call" | custom-call | tf_op jit(solution)/shard_map/pick/pallas_call | solution.py:358
  78.4 4.1 %all-to-all-start.2 = ((f32[32,6,4,128]{3,2,1,0:T(4,128)}), f32[32,6,4,128]{3,2,1,0:T(4,128)S(1)}, u32[]{:S(2)}, u32[]{:S(2)}) async-start(f32[32,6,4,128]{3,2,1,0:T(4,128)} %bitcast.29), calls=%async_computation.2 | async-start | bytes 786432 | tf_op jit(solution)/shard_map/all_to_all | solution.py:394
  82.5 0.0 copy-start.4
  82.5 0.6 copy-done.4
  83.1 1.9 %collective-permute-start.2 = (f32[1,128]{1,0:T(1,128)S(1)}, f32[1,128]{1,0:T(1,128)S(1)}, u32[]{:S(2)}, u32[]{:S(2)}) collective-permute-start(f32[1,128]{1,0:T(1,128)S(1)} %copy-done.4), channel_id=1, source_target_pairs={{0,1},{1,0},{2,3},{3,2},{4,5},{5,4},{6,7},{7,6},{8,9},{9,8},{10,11... | collective-permute-start | bytes 1544 | tf_op jit(solution)/shard_map/ppermute | solution.py:397
  85.0 1.1 collective-permute-done.2
  86.1 2.5 %collective-permute-start.3 = (f32[1,128]{1,0:T(1,128)S(1)}, f32[1,128]{1,0:T(1,128)S(1)}, u32[]{:S(2)}, u32[]{:S(2)}) collective-permute-start(f32[1,128]{1,0:T(1,128)S(1)} %add.14), channel_id=1, source_target_pairs={{0,2},{1,3},{2,0},{3,1},{4,6},{5,7},{6,4},{7,5},{8,10},{9,11},{10,... | collective-permute-start | bytes 1544 | tf_op jit(solution)/shard_map/ppermute | solution.py:397
  88.7 2.9 %collective-permute-done.3 = f32[1,128]{1,0:T(1,128)S(1)} collective-permute-done((f32[1,128]{1,0:T(1,128)S(1)}, f32[1,128]{1,0:T(1,128)S(1)}, u32[]{:S(2)}, u32[]{:S(2)}) %collective-permute-start.3) | collective-permute-done | bytes 544 | tf_op jit(solution)/shard_map/ppermute | solution.py:397
  91.6 3.2 %collective-permute-start.4 = (f32[1,128]{1,0:T(1,128)S(1)}, f32[1,128]{1,0:T(1,128)S(1)}, u32[]{:S(2)}, u32[]{:S(2)}) collective-permute-start(f32[1,128]{1,0:T(1,128)S(1)} %add.15), channel_id=1, source_target_pairs={{0,4},{1,5},{2,6},{3,7},{4,0},{5,1},{6,2},{7,3},{8,12},{9,13},{10,... | collective-permute-start | bytes 1544 | tf_op jit(solution)/shard_map/ppermute | solution.py:397
  94.7 3.7 %collective-permute-done.4 = f32[1,128]{1,0:T(1,128)S(1)} collective-permute-done((f32[1,128]{1,0:T(1,128)S(1)}, f32[1,128]{1,0:T(1,128)S(1)}, u32[]{:S(2)}, u32[]{:S(2)}) %collective-permute-start.4) | collective-permute-done | bytes 544 | tf_op jit(solution)/shard_map/ppermute | solution.py:397
  98.5 2.8 %collective-permute-start.5 = (f32[1,128]{1,0:T(1,128)S(1)}, f32[1,128]{1,0:T(1,128)S(1)}, u32[]{:S(2)}, u32[]{:S(2)}) collective-permute-start(f32[1,128]{1,0:T(1,128)S(1)} %add.16), channel_id=1, source_target_pairs={{0,8},{1,9},{2,10},{3,11},{4,12},{5,13},{6,14},{7,15},{8,0},{9,1},... | collective-permute-start | bytes 1544 | tf_op jit(solution)/shard_map/ppermute | solution.py:397
  101.3 4.1 %collective-permute-done.5 = f32[1,128]{1,0:T(1,128)S(1)} collective-permute-done((f32[1,128]{1,0:T(1,128)S(1)}, f32[1,128]{1,0:T(1,128)S(1)}, u32[]{:S(2)}, u32[]{:S(2)}) %collective-permute-start.5) | collective-permute-done | bytes 544 | tf_op jit(solution)/shard_map/ppermute | solution.py:397
  105.4 0.6 add.17.sums_ref
  106.0 2.5 %all-to-all-done.2 = f32[32,6,4,128]{3,2,1,0:T(4,128)S(1)} async-done(((f32[32,6,4,128]{3,2,1,0:T(4,128)}), f32[32,6,4,128]{3,2,1,0:T(4,128)S(1)}, u32[]{:S(2)}, u32[]{:S(2)}) %all-to-all-start.2) | async-done | bytes 393248 | tf_op jit(solution)/shard_map/all_to_all | solution.py:394
  108.5 0.0 copy-start
  108.5 0.8 copy-done
  109.2 2.0 %finish.1 = (f32[6,4,4096]{2,1,0:T(4,128)}, f32[6,16]{1,0:T(8,128)}) custom-call(f32[192,4,128]{2,1,0:T(4,128)} %bitcast.26, f32[1,128]{1,0:T(1,128)} %add.17.sums_ref), custom_call_target="tpu_custom_call" | custom-call | tf_op jit(solution)/shard_map/finish/pallas_call | solution.py:368
  (3 shorter events, 0.0 us)
Async XLA Ops:
  0.6 12.2 %copy-start.3 = (s32[4,64,33]{1,0,2:T(4,128)S(1)}, s32[4,64,33]{1,0,2:T(4,128)}, u32[]{:S(2)}) copy-start(s32[4,64,33]{1,0,2:T(4,128)} %param.14) | copy-start | bytes 101380
  3.7 11.9 %collective-permute-start = (f32[6,32,128]{2,1,0:T(8,128)}, f32[6,32,128]{2,1,0:T(8,128)S(1)}, u32[]{:S(2)}, u32[]{:S(2)}) collective-permute-start(f32[6,32,128]{2,1,0:T(8,128)} %get-tuple-element.17.up), channel_id=1, source_target_pairs={{0,1},{1,2},{2,3},{3,4},{4,5},{5,6},{6,7},{7,8},{8,9},{9,10},{10,1... | collective-permute-start | bytes 294920 | tf_op jit(solution)/shard_map/ppermute | solution.py:385
  5.6 10.0 %collective-permute-start.1 = (f32[6,32,128]{2,1,0:T(8,128)}, f32[6,32,128]{2,1,0:T(8,128)S(1)}, u32[]{:S(2)}, u32[]{:S(2)}) collective-permute-start(f32[6,32,128]{2,1,0:T(8,128)} %get-tuple-element.18.down), channel_id=1, source_target_pairs={{1,0},{2,1},{3,2},{4,3},{5,4},{6,5},{7,6},{8,7},{9,8},{10,9},{11,1... | collective-permute-start | bytes 294920 | tf_op jit(solution)/shard_map/ppermute | solution.py:386
  15.6 0.6 copy-start.1
  15.6 0.7 copy-start.2
  78.4 30.0 %all-to-all-start.2 = ((f32[32,6,4,128]{3,2,1,0:T(4,128)}), f32[32,6,4,128]{3,2,1,0:T(4,128)S(1)}, u32[]{:S(2)}, u32[]{:S(2)}) async-start(f32[32,6,4,128]{3,2,1,0:T(4,128)} %bitcast.29), calls=%async_computation.2 | async-start | bytes 786432 | tf_op jit(solution)/shard_map/all_to_all | solution.py:394
  82.5 0.6 copy-start.4
  83.1 3.0 %collective-permute-start.2 = (f32[1,128]{1,0:T(1,128)S(1)}, f32[1,128]{1,0:T(1,128)S(1)}, u32[]{:S(2)}, u32[]{:S(2)}) collective-permute-start(f32[1,128]{1,0:T(1,128)S(1)} %copy-done.4), channel_id=1, source_target_pairs={{0,1},{1,0},{2,3},{3,2},{4,5},{5,4},{6,7},{7,6},{8,9},{9,8},{10,11... | collective-permute-start | bytes 1544 | tf_op jit(solution)/shard_map/ppermute | solution.py:397
  86.1 5.4 %collective-permute-start.3 = (f32[1,128]{1,0:T(1,128)S(1)}, f32[1,128]{1,0:T(1,128)S(1)}, u32[]{:S(2)}, u32[]{:S(2)}) collective-permute-start(f32[1,128]{1,0:T(1,128)S(1)} %add.14), channel_id=1, source_target_pairs={{0,2},{1,3},{2,0},{3,1},{4,6},{5,7},{6,4},{7,5},{8,10},{9,11},{10,... | collective-permute-start | bytes 1544 | tf_op jit(solution)/shard_map/ppermute | solution.py:397
  91.6 6.9 %collective-permute-start.4 = (f32[1,128]{1,0:T(1,128)S(1)}, f32[1,128]{1,0:T(1,128)S(1)}, u32[]{:S(2)}, u32[]{:S(2)}) collective-permute-start(f32[1,128]{1,0:T(1,128)S(1)} %add.15), channel_id=1, source_target_pairs={{0,4},{1,5},{2,6},{3,7},{4,0},{5,1},{6,2},{7,3},{8,12},{9,13},{10,... | collective-permute-start | bytes 1544 | tf_op jit(solution)/shard_map/ppermute | solution.py:397
  98.5 6.9 %collective-permute-start.5 = (f32[1,128]{1,0:T(1,128)S(1)}, f32[1,128]{1,0:T(1,128)S(1)}, u32[]{:S(2)}, u32[]{:S(2)}) collective-permute-start(f32[1,128]{1,0:T(1,128)S(1)} %add.16), channel_id=1, source_target_pairs={{0,8},{1,9},{2,10},{3,11},{4,12},{5,13},{6,14},{7,15},{8,0},{9,1},... | collective-permute-start | bytes 1544 | tf_op jit(solution)/shard_map/ppermute | solution.py:397
  108.5 0.8 copy-start

commit v5 on v4

--- a/solution.py
+++ b/solution.py
@@ -14,6 +14,7 @@
 ROWS = 32
 PER = 6
 BLOCKS = LIVE + 1
+GRANT = 8 << 20
 
 VMEM = pltpu.VMEM
 SMEM = pltpu.SMEM
@@ -88,7 +89,8 @@
     return center * (0.4 - 0.1 * mass - 0.05 * (center * center)) + 0.1 * near + KICK * noise_now
 
 
-def edges_kernel(base_ref, counts_ref, field, noise, masses, up, down, mid, fbuf, nbuf, mbuf, sems):
+def edges_kernel(base_ref, odd_ref, counts_ref, field, noise, masses, near_out, far_out, mid, fbuf, nbuf, mbuf, sems):
+    odd = odd_ref[0] > 0
     live = live_of(counts_ref, base_ref[0])
     first = pltpu.make_async_copy(masses, mbuf, sems.at[2 * LIVE])
     first.start()
@@ -112,10 +114,9 @@
         kicks = planes(nbuf, k)
         near = (old[1], old[0] + old[2], old[1] + old[3], old[2])
         new = [update(old[z], near[z], mass[z], kicks[z], lane) for z in range(DEPTH)]
-        down[2 * k] = old[0]
-        down[2 * k + 1] = new[0]
-        up[2 * k] = old[3]
-        up[2 * k + 1] = new[3]
+        for i, value in ((0, old), (1, new)):
+            near_out[2 * k + i] = jnp.where(odd, value[0], value[3])
+            far_out[2 * k + i] = jnp.where(odd, value[3], value[0])
         mid[2 * k] = new[1]
         mid[2 * k + 1] = new[2]
 
@@ -167,8 +168,25 @@
 
 
 def sweep_kernel(
-    base_ref, counts_ref, noise, masses, lo, hi, up, down, mid, along_x, along_y, pieces, chunks, nbuf, mbuf, sems
+    base_ref,
+    odd_ref,
+    counts_ref,
+    noise,
+    masses,
+    near_in,
+    far_in,
+    near_own,
+    far_own,
+    mid,
+    along_x,
+    along_y,
+    pieces,
+    chunks,
+    nbuf,
+    mbuf,
+    sems,
 ):
+    odd = odd_ref[0] > 0
     live = live_of(counts_ref, base_ref[0])
     first = pltpu.make_async_copy(masses, mbuf, sems.at[LIVE])
     first.start()
@@ -181,13 +199,15 @@
     left = []
     for k in range(LIVE):
         copies[k].wait()
+        beyond = [t[2 * k + 1] + 0.1 * own[2 * k] for t, own in ((near_in, near_own), (far_in, far_own))]
+        within = [own[2 * k + 1] + 0.1 * t[2 * k] for t, own in ((near_in, near_own), (far_in, far_own))]
         now = [
-            lo[2 * k + 1] + 0.1 * down[2 * k],
-            down[2 * k + 1] + 0.1 * lo[2 * k],
+            jnp.where(odd, beyond[0], beyond[1]),
+            jnp.where(odd, within[0], within[1]),
             mid[2 * k],
             mid[2 * k + 1],
-            up[2 * k + 1] + 0.1 * hi[2 * k],
-            hi[2 * k + 1] + 0.1 * up[2 * k],
+            jnp.where(odd, within[1], within[0]),
+            jnp.where(odd, beyond[1], beyond[0]),
         ]
         kicks = planes(nbuf, k)
         new = [update(now[p + 1], now[p] + now[p + 2], mass[p], kicks[p], lane) for p in range(DEPTH)]
@@ -290,11 +310,11 @@
     return jnp.swapaxes(parts, -3, -2).reshape(*lead, DEPTH * ROWS, 128)
 
 
-def edges(base, counts, field, noise, masses):
+def edges(base, odd, counts, field, noise, masses):
     return pl.pallas_call(
         edges_kernel,
         out_shape=[shape(2 * LIVE, ROWS, 128)] * 3,
-        in_specs=[spec(SMEM)] * 2 + [spec(pl.ANY)] * 3,
+        in_specs=[spec(SMEM)] * 3 + [spec(pl.ANY)] * 3,
         out_specs=[spec(VMEM)] * 3,
         scratch_shapes=[
             VMEM((LIVE, 128, 128), jnp.float32),
@@ -303,7 +323,7 @@
             pltpu.SemaphoreType.DMA((2 * LIVE + 1,)),
         ],
         name="edges",
-    )(base, counts, field, noise, masses)
+    )(base, odd, counts, field, noise, masses)
 
 
 def plan(counts, dest_slots, mode_bins):
@@ -318,23 +338,25 @@
         ],
         in_specs=[spec(VMEM)] * 3,
         out_specs=[spec(VMEM)] * 3,
+        compiler_params=pltpu.CompilerParams(vmem_limit_bytes=GRANT),
         name="plan",
     )(counts.reshape(1, total), dest_slots.reshape(1, total), padded)
 
 
-def sweeps(base, counts, noise, masses, *blocks):
+def sweeps(base, odd, counts, noise, masses, *blocks):
     return pl.pallas_call(
         sweep_kernel,
         out_shape=[shape(ROWS * BLOCKS * DEPTH, 128), shape(16 * 8 * LIVE, 128)],
-        in_specs=[spec(SMEM)] * 2 + [spec(pl.ANY)] * 2 + [spec(VMEM)] * 7,
+        in_specs=[spec(SMEM)] * 3 + [spec(pl.ANY)] * 2 + [spec(VMEM)] * 7,
         out_specs=[spec(VMEM)] * 2,
         scratch_shapes=[
             VMEM((LIVE, 128, 128), jnp.float32),
             VMEM((128, 128), jnp.float32),
             pltpu.SemaphoreType.DMA((LIVE + 1,)),
         ],
+        compiler_params=pltpu.CompilerParams(vmem_limit_bytes=GRANT),
         name="sweeps",
-    )(base, counts, noise, masses, *blocks)
+    )(base, odd, counts, noise, masses, *blocks)
 
 
 def bins(me, chunks, place, wide, along_z, pieces):
@@ -350,6 +372,7 @@
             pltpu.SemaphoreType.DMA,
         ],
         input_output_aliases={5: 0},
+        compiler_params=pltpu.CompilerParams(vmem_limit_bytes=GRANT),
         name="bins",
     )(me, chunks, place, wide, along_z, pieces)
 
@@ -360,6 +383,7 @@
         out_shape=[shape(item.shape[0], DEPTH, 128), shape(1, 128)],
         in_specs=[spec(SMEM), spec(VMEM)],
         out_specs=[spec(VMEM)] * 2,
+        compiler_params=pltpu.CompilerParams(vmem_limit_bytes=GRANT),
         name="pick",
     )(item, pieces)
 
@@ -370,6 +394,7 @@
         out_shape=[shape(PER, DEPTH, L * L), shape(PER, NBINS)],
         in_specs=[spec(VMEM)] * 2,
         out_specs=[spec(VMEM)] * 2,
+        compiler_params=pltpu.CompilerParams(vmem_limit_bytes=GRANT),
         name="finish",
     )(got, sums)
 
@@ -379,13 +404,15 @@
     me = lax.axis_index("rep").astype(jnp.int32).reshape(1)
     base = me * PER
     field, noise, mass = rows_view(lattice_field), rows_view(langevin_noise), rows_view(masses)
-    up, down, mid = edges(base, counts, field, noise, mass)
+    odd = (lax.axis_index("gz").astype(jnp.int32) & 1).reshape(1)
+    near, far, mid = edges(base, odd, counts, field, noise, mass)
     ring = lax.axis_size("gz")
-    forward = [(i, (i + 1) % ring) for i in range(ring)]
-    lo = lax.ppermute(up, "gz", forward)
-    hi = lax.ppermute(down, "gz", [(b, a) for a, b in forward])
-    lo, hi, item, wide, place = lax.optimization_barrier((lo, hi, *plan(counts, dest_slots, mode_bins)))
-    pieces, chunks = sweeps(base, counts, noise, mass, lo, hi, up, down, mid, along_x, along_y)
+    near_in = lax.ppermute(near, "gz", [(i, i ^ 1) for i in range(ring)])
+    far_in = lax.ppermute(far, "gz", [(i, (i + 1) % ring if i % 2 else (i - 1) % ring) for i in range(ring)])
+    far_in, near_in, item, wide, place = lax.optimization_barrier(
+        (far_in, near_in, *plan(counts, dest_slots, mode_bins))
+    )
+    pieces, chunks = sweeps(base, odd, counts, noise, mass, near_in, far_in, near, far, mid, along_x, along_y)
     reps = lax.axis_size("rep")
     chunks = lax.all_to_all(chunks.reshape(ring, 8 * LIVE, 128), "gz", 0, 0, tiled=True)
     pieces = bins(me, chunks, place, wide, along_z, pieces.reshape(reps, BLOCKS, DEPTH, 128))

time: 112 us -> 103 us (0.920)
  Pallas kernels: 15.3 us -> 8.97 us
  blocking collectives: 53.7 us -> 52.1 us
  waiting for transfers between devices: 14.3 us -> 15.9 us
  starting transfers between devices: 23.7 us -> 22.5 us
    pallas_call x1, Pallas kernels: 3.85 us -> 2.06 us  [sweeps(): pl.pallas_call(sweep_kernel, out_shape=[shape(ROWS * BLOCKS * DEPTH, 128)...]
    pallas_call x1, Pallas kernels: 2.74 us -> 1.14 us  [bins(): pl.pallas_call(bins_kernel, out_shape=shape(devices, BLOCKS, DEPTH, 128),...]
    pallas_call x1, Pallas kernels: 1.91 us -> 0.33 us  [plan(): pl.pallas_call(plan_kernel, out_shape=[shape(1, total, dtype=jnp.int32),...]
    all_to_all x1, blocking collectives: 15.5 us -> 14.2 us  [local(): lax.all_to_all(chunks.reshape(ring, 8 * LIVE, 128), 'gz', 0, 0, tiled=True)]
    ppermute x2, starting transfers between devices: 9.18 us -> 7.97 us  [the longest x1 5.92 us: local(): lax.ppermute(far, 'gz', [(i, (i + 1) % ring if i % 2 else (i - 1) % ring)...]
    all_to_all x1, waiting for transfers between devices: 2.48 us -> 3.63 us  [local(): lax.all_to_all(out.reshape(reps, PER, DEPTH, 128), 'rep', 0, 0, tiled=True)]
  transfers between devices with their start and end apart: 7 -> 7, of which waited for: 5 -> 6; matrix products, arithmetic and copies ran while one was open for 1% -> 0% of each run, Pallas kernels for 2% -> 0%
where the time goes in v5:
time: 103 us; the launch traced here: 102 us
  blocking collectives  52.1 us (51%)
  starting transfers between devices  22.5 us (22%)
  waiting for transfers between devices  15.9 us (15%)
  Pallas kernels  8.97 us (9%)
  local copies, waits for them, and re-layouts  1.78 us (2%)
    all_to_all x1, blocking collectives, local(): pieces = lax.all_to_all(pieces, 'rep', 0, 0, tiled=True)  37.9 us
    all_to_all x1, blocking collectives, local(): lax.all_to_all(chunks.reshape(ring, 8 * LIVE, 128), 'gz', 0, 0, tiled=True)  14.2 us
    ppermute x4, waiting for transfers between devices, local(): sums = sums + lax.ppermute(sums, 'gz', [(i, i ^ step) for i in range(ring)])  11.8 us
    ppermute x4, starting transfers between devices, local(): sums = sums + lax.ppermute(sums, 'gz', [(i, i ^ step) for i in range(ring)])  10.5 us
    ppermute x1, starting transfers between devices, local(): lax.ppermute(far, 'gz', [(i, (i + 1) % ring if i % 2 else (i - 1) % ring)...  5.92 us
    all_to_all x1, starting transfers between devices, local(): lax.all_to_all(out.reshape(reps, PER, DEPTH, 128), 'rep', 0, 0, tiled=True)  4.1 us
    all_to_all x1, waiting for transfers between devices, local(): lax.all_to_all(out.reshape(reps, PER, DEPTH, 128), 'rep', 0, 0, tiled=True)  3.63 us
    pallas_call x1, Pallas kernels, edges(): pl.pallas_call(edges_kernel, out_shape=[shape(2 * LIVE, ROWS, 128)] * 3,...  3.02 us
  transfers between devices with their start and end apart: 7, of which 6 were waited for; matrix products, arithmetic and copies ran while one was open for 0% of the time, Pallas kernels for 0%

profile of v5, /device:TPU:2, one launch (start us, length us, event | category | flops | bytes accessed | tf_op | source)
XLA Modules:
  0.0 102.2 jit_solution(16065630205336963971)
XLA Ops:
  0.6 0.0 copy-start.10
  0.6 0.0 copy-start
  0.7 3.0 %edges.1 = (f32[6,32,128]{2,1,0:T(8,128)}, f32[6,32,128]{2,1,0:T(8,128)}, f32[6,32,128]{2,1,0:T(8,128)}) custom-call(s32[1]{0:T(128)S(6)} %mul.3.base_ref, s32[1]{0:T(128)} %bitcast.1.odd_ref, s32[192]{0:T(256)} %counts_ref.3, f32[6,128,128]{2,1,0:T(8,128)} %bitcast.36, f32[2,6,128,128]{3,2,1,0:T(8,128)} %bitcast.25, f32[128,128]{1,0:T(8,128)} %bitcast.30), custom_call_target="tpu_custom_call" | custom-call | tf_op jit(solution)/shard_map/edges/pallas_call | solution.py:314
  3.7 5.9 %collective-permute-start = (f32[6,32,128]{2,1,0:T(8,128)}, f32[6,32,128]{2,1,0:T(8,128)S(1)}, u32[]{:S(2)}, u32[]{:S(2)}) collective-permute-start(f32[6,32,128]{2,1,0:T(8,128)} %get-tuple-element.17.far_own), channel_id=1, source_target_pairs={{0,15},{1,2},{2,1},{3,4},{4,3},{5,6},{6,5},{7,8},{8,7},{9,10},{10,... | collective-permute-start | bytes 294920 | tf_op jit(solution)/shard_map/ppermute | solution.py:411
  9.6 0.0 copy-start.1
  9.6 2.1 %collective-permute-start.1 = (f32[6,32,128]{2,1,0:T(8,128)}, f32[6,32,128]{2,1,0:T(8,128)S(1)}, u32[]{:S(2)}, u32[]{:S(2)}) collective-permute-start(f32[6,32,128]{2,1,0:T(8,128)} %get-tuple-element.18.near_own), channel_id=1, source_target_pairs={{0,1},{1,0},{2,3},{3,2},{4,5},{5,4},{6,7},{7,6},{8,9},{9,8},{10,11... | collective-permute-start | bytes 294920 | tf_op jit(solution)/shard_map/ppermute | solution.py:410
  11.7 0.0 copy-done.10
  11.7 0.1 copy.15
  11.8 0.0 copy-start.9
  11.8 0.0 copy-start.3
  11.8 0.0 copy-start.4
  11.9 0.0 copy-start.8
  11.9 0.6 copy-done.9
  12.5 0.1 copy-done.8
  12.6 0.0 copy-start.2
  12.6 0.0 copy-start.7
  12.6 0.3 plan.1
  13.0 0.5 collective-permute-done.far_in
  13.4 0.0 collective-permute-done.1.near_in
  13.4 0.0 copy-done
  13.5 0.0 copy-done.1
  13.5 0.0 copy-done.3
  13.5 0.0 copy-done.4
  13.5 0.0 copy-done.2
  13.5 0.0 copy-done.7
  13.5 0.0 copy-start.5
  13.5 0.9 copy-done.5
  14.4 2.1 %sweeps.1 = (f32[512,128]{1,0:T(8,128)S(1)}, f32[384,128]{1,0:T(8,128)S(1)}) custom-call(s32[1]{0:T(128)S(6)} %mul.3.base_ref, s32[1]{0:T(128)} %bitcast.1.odd_ref, s32[192]{0:T(256)S(1)} %copy-done.8, f32[2,6,128,128]{3,2,1,0:T(8,128)S(1)} %bitcast.26, f32[128,128]{1,0:T(8,128)S(1)} %bitcast.31, f32[6,32,128]{2,1,0:T(8,128)S(1)} %collective-permute-done.1.near_in, ...), custom_call_target="tpu_custom_call" | custom-call | tf_op jit(solution)/shard_map/sweeps/pallas_call | solution.py:347
  16.5 0.0 copy-start.6
  16.5 14.2 %all_to_all.15.chunks = f32[16,24,128]{2,1,0:T(8,128)S(1)} all-to-all(f32[16,24,128]{2,1,0:T(8,128)S(1)} %bitcast.32), channel_id=1, replica_groups=mesh['rep'=32,'gz'=16] {'gz'}, dimensions={0} | all-to-all | bytes 393216 | tf_op jit(solution)/shard_map/all_to_all | solution.py:417
  30.7 0.0 copy-done.6
  30.7 1.1 %bins.1 = f32[32,4,4,128]{3,2,1,0:T(4,128)S(1)} custom-call(s32[1]{0:T(128)} %bitcast.me_ref, f32[16,24,128]{2,1,0:T(8,128)S(1)} %all_to_all.15.chunks, s32[128,128]{1,0:T(8,128)S(1)} %get-tuple-element.27.map_ref, s32[32,128]{1,0:T(8,128)S(1)} %get-tuple-element.28.wide, bf16[2,128,128]{2,1,0:T(8,128)(2,1)S(1)} %copy-done.6, ...), custom_call_target="tpu_custom_call", output_to_operand_aliasing={{}: (5, {})} | custom-call | tf_op jit(solution)/shard_map/bins/pallas_call | solution.py:364
  31.8 37.9 %all_to_all.16 = f32[32,4,4,128]{3,2,1,0:T(4,128)S(1)} all-to-all(f32[32,4,4,128]{3,2,1,0:T(4,128)S(1)} %bins.1), channel_id=1, replica_groups=mesh['rep'=32,'gz'=16] {'rep'}, dimensions={0} | all-to-all | bytes 524288 | tf_op jit(solution)/shard_map/all_to_all | solution.py:419
  69.8 1.4 %pick.1 = (f32[192,4,128]{2,1,0:T(4,128)}, f32[1,128]{1,0:T(1,128)S(1)}) custom-call(s32[192]{0:T(256)S(1)} %bitcast.35, f32[128,4,128]{2,1,0:T(4,128)S(1)} %bitcast.29), custom_call_target="tpu_custom_call" | custom-call | tf_op jit(solution)/shard_map/pick/pallas_call | solution.py:381
  71.2 4.1 %all-to-all-start.2 = ((f32[32,6,4,128]{3,2,1,0:T(4,128)}), f32[32,6,4,128]{3,2,1,0:T(4,128)S(1)}, u32[]{:S(2)}, u32[]{:S(2)}) async-start(f32[32,6,4,128]{3,2,1,0:T(4,128)} %bitcast.21), calls=%async_computation.2 | async-start | bytes 786432 | tf_op jit(solution)/shard_map/all_to_all | solution.py:421
  75.3 1.9 %collective-permute-start.2 = (f32[1,128]{1,0:T(1,128)S(1)}, f32[1,128]{1,0:T(1,128)S(1)}, u32[]{:S(2)}, u32[]{:S(2)}) collective-permute-start(f32[1,128]{1,0:T(1,128)S(1)} %get-tuple-element.31), channel_id=1, source_target_pairs={{0,1},{1,0},{2,3},{3,2},{4,5},{5,4},{6,7},{7,6},{8,9},{9,8},{10,11... | collective-permute-start | bytes 1544 | tf_op jit(solution)/shard_map/ppermute | solution.py:424
  77.2 1.1 %collective-permute-done.2 = f32[1,128]{1,0:T(1,128)S(1)} collective-permute-done((f32[1,128]{1,0:T(1,128)S(1)}, f32[1,128]{1,0:T(1,128)S(1)}, u32[]{:S(2)}, u32[]{:S(2)}) %collective-permute-start.2) | collective-permute-done | bytes 544 | tf_op jit(solution)/shard_map/ppermute | solution.py:424
  78.3 2.5 %collective-permute-start.3 = (f32[1,128]{1,0:T(1,128)S(1)}, f32[1,128]{1,0:T(1,128)S(1)}, u32[]{:S(2)}, u32[]{:S(2)}) collective-permute-start(f32[1,128]{1,0:T(1,128)S(1)} %add.14), channel_id=1, source_target_pairs={{0,2},{1,3},{2,0},{3,1},{4,6},{5,7},{6,4},{7,5},{8,10},{9,11},{10,... | collective-permute-start | bytes 1544 | tf_op jit(solution)/shard_map/ppermute | solution.py:424
  80.9 2.9 %collective-permute-done.3 = f32[1,128]{1,0:T(1,128)S(1)} collective-permute-done((f32[1,128]{1,0:T(1,128)S(1)}, f32[1,128]{1,0:T(1,128)S(1)}, u32[]{:S(2)}, u32[]{:S(2)}) %collective-permute-start.3) | collective-permute-done | bytes 544 | tf_op jit(solution)/shard_map/ppermute | solution.py:424
  83.8 3.2 %collective-permute-start.4 = (f32[1,128]{1,0:T(1,128)S(1)}, f32[1,128]{1,0:T(1,128)S(1)}, u32[]{:S(2)}, u32[]{:S(2)}) collective-permute-start(f32[1,128]{1,0:T(1,128)S(1)} %add.15), channel_id=1, source_target_pairs={{0,4},{1,5},{2,6},{3,7},{4,0},{5,1},{6,2},{7,3},{8,12},{9,13},{10,... | collective-permute-start | bytes 1544 | tf_op jit(solution)/shard_map/ppermute | solution.py:424
  86.9 3.7 %collective-permute-done.4 = f32[1,128]{1,0:T(1,128)S(1)} collective-permute-done((f32[1,128]{1,0:T(1,128)S(1)}, f32[1,128]{1,0:T(1,128)S(1)}, u32[]{:S(2)}, u32[]{:S(2)}) %collective-permute-start.4) | collective-permute-done | bytes 544 | tf_op jit(solution)/shard_map/ppermute | solution.py:424
  90.7 2.8 %collective-permute-start.5 = (f32[1,128]{1,0:T(1,128)S(1)}, f32[1,128]{1,0:T(1,128)S(1)}, u32[]{:S(2)}, u32[]{:S(2)}) collective-permute-start(f32[1,128]{1,0:T(1,128)S(1)} %add.16), channel_id=1, source_target_pairs={{0,8},{1,9},{2,10},{3,11},{4,12},{5,13},{6,14},{7,15},{8,0},{9,1},... | collective-permute-start | bytes 1544 | tf_op jit(solution)/shard_map/ppermute | solution.py:424
  93.5 4.1 %collective-permute-done.5 = f32[1,128]{1,0:T(1,128)S(1)} collective-permute-done((f32[1,128]{1,0:T(1,128)S(1)}, f32[1,128]{1,0:T(1,128)S(1)}, u32[]{:S(2)}, u32[]{:S(2)}) %collective-permute-start.5) | collective-permute-done | bytes 544 | tf_op jit(solution)/shard_map/ppermute | solution.py:424
  97.6 3.6 %all-to-all-done.2 = f32[32,6,4,128]{3,2,1,0:T(4,128)S(1)} async-done(((f32[32,6,4,128]{3,2,1,0:T(4,128)}), f32[32,6,4,128]{3,2,1,0:T(4,128)S(1)}, u32[]{:S(2)}, u32[]{:S(2)}) %all-to-all-start.2) | async-done | bytes 393248 | tf_op jit(solution)/shard_map/all_to_all | solution.py:421
  101.3 1.0 finish.1
  (5 shorter events, 0.0 us)
Async XLA Ops:
  0.6 11.1 %copy-start.10 = (s32[4,64,33]{1,0,2:T(4,128)S(1)}, s32[4,64,33]{1,0,2:T(4,128)}, u32[]{:S(2)}) copy-start(s32[4,64,33]{1,0,2:T(4,128)} %param.14) | copy-start | bytes 101380
  0.6 12.8 %copy-start = (f32[2,6,4,4096]{3,2,1,0:T(4,128)S(1)}, f32[2,6,4,4096]{3,2,1,0:T(4,128)}, u32[]{:S(2)}) copy-start(f32[2,6,4,4096]{3,2,1,0:T(4,128)} %param.10) | copy-start | bytes 2359300
  3.7 9.8 %collective-permute-start = (f32[6,32,128]{2,1,0:T(8,128)}, f32[6,32,128]{2,1,0:T(8,128)S(1)}, u32[]{:S(2)}, u32[]{:S(2)}) collective-permute-start(f32[6,32,128]{2,1,0:T(8,128)} %get-tuple-element.17.far_own), channel_id=1, source_target_pairs={{0,15},{1,2},{2,1},{3,4},{4,3},{5,6},{6,5},{7,8},{8,7},{9,10},{10,... | collective-permute-start | bytes 294920 | tf_op jit(solution)/shard_map/ppermute | solution.py:411
  9.6 3.8 %copy-start.1 = (bf16[2,256,256]{2,1,0:T(8,128)(2,1)S(1)}, bf16[2,256,256]{2,1,0:T(8,128)(2,1)}, u32[]{:S(2)}) copy-start(bf16[2,256,256]{2,1,0:T(8,128)(2,1)} %constant.21.clone.along_x) | copy-start | bytes 786436
  9.6 3.8 %collective-permute-start.1 = (f32[6,32,128]{2,1,0:T(8,128)}, f32[6,32,128]{2,1,0:T(8,128)S(1)}, u32[]{:S(2)}, u32[]{:S(2)}) collective-permute-start(f32[6,32,128]{2,1,0:T(8,128)} %get-tuple-element.18.near_own), channel_id=1, source_target_pairs={{0,1},{1,0},{2,3},{3,2},{4,5},{5,4},{6,7},{7,6},{8,9},{9,8},{10,11... | collective-permute-start | bytes 294920 | tf_op jit(solution)/shard_map/ppermute | solution.py:410
  11.8 0.7 copy-start.9
  11.8 1.6 %copy-start.3 = (f32[6,32,128]{2,1,0:T(8,128)S(1)}, f32[6,32,128]{2,1,0:T(8,128)}, u32[]{:S(2)}) copy-start(f32[6,32,128]{2,1,0:T(8,128)} %get-tuple-element.18.near_own) | copy-start | bytes 294916
  11.8 1.6 %copy-start.4 = (f32[6,32,128]{2,1,0:T(8,128)S(1)}, f32[6,32,128]{2,1,0:T(8,128)}, u32[]{:S(2)}) copy-start(f32[6,32,128]{2,1,0:T(8,128)} %get-tuple-element.17.far_own) | copy-start | bytes 294916
  11.9 0.7 copy-start.8
  12.6 0.9 copy-start.2
  12.6 0.9 copy-start.7
  13.5 0.9 copy-start.5
  16.5 14.2 %copy-start.6 = (bf16[2,128,128]{2,1,0:T(8,128)(2,1)S(1)}, bf16[2,128,128]{2,1,0:T(8,128)(2,1)}, u32[]{:S(2)}) copy-start(bf16[2,128,128]{2,1,0:T(8,128)(2,1)} %constant.23.clone.along_z) | copy-start | bytes 196612
  71.2 30.0 %all-to-all-start.2 = ((f32[32,6,4,128]{3,2,1,0:T(4,128)}), f32[32,6,4,128]{3,2,1,0:T(4,128)S(1)}, u32[]{:S(2)}, u32[]{:S(2)}) async-start(f32[32,6,4,128]{3,2,1,0:T(4,128)} %bitcast.21), calls=%async_computation.2 | async-start | bytes 786432 | tf_op jit(solution)/shard_map/all_to_all | solution.py:421
  75.3 3.0 %collective-permute-start.2 = (f32[1,128]{1,0:T(1,128)S(1)}, f32[1,128]{1,0:T(1,128)S(1)}, u32[]{:S(2)}, u32[]{:S(2)}) collective-permute-start(f32[1,128]{1,0:T(1,128)S(1)} %get-tuple-element.31), channel_id=1, source_target_pairs={{0,1},{1,0},{2,3},{3,2},{4,5},{5,4},{6,7},{7,6},{8,9},{9,8},{10,11... | collective-permute-start | bytes 1544 | tf_op jit(solution)/shard_map/ppermute | solution.py:424
  78.3 5.4 %collective-permute-start.3 = (f32[1,128]{1,0:T(1,128)S(1)}, f32[1,128]{1,0:T(1,128)S(1)}, u32[]{:S(2)}, u32[]{:S(2)}) collective-permute-start(f32[1,128]{1,0:T(1,128)S(1)} %add.14), channel_id=1, source_target_pairs={{0,2},{1,3},{2,0},{3,1},{4,6},{5,7},{6,4},{7,5},{8,10},{9,11},{10,... | collective-permute-start | bytes 1544 | tf_op jit(solution)/shard_map/ppermute | solution.py:424
  83.8 6.9 %collective-permute-start.4 = (f32[1,128]{1,0:T(1,128)S(1)}, f32[1,128]{1,0:T(1,128)S(1)}, u32[]{:S(2)}, u32[]{:S(2)}) collective-permute-start(f32[1,128]{1,0:T(1,128)S(1)} %add.15), channel_id=1, source_target_pairs={{0,4},{1,5},{2,6},{3,7},{4,0},{5,1},{6,2},{7,3},{8,12},{9,13},{10,... | collective-permute-start | bytes 1544 | tf_op jit(solution)/shard_map/ppermute | solution.py:424
  90.7 6.9 %collective-permute-start.5 = (f32[1,128]{1,0:T(1,128)S(1)}, f32[1,128]{1,0:T(1,128)S(1)}, u32[]{:S(2)}, u32[]{:S(2)}) collective-permute-start(f32[1,128]{1,0:T(1,128)S(1)} %add.16), channel_id=1, source_target_pairs={{0,8},{1,9},{2,10},{3,11},{4,12},{5,13},{6,14},{7,15},{8,0},{9,1},... | collective-permute-start | bytes 1544 | tf_op jit(solution)/shard_map/ppermute | solution.py:424

commit v6 on v5

--- a/solution.py
+++ b/solution.py
@@ -89,7 +89,7 @@
     return center * (0.4 - 0.1 * mass - 0.05 * (center * center)) + 0.1 * near + KICK * noise_now
 
 
-def edges_kernel(base_ref, odd_ref, counts_ref, field, noise, masses, near_out, far_out, mid, fbuf, nbuf, mbuf, sems):
+def edges_kernel(base_ref, odd_ref, counts_ref, field, noise, masses, near_out, far_out, mid, later, mbuf, fbuf, nbuf, sems):
     odd = odd_ref[0] > 0
     live = live_of(counts_ref, base_ref[0])
     first = pltpu.make_async_copy(masses, mbuf, sems.at[2 * LIVE])
@@ -104,6 +104,9 @@
         )
         for copy in copies[-1]:
             copy.start()
+    last = [pltpu.make_async_copy(noise.at[1, live[k]], later.at[k], sems.at[2 * LIVE + 1 + k]) for k in range(LIVE)]
+    for copy in last:
+        copy.start()
     first.wait()
     lane = lax.broadcasted_iota(jnp.int32, (ROWS, 128), 1)
     mass = planes(mbuf)
@@ -119,6 +122,8 @@
             far_out[2 * k + i] = jnp.where(odd, value[3], value[0])
         mid[2 * k] = new[1]
         mid[2 * k + 1] = new[2]
+    for copy in last:
+        copy.wait()
 
 
 def floor_div(value, by):
@@ -168,37 +173,13 @@
 
 
 def sweep_kernel(
-    base_ref,
-    odd_ref,
-    counts_ref,
-    noise,
-    masses,
-    near_in,
-    far_in,
-    near_own,
-    far_own,
-    mid,
-    along_x,
-    along_y,
-    pieces,
-    chunks,
-    nbuf,
-    mbuf,
-    sems,
+    odd_ref, near_in, far_in, near_own, far_own, mid, later, masses, along_x, along_y, pieces, chunks
 ):
     odd = odd_ref[0] > 0
-    live = live_of(counts_ref, base_ref[0])
-    first = pltpu.make_async_copy(masses, mbuf, sems.at[LIVE])
-    first.start()
-    copies = [pltpu.make_async_copy(noise.at[1, live[k]], nbuf.at[k], sems.at[k]) for k in range(LIVE)]
-    for copy in copies:
-        copy.start()
-    first.wait()
     lane = lax.broadcasted_iota(jnp.int32, (ROWS, 128), 1)
-    mass = planes(mbuf)
+    mass = planes(masses)
     left = []
     for k in range(LIVE):
-        copies[k].wait()
         beyond = [t[2 * k + 1] + 0.1 * own[2 * k] for t, own in ((near_in, near_own), (far_in, far_own))]
         within = [own[2 * k + 1] + 0.1 * t[2 * k] for t, own in ((near_in, near_own), (far_in, far_own))]
         now = [
@@ -209,7 +190,7 @@
             jnp.where(odd, within[1], within[0]),
             jnp.where(odd, beyond[1], beyond[0]),
         ]
-        kicks = planes(nbuf, k)
+        kicks = planes(later, k)
         new = [update(now[p + 1], now[p] + now[p + 2], mass[p], kicks[p], lane) for p in range(DEPTH)]
         for z in range(DEPTH):
             pieces[pl.ds(k * DEPTH + z, ROWS, stride=BLOCKS * DEPTH), :] = new[z]
@@ -313,15 +294,15 @@
 def edges(base, odd, counts, field, noise, masses):
     return pl.pallas_call(
         edges_kernel,
-        out_shape=[shape(2 * LIVE, ROWS, 128)] * 3,
+        out_shape=[shape(2 * LIVE, ROWS, 128)] * 3 + [shape(LIVE, 128, 128), shape(128, 128)],
         in_specs=[spec(SMEM)] * 3 + [spec(pl.ANY)] * 3,
-        out_specs=[spec(VMEM)] * 3,
+        out_specs=[spec(VMEM)] * 5,
         scratch_shapes=[
             VMEM((LIVE, 128, 128), jnp.float32),
             VMEM((LIVE, 128, 128), jnp.float32),
-            VMEM((128, 128), jnp.float32),
-            pltpu.SemaphoreType.DMA((2 * LIVE + 1,)),
+            pltpu.SemaphoreType.DMA((3 * LIVE + 1,)),
         ],
+        compiler_params=pltpu.CompilerParams(vmem_limit_bytes=GRANT),
         name="edges",
     )(base, odd, counts, field, noise, masses)
 
@@ -343,20 +324,15 @@
     )(counts.reshape(1, total), dest_slots.reshape(1, total), padded)
 
 
-def sweeps(base, odd, counts, noise, masses, *blocks):
+def sweeps(*blocks):
     return pl.pallas_call(
         sweep_kernel,
         out_shape=[shape(ROWS * BLOCKS * DEPTH, 128), shape(16 * 8 * LIVE, 128)],
-        in_specs=[spec(SMEM)] * 3 + [spec(pl.ANY)] * 2 + [spec(VMEM)] * 7,
+        in_specs=[spec(SMEM)] + [spec(VMEM)] * 9,
         out_specs=[spec(VMEM)] * 2,
-        scratch_shapes=[
-            VMEM((LIVE, 128, 128), jnp.float32),
-            VMEM((128, 128), jnp.float32),
-            pltpu.SemaphoreType.DMA((LIVE + 1,)),
-        ],
         compiler_params=pltpu.CompilerParams(vmem_limit_bytes=GRANT),
         name="sweeps",
-    )(base, odd, counts, noise, masses, *blocks)
+    )(*blocks)
 
 
 def bins(me, chunks, place, wide, along_z, pieces):
@@ -405,14 +381,15 @@
     base = me * PER
     field, noise, mass = rows_view(lattice_field), rows_view(langevin_noise), rows_view(masses)
     odd = (lax.axis_index("gz").astype(jnp.int32) & 1).reshape(1)
-    near, far, mid = edges(base, odd, counts, field, noise, mass)
+    held = (pltpu.with_memory_space_constraint(a, pltpu.HBM) for a in (counts, field, noise, mass))
+    near, far, mid, later, mass = edges(base, odd, *held)
     ring = lax.axis_size("gz")
     near_in = lax.ppermute(near, "gz", [(i, i ^ 1) for i in range(ring)])
     far_in = lax.ppermute(far, "gz", [(i, (i + 1) % ring if i % 2 else (i - 1) % ring) for i in range(ring)])
     far_in, near_in, item, wide, place = lax.optimization_barrier(
         (far_in, near_in, *plan(counts, dest_slots, mode_bins))
     )
-    pieces, chunks = sweeps(base, odd, counts, noise, mass, near_in, far_in, near, far, mid, along_x, along_y)
+    pieces, chunks = sweeps(odd, near_in, far_in, near, far, mid, later, mass, along_x, along_y)
     reps = lax.axis_size("rep")
     chunks = lax.all_to_all(chunks.reshape(ring, 8 * LIVE, 128), "gz", 0, 0, tiled=True)
     pieces = bins(me, chunks, place, wide, along_z, pieces.reshape(reps, BLOCKS, DEPTH, 128))

time: 103 us -> 99.8 us (0.969)
  Pallas kernels: 8.97 us -> 7.09 us
    pallas_call x1, Pallas kernels: 2.06 us -> 0.84 us  [sweeps(): pl.pallas_call(sweep_kernel, out_shape=[shape(ROWS * BLOCKS * DEPTH, 128)...]
where the time goes in v6:
time: 99.8 us; the launch traced here: 99.2 us
  blocking collectives  52.1 us (52%)
  starting transfers between devices  22.5 us (23%)
  waiting for transfers between devices  15.8 us (16%)
  Pallas kernels  7.09 us (7%)
    all_to_all x1, blocking collectives, local(): pieces = lax.all_to_all(pieces, 'rep', 0, 0, tiled=True)  37.9 us
    all_to_all x1, blocking collectives, local(): lax.all_to_all(chunks.reshape(ring, 8 * LIVE, 128), 'gz', 0, 0, tiled=True)  14.2 us
    ppermute x4, waiting for transfers between devices, local(): sums = sums + lax.ppermute(sums, 'gz', [(i, i ^ step) for i in range(ring)])  11.8 us
    ppermute x4, starting transfers between devices, local(): sums = sums + lax.ppermute(sums, 'gz', [(i, i ^ step) for i in range(ring)])  10.5 us
    ppermute x1, starting transfers between devices, local(): lax.ppermute(far, 'gz', [(i, (i + 1) % ring if i % 2 else (i - 1) % ring)...  5.92 us
    all_to_all x1, starting transfers between devices, local(): lax.all_to_all(out.reshape(reps, PER, DEPTH, 128), 'rep', 0, 0, tiled=True)  4.1 us
    all_to_all x1, waiting for transfers between devices, local(): lax.all_to_all(out.reshape(reps, PER, DEPTH, 128), 'rep', 0, 0, tiled=True)  3.63 us
    pallas_call x1, Pallas kernels, edges(): pl.pallas_call(edges_kernel, out_shape=[shape(2 * LIVE, ROWS, 128)] * 3 +...  2.36 us
  transfers between devices with their start and end apart: 7, of which 6 were waited for; matrix products, arithmetic and copies ran while one was open for 0% of the time, Pallas kernels for 0%

profile of v6, /device:TPU:2, one launch (start us, length us, event | category | flops | bytes accessed | tf_op | source)
XLA Modules:
  0.0 99.2 jit_solution(15567327608319753569)
XLA Ops:
  0.6 0.0 copy-start.5
  0.6 2.4 %edges.1 = (f32[6,32,128]{2,1,0:T(8,128)S(1)}, f32[6,32,128]{2,1,0:T(8,128)S(1)}, f32[6,32,128]{2,1,0:T(8,128)S(1)}, f32[3,128,128]{2,1,0:T(8,128)S(1)}, f32[128,128]{1,0:T(8,128)S(1)}) custom-call(s32[1]{0:T(128)S(6)} %mul.3.base_ref, s32[1]{0:T(128)} %bitcast.1.odd_ref, s32[192]{0:T(256)} %counts_ref.1, f32[6,128,128]{2,1,0:T(8,128)} %bitcast.33, ...), custom_call_target="tpu_custom_call" | custom-call | tf_op jit(solution)/shard_map/edges/pallas_call | solution.py:295
  3.0 5.9 %collective-permute-start = (f32[6,32,128]{2,1,0:T(8,128)S(1)}, f32[6,32,128]{2,1,0:T(8,128)S(1)}, u32[]{:S(2)}, u32[]{:S(2)}) collective-permute-start(f32[6,32,128]{2,1,0:T(8,128)S(1)} %get-tuple-element.19.far_own), channel_id=1, source_target_pairs={{0,15},{1,2},{2,1},{3,4},{4,3},{5,6},{6,5},{7,8},{8,7},{9,10},{10,... | collective-permute-start | bytes 294920 | tf_op jit(solution)/shard_map/ppermute | solution.py:388
  8.9 0.0 copy-start
  9.0 2.1 %collective-permute-start.1 = (f32[6,32,128]{2,1,0:T(8,128)S(1)}, f32[6,32,128]{2,1,0:T(8,128)S(1)}, u32[]{:S(2)}, u32[]{:S(2)}) collective-permute-start(f32[6,32,128]{2,1,0:T(8,128)S(1)} %get-tuple-element.20.near_own), channel_id=1, source_target_pairs={{0,1},{1,0},{2,3},{3,2},{4,5},{5,4},{6,7},{7,6},{8,9},{9,8},{10,11... | collective-permute-start | bytes 294920 | tf_op jit(solution)/shard_map/ppermute | solution.py:387
  11.0 0.0 copy-done.5
  11.0 0.1 copy.15
  11.1 0.0 copy-start.4
  11.2 0.0 copy-start.3
  11.2 0.6 copy-done.4
  11.8 0.0 copy-done.3
  11.9 0.0 copy-start.2
  11.9 0.3 plan.1
  12.2 0.4 collective-permute-done.far_in
  12.6 0.0 collective-permute-done.1.near_in
  12.6 0.0 copy-done
  12.6 0.0 copy-done.2
  12.6 0.8 sweeps.1
  13.5 0.0 copy-start.1
  13.5 14.2 %all_to_all.15.chunks = f32[16,24,128]{2,1,0:T(8,128)S(1)} all-to-all(f32[16,24,128]{2,1,0:T(8,128)S(1)} %bitcast.28), channel_id=1, replica_groups=mesh['rep'=32,'gz'=16] {'gz'}, dimensions={0} | all-to-all | bytes 393216 | tf_op jit(solution)/shard_map/all_to_all | solution.py:394
  27.7 0.0 copy-done.1
  27.7 1.1 %bins.1 = f32[32,4,4,128]{3,2,1,0:T(4,128)S(1)} custom-call(s32[1]{0:T(128)} %bitcast.me_ref, f32[16,24,128]{2,1,0:T(8,128)S(1)} %all_to_all.15.chunks, s32[128,128]{1,0:T(8,128)S(1)} %get-tuple-element.31.map_ref, s32[32,128]{1,0:T(8,128)S(1)} %get-tuple-element.32.wide, bf16[2,128,128]{2,1,0:T(8,128)(2,1)S(1)} %copy-done.1, ...), custom_call_target="tpu_custom_call", output_to_operand_aliasing={{}: (5, {})} | custom-call | tf_op jit(solution)/shard_map/bins/pallas_call | solution.py:340
  28.8 37.9 %all_to_all.16 = f32[32,4,4,128]{3,2,1,0:T(4,128)S(1)} all-to-all(f32[32,4,4,128]{3,2,1,0:T(4,128)S(1)} %bins.1), channel_id=1, replica_groups=mesh['rep'=32,'gz'=16] {'rep'}, dimensions={0} | all-to-all | bytes 524288 | tf_op jit(solution)/shard_map/all_to_all | solution.py:396
  66.7 1.4 %pick.1 = (f32[192,4,128]{2,1,0:T(4,128)}, f32[1,128]{1,0:T(1,128)S(1)}) custom-call(s32[192]{0:T(256)S(1)} %bitcast.31, f32[128,4,128]{2,1,0:T(4,128)S(1)} %bitcast.27), custom_call_target="tpu_custom_call" | custom-call | tf_op jit(solution)/shard_map/pick/pallas_call | solution.py:357
  68.2 4.1 %all-to-all-start.2 = ((f32[32,6,4,128]{3,2,1,0:T(4,128)}), f32[32,6,4,128]{3,2,1,0:T(4,128)S(1)}, u32[]{:S(2)}, u32[]{:S(2)}) async-start(f32[32,6,4,128]{3,2,1,0:T(4,128)} %bitcast.17), calls=%async_computation.2 | async-start | bytes 786432 | tf_op jit(solution)/shard_map/all_to_all | solution.py:398
  72.3 1.9 %collective-permute-start.2 = (f32[1,128]{1,0:T(1,128)S(1)}, f32[1,128]{1,0:T(1,128)S(1)}, u32[]{:S(2)}, u32[]{:S(2)}) collective-permute-start(f32[1,128]{1,0:T(1,128)S(1)} %get-tuple-element.35), channel_id=1, source_target_pairs={{0,1},{1,0},{2,3},{3,2},{4,5},{5,4},{6,7},{7,6},{8,9},{9,8},{10,11... | collective-permute-start | bytes 1544 | tf_op jit(solution)/shard_map/ppermute | solution.py:401
  74.2 1.1 %collective-permute-done.2 = f32[1,128]{1,0:T(1,128)S(1)} collective-permute-done((f32[1,128]{1,0:T(1,128)S(1)}, f32[1,128]{1,0:T(1,128)S(1)}, u32[]{:S(2)}, u32[]{:S(2)}) %collective-permute-start.2) | collective-permute-done | bytes 544 | tf_op jit(solution)/shard_map/ppermute | solution.py:401
  75.3 2.5 %collective-permute-start.3 = (f32[1,128]{1,0:T(1,128)S(1)}, f32[1,128]{1,0:T(1,128)S(1)}, u32[]{:S(2)}, u32[]{:S(2)}) collective-permute-start(f32[1,128]{1,0:T(1,128)S(1)} %add.14), channel_id=1, source_target_pairs={{0,2},{1,3},{2,0},{3,1},{4,6},{5,7},{6,4},{7,5},{8,10},{9,11},{10,... | collective-permute-start | bytes 1544 | tf_op jit(solution)/shard_map/ppermute | solution.py:401
  77.9 2.9 %collective-permute-done.3 = f32[1,128]{1,0:T(1,128)S(1)} collective-permute-done((f32[1,128]{1,0:T(1,128)S(1)}, f32[1,128]{1,0:T(1,128)S(1)}, u32[]{:S(2)}, u32[]{:S(2)}) %collective-permute-start.3) | collective-permute-done | bytes 544 | tf_op jit(solution)/shard_map/ppermute | solution.py:401
  80.7 3.2 %collective-permute-start.4 = (f32[1,128]{1,0:T(1,128)S(1)}, f32[1,128]{1,0:T(1,128)S(1)}, u32[]{:S(2)}, u32[]{:S(2)}) collective-permute-start(f32[1,128]{1,0:T(1,128)S(1)} %add.15), channel_id=1, source_target_pairs={{0,4},{1,5},{2,6},{3,7},{4,0},{5,1},{6,2},{7,3},{8,12},{9,13},{10,... | collective-permute-start | bytes 1544 | tf_op jit(solution)/shard_map/ppermute | solution.py:401
  83.9 3.7 %collective-permute-done.4 = f32[1,128]{1,0:T(1,128)S(1)} collective-permute-done((f32[1,128]{1,0:T(1,128)S(1)}, f32[1,128]{1,0:T(1,128)S(1)}, u32[]{:S(2)}, u32[]{:S(2)}) %collective-permute-start.4) | collective-permute-done | bytes 544 | tf_op jit(solution)/shard_map/ppermute | solution.py:401
  87.7 2.8 %collective-permute-start.5 = (f32[1,128]{1,0:T(1,128)S(1)}, f32[1,128]{1,0:T(1,128)S(1)}, u32[]{:S(2)}, u32[]{:S(2)}) collective-permute-start(f32[1,128]{1,0:T(1,128)S(1)} %add.16), channel_id=1, source_target_pairs={{0,8},{1,9},{2,10},{3,11},{4,12},{5,13},{6,14},{7,15},{8,0},{9,1},... | collective-permute-start | bytes 1544 | tf_op jit(solution)/shard_map/ppermute | solution.py:401
  90.5 4.1 %collective-permute-done.5 = f32[1,128]{1,0:T(1,128)S(1)} collective-permute-done((f32[1,128]{1,0:T(1,128)S(1)}, f32[1,128]{1,0:T(1,128)S(1)}, u32[]{:S(2)}, u32[]{:S(2)}) %collective-permute-start.5) | collective-permute-done | bytes 544 | tf_op jit(solution)/shard_map/ppermute | solution.py:401
  94.6 3.6 %all-to-all-done.2 = f32[32,6,4,128]{3,2,1,0:T(4,128)S(1)} async-done(((f32[32,6,4,128]{3,2,1,0:T(4,128)}), f32[32,6,4,128]{3,2,1,0:T(4,128)S(1)}, u32[]{:S(2)}, u32[]{:S(2)}) %all-to-all-start.2) | async-done | bytes 393248 | tf_op jit(solution)/shard_map/all_to_all | solution.py:398
  98.2 1.0 finish.1
  (5 shorter events, 0.0 us)
Async XLA Ops:
  0.6 10.4 %copy-start.5 = (s32[4,64,33]{1,0,2:T(4,128)S(1)}, s32[4,64,33]{1,0,2:T(4,128)}, u32[]{:S(2)}) copy-start(s32[4,64,33]{1,0,2:T(4,128)} %param.14) | copy-start | bytes 101380
  3.0 9.5 %collective-permute-start = (f32[6,32,128]{2,1,0:T(8,128)S(1)}, f32[6,32,128]{2,1,0:T(8,128)S(1)}, u32[]{:S(2)}, u32[]{:S(2)}) collective-permute-start(f32[6,32,128]{2,1,0:T(8,128)S(1)} %get-tuple-element.19.far_own), channel_id=1, source_target_pairs={{0,15},{1,2},{2,1},{3,4},{4,3},{5,6},{6,5},{7,8},{8,7},{9,10},{10,... | collective-permute-start | bytes 294920 | tf_op jit(solution)/shard_map/ppermute | solution.py:388
  8.9 3.6 %copy-start = (bf16[2,256,256]{2,1,0:T(8,128)(2,1)S(1)}, bf16[2,256,256]{2,1,0:T(8,128)(2,1)}, u32[]{:S(2)}) copy-start(bf16[2,256,256]{2,1,0:T(8,128)(2,1)} %constant.21.clone.along_x) | copy-start | bytes 786436
  9.0 3.6 %collective-permute-start.1 = (f32[6,32,128]{2,1,0:T(8,128)S(1)}, f32[6,32,128]{2,1,0:T(8,128)S(1)}, u32[]{:S(2)}, u32[]{:S(2)}) collective-permute-start(f32[6,32,128]{2,1,0:T(8,128)S(1)} %get-tuple-element.20.near_own), channel_id=1, source_target_pairs={{0,1},{1,0},{2,3},{3,2},{4,5},{5,4},{6,7},{7,6},{8,9},{9,8},{10,11... | collective-permute-start | bytes 294920 | tf_op jit(solution)/shard_map/ppermute | solution.py:387
  11.1 0.7 copy-start.4
  11.2 0.7 copy-start.3
  11.9 0.8 copy-start.2
  13.5 14.2 %copy-start.1 = (bf16[2,128,128]{2,1,0:T(8,128)(2,1)S(1)}, bf16[2,128,128]{2,1,0:T(8,128)(2,1)}, u32[]{:S(2)}) copy-start(bf16[2,128,128]{2,1,0:T(8,128)(2,1)} %constant.23.clone.along_z) | copy-start | bytes 196612
  68.2 30.0 %all-to-all-start.2 = ((f32[32,6,4,128]{3,2,1,0:T(4,128)}), f32[32,6,4,128]{3,2,1,0:T(4,128)S(1)}, u32[]{:S(2)}, u32[]{:S(2)}) async-start(f32[32,6,4,128]{3,2,1,0:T(4,128)} %bitcast.17), calls=%async_computation.2 | async-start | bytes 786432 | tf_op jit(solution)/shard_map/all_to_all | solution.py:398
  72.3 3.0 %collective-permute-start.2 = (f32[1,128]{1,0:T(1,128)S(1)}, f32[1,128]{1,0:T(1,128)S(1)}, u32[]{:S(2)}, u32[]{:S(2)}) collective-permute-start(f32[1,128]{1,0:T(1,128)S(1)} %get-tuple-element.35), channel_id=1, source_target_pairs={{0,1},{1,0},{2,3},{3,2},{4,5},{5,4},{6,7},{7,6},{8,9},{9,8},{10,11... | collective-permute-start | bytes 1544 | tf_op jit(solution)/shard_map/ppermute | solution.py:401
  75.3 5.4 %collective-permute-start.3 = (f32[1,128]{1,0:T(1,128)S(1)}, f32[1,128]{1,0:T(1,128)S(1)}, u32[]{:S(2)}, u32[]{:S(2)}) collective-permute-start(f32[1,128]{1,0:T(1,128)S(1)} %add.14), channel_id=1, source_target_pairs={{0,2},{1,3},{2,0},{3,1},{4,6},{5,7},{6,4},{7,5},{8,10},{9,11},{10,... | collective-permute-start | bytes 1544 | tf_op jit(solution)/shard_map/ppermute | solution.py:401
  80.7 6.9 %collective-permute-start.4 = (f32[1,128]{1,0:T(1,128)S(1)}, f32[1,128]{1,0:T(1,128)S(1)}, u32[]{:S(2)}, u32[]{:S(2)}) collective-permute-start(f32[1,128]{1,0:T(1,128)S(1)} %add.15), channel_id=1, source_target_pairs={{0,4},{1,5},{2,6},{3,7},{4,0},{5,1},{6,2},{7,3},{8,12},{9,13},{10,... | collective-permute-start | bytes 1544 | tf_op jit(solution)/shard_map/ppermute | solution.py:401
  87.7 6.9 %collective-permute-start.5 = (f32[1,128]{1,0:T(1,128)S(1)}, f32[1,128]{1,0:T(1,128)S(1)}, u32[]{:S(2)}, u32[]{:S(2)}) collective-permute-start(f32[1,128]{1,0:T(1,128)S(1)} %add.16), channel_id=1, source_target_pairs={{0,8},{1,9},{2,10},{3,11},{4,12},{5,13},{6,14},{7,15},{8,0},{9,1},... | collective-permute-start | bytes 1544 | tf_op jit(solution)/shard_map/ppermute | solution.py:401

commit v7 on v6

--- a/solution.py
+++ b/solution.py
@@ -14,6 +14,7 @@
 ROWS = 32
 PER = 6
 BLOCKS = LIVE + 1
+SPAN = LIVE * DEPTH + 1
 GRANT = 8 << 20
 
 VMEM = pltpu.VMEM
@@ -146,7 +147,7 @@
     block_row = floor_div(row, PER)
     block_col = floor_div(col, PER)
     rank = along((block_row == block_col) & (col < row) & (number > 0.0), jnp.ones_like(number))
-    name = rank + BLOCKS * block_row[:, :1].astype(jnp.float32)
+    name = DEPTH * rank + SPAN * block_row[:, :1].astype(jnp.float32)
     position = jnp.sum(
         jnp.where(slot_column == col.astype(jnp.float32), row.astype(jnp.float32), 0.0), axis=0, keepdims=True
     )
@@ -193,7 +194,7 @@
         kicks = planes(later, k)
         new = [update(now[p + 1], now[p] + now[p + 2], mass[p], kicks[p], lane) for p in range(DEPTH)]
         for z in range(DEPTH):
-            pieces[pl.ds(k * DEPTH + z, ROWS, stride=BLOCKS * DEPTH), :] = new[z]
+            pieces[pl.ds(k * DEPTH + z, ROWS, stride=SPAN), :] = new[z]
         left += [jnp.concatenate(new[0:2], axis=1), jnp.concatenate(new[2:4], axis=1)]
     high, low = split(jnp.concatenate(left, axis=0))
     across = dot(high, along_x[0]) + (dot(low, along_x[0]) + dot(high, along_x[1]))
@@ -240,10 +241,10 @@
     mine = jnp.where(lane >= NBINS * PER, spread(sums, LIVE, lane) * (1.0 / devices), 0.0)
     mine = jnp.broadcast_to(mine, (devices, 128))
     for k in range(LIVE):
-        mine = jnp.where(wide[...] == me_ref[0] * BLOCKS + k, spread(sums, k, lane), mine)
+        mine = jnp.where(wide[...] == me_ref[0] * SPAN + DEPTH * k, spread(sums, k, lane), mine)
     for d in range(devices):
-        block[d] = jnp.broadcast_to(mine[d : d + 1], (DEPTH, 128))
-    copy = pltpu.make_async_copy(block, pieces.at[:, LIVE], sem)
+        block[d] = mine[d : d + 1]
+    copy = pltpu.make_async_copy(block, pieces.at[:, SPAN - 1], sem)
     copy.start()
     copy.wait()
 
@@ -256,13 +257,10 @@
 
 
 def pick_kernel(item_ref, pieces, out, part):
-    devices = pieces.shape[0] // BLOCKS
+    devices = pieces.shape[0] // SPAN
     for s in range(devices * PER):
-        out[s] = pieces[item_ref[s]]
-    sums = pieces[LIVE]
-    for d in range(1, devices):
-        sums = sums + pieces[d * BLOCKS + LIVE]
-    part[...] = sums[0:1]
+        out[s] = pieces[pl.ds(item_ref[s], DEPTH), :]
+    part[...] = jnp.sum(pieces[pl.ds(SPAN - 1, devices, stride=SPAN), :], axis=0, keepdims=True)
 
 
 def finish_kernel(got, sums_ref, resampled, propagator):
@@ -327,7 +325,7 @@
 def sweeps(*blocks):
     return pl.pallas_call(
         sweep_kernel,
-        out_shape=[shape(ROWS * BLOCKS * DEPTH, 128), shape(16 * 8 * LIVE, 128)],
+        out_shape=[shape(ROWS * SPAN, 128), shape(16 * 8 * LIVE, 128)],
         in_specs=[spec(SMEM)] + [spec(VMEM)] * 9,
         out_specs=[spec(VMEM)] * 2,
         compiler_params=pltpu.CompilerParams(vmem_limit_bytes=GRANT),
@@ -339,12 +337,12 @@
     devices = wide.shape[0]
     return pl.pallas_call(
         bins_kernel,
-        out_shape=shape(devices, BLOCKS, DEPTH, 128),
+        out_shape=shape(devices, SPAN, 1, 128),
         in_specs=[spec(SMEM)] + [spec(VMEM)] * 4 + [spec(pl.ANY)],
         out_specs=spec(pl.ANY),
         scratch_shapes=[
             VMEM((128, 128), jnp.float32),
-            VMEM((devices, DEPTH, 128), jnp.float32),
+            VMEM((devices, 1, 128), jnp.float32),
             pltpu.SemaphoreType.DMA,
         ],
         input_output_aliases={5: 0},
@@ -392,9 +390,9 @@
     pieces, chunks = sweeps(odd, near_in, far_in, near, far, mid, later, mass, along_x, along_y)
     reps = lax.axis_size("rep")
     chunks = lax.all_to_all(chunks.reshape(ring, 8 * LIVE, 128), "gz", 0, 0, tiled=True)
-    pieces = bins(me, chunks, place, wide, along_z, pieces.reshape(reps, BLOCKS, DEPTH, 128))
+    pieces = bins(me, chunks, place, wide, along_z, pieces.reshape(reps, SPAN, 1, 128))
     pieces = lax.all_to_all(pieces, "rep", 0, 0, tiled=True)
-    out, sums = pick(item.reshape(-1), pieces.reshape(reps * BLOCKS, DEPTH, 128))
+    out, sums = pick(item.reshape(-1), pieces.reshape(reps * SPAN, 128))
     got = lax.all_to_all(out.reshape(reps, PER, DEPTH, 128), "rep", 0, 0, tiled=True)
     step = 1
     while step < ring:

time: 99.8 us -> 97.9 us (0.981)
  blocking collectives: 52.1 us -> 50 us
    all_to_all x1, blocking collectives: 37.9 us -> 35.8 us  [local(): pieces = lax.all_to_all(pieces, 'rep', 0, 0, tiled=True)]
where the time goes in v7:
time: 97.9 us; the launch traced here: 97.2 us
  blocking collectives  50 us (51%)
  starting transfers between devices  22.5 us (23%)
  waiting for transfers between devices  16 us (16%)
  Pallas kernels  7 us (7%)
    all_to_all x1, blocking collectives, local(): pieces = lax.all_to_all(pieces, 'rep', 0, 0, tiled=True)  35.8 us
    all_to_all x1, blocking collectives, local(): lax.all_to_all(chunks.reshape(ring, 8 * LIVE, 128), 'gz', 0, 0, tiled=True)  14.2 us
    ppermute x4, waiting for transfers between devices, local(): sums = sums + lax.ppermute(sums, 'gz', [(i, i ^ step) for i in range(ring)])  11.9 us
    ppermute x4, starting transfers between devices, local(): sums = sums + lax.ppermute(sums, 'gz', [(i, i ^ step) for i in range(ring)])  10.4 us
    ppermute x1, starting transfers between devices, local(): lax.ppermute(far, 'gz', [(i, (i + 1) % ring if i % 2 else (i - 1) % ring)...  5.92 us
    all_to_all x1, starting transfers between devices, local(): lax.all_to_all(out.reshape(reps, PER, DEPTH, 128), 'rep', 0, 0, tiled=True)  4.17 us
    all_to_all x1, waiting for transfers between devices, local(): lax.all_to_all(out.reshape(reps, PER, DEPTH, 128), 'rep', 0, 0, tiled=True)  3.79 us
    pallas_call x1, Pallas kernels, edges(): pl.pallas_call(edges_kernel, out_shape=[shape(2 * LIVE, ROWS, 128)] * 3 +...  2.36 us
  transfers between devices with their start and end apart: 7, of which 6 were waited for; matrix products, arithmetic and copies ran while one was open for 0% of the time, Pallas kernels for 0%

profile of v7, /device:TPU:2, one launch (start us, length us, event | category | flops | bytes accessed | tf_op | source)
XLA Modules:
  0.0 97.2 jit_solution(10136353336979898198)
XLA Ops:
  0.6 0.0 copy-start.5
  0.6 2.4 %edges.1 = (f32[6,32,128]{2,1,0:T(8,128)S(1)}, f32[6,32,128]{2,1,0:T(8,128)S(1)}, f32[6,32,128]{2,1,0:T(8,128)S(1)}, f32[3,128,128]{2,1,0:T(8,128)S(1)}, f32[128,128]{1,0:T(8,128)S(1)}) custom-call(s32[1]{0:T(128)S(6)} %mul.3.base_ref, s32[1]{0:T(128)} %bitcast.1.odd_ref, s32[192]{0:T(256)} %counts_ref.1, f32[6,128,128]{2,1,0:T(8,128)} %bitcast.33, ...), custom_call_target="tpu_custom_call" | custom-call | tf_op jit(solution)/shard_map/edges/pallas_call | solution.py:293
  3.0 5.9 %collective-permute-start = (f32[6,32,128]{2,1,0:T(8,128)S(1)}, f32[6,32,128]{2,1,0:T(8,128)S(1)}, u32[]{:S(2)}, u32[]{:S(2)}) collective-permute-start(f32[6,32,128]{2,1,0:T(8,128)S(1)} %get-tuple-element.19.far_own), channel_id=1, source_target_pairs={{0,15},{1,2},{2,1},{3,4},{4,3},{5,6},{6,5},{7,8},{8,7},{9,10},{10,... | collective-permute-start | bytes 294920 | tf_op jit(solution)/shard_map/ppermute | solution.py:386
  8.9 0.0 copy-start
  9.0 2.1 %collective-permute-start.1 = (f32[6,32,128]{2,1,0:T(8,128)S(1)}, f32[6,32,128]{2,1,0:T(8,128)S(1)}, u32[]{:S(2)}, u32[]{:S(2)}) collective-permute-start(f32[6,32,128]{2,1,0:T(8,128)S(1)} %get-tuple-element.20.near_own), channel_id=1, source_target_pairs={{0,1},{1,0},{2,3},{3,2},{4,5},{5,4},{6,7},{7,6},{8,9},{9,8},{10,11... | collective-permute-start | bytes 294920 | tf_op jit(solution)/shard_map/ppermute | solution.py:385
  11.0 0.0 copy-done.5
  11.0 0.1 copy.15
  11.1 0.0 copy-start.4
  11.2 0.0 copy-start.3
  11.2 0.6 copy-done.4
  11.8 0.0 copy-done.3
  11.9 0.0 copy-start.2
  11.9 0.3 plan.1
  12.2 0.4 collective-permute-done.far_in
  12.6 0.0 collective-permute-done.1.near_in
  12.6 0.0 copy-done
  12.6 0.0 copy-done.2
  12.6 0.8 sweeps.1
  13.4 0.0 copy-start.1
  13.4 14.2 %all_to_all.15.chunks = f32[16,24,128]{2,1,0:T(8,128)S(1)} all-to-all(f32[16,24,128]{2,1,0:T(8,128)S(1)} %bitcast.28), channel_id=1, replica_groups=mesh['rep'=32,'gz'=16] {'gz'}, dimensions={0} | all-to-all | bytes 393216 | tf_op jit(solution)/shard_map/all_to_all | solution.py:392
  27.6 0.0 copy-done.1
  27.6 1.1 %bins.1 = f32[32,13,1,128]{3,2,1,0:T(1,128)S(1)} custom-call(s32[1]{0:T(128)} %bitcast.me_ref, f32[16,24,128]{2,1,0:T(8,128)S(1)} %all_to_all.15.chunks, s32[128,128]{1,0:T(8,128)S(1)} %get-tuple-element.31.map_ref, s32[32,128]{1,0:T(8,128)S(1)} %get-tuple-element.32.wide, bf16[2,128,128]{2,1,0:T(8,128)(2,1)S(1)} %copy-done.1, ...), custom_call_target="tpu_custom_call", output_to_operand_aliasing={{}: (5, {})} | custom-call | tf_op jit(solution)/shard_map/bins/pallas_call | solution.py:338
  28.8 35.8 %all_to_all.16 = f32[32,13,1,128]{3,2,1,0:T(1,128)S(1)} all-to-all(f32[32,13,1,128]{3,2,1,0:T(1,128)S(1)} %bins.1), channel_id=1, replica_groups=mesh['rep'=32,'gz'=16] {'rep'}, dimensions={0} | all-to-all | bytes 425984 | tf_op jit(solution)/shard_map/all_to_all | solution.py:394
  64.6 1.4 %pick.1 = (f32[192,4,128]{2,1,0:T(4,128)}, f32[1,128]{1,0:T(1,128)S(1)}) custom-call(s32[192]{0:T(256)S(1)} %bitcast.31, f32[416,128]{1,0:T(8,128)S(1)} %bitcast.26), custom_call_target="tpu_custom_call" | custom-call | tf_op jit(solution)/shard_map/pick/pallas_call | solution.py:355
  66.0 4.2 %all-to-all-start.2 = ((f32[32,6,4,128]{3,2,1,0:T(4,128)}), f32[32,6,4,128]{3,2,1,0:T(4,128)S(1)}, u32[]{:S(2)}, u32[]{:S(2)}) async-start(f32[32,6,4,128]{3,2,1,0:T(4,128)} %bitcast.17), calls=%async_computation.2 | async-start | bytes 786432 | tf_op jit(solution)/shard_map/all_to_all | solution.py:396
  70.2 1.9 %collective-permute-start.2 = (f32[1,128]{1,0:T(1,128)S(1)}, f32[1,128]{1,0:T(1,128)S(1)}, u32[]{:S(2)}, u32[]{:S(2)}) collective-permute-start(f32[1,128]{1,0:T(1,128)S(1)} %get-tuple-element.35), channel_id=1, source_target_pairs={{0,1},{1,0},{2,3},{3,2},{4,5},{5,4},{6,7},{7,6},{8,9},{9,8},{10,11... | collective-permute-start | bytes 1544 | tf_op jit(solution)/shard_map/ppermute | solution.py:399
  72.1 1.1 %collective-permute-done.2 = f32[1,128]{1,0:T(1,128)S(1)} collective-permute-done((f32[1,128]{1,0:T(1,128)S(1)}, f32[1,128]{1,0:T(1,128)S(1)}, u32[]{:S(2)}, u32[]{:S(2)}) %collective-permute-start.2) | collective-permute-done | bytes 544 | tf_op jit(solution)/shard_map/ppermute | solution.py:399
  73.2 2.4 %collective-permute-start.3 = (f32[1,128]{1,0:T(1,128)S(1)}, f32[1,128]{1,0:T(1,128)S(1)}, u32[]{:S(2)}, u32[]{:S(2)}) collective-permute-start(f32[1,128]{1,0:T(1,128)S(1)} %add.14), channel_id=1, source_target_pairs={{0,2},{1,3},{2,0},{3,1},{4,6},{5,7},{6,4},{7,5},{8,10},{9,11},{10,... | collective-permute-start | bytes 1544 | tf_op jit(solution)/shard_map/ppermute | solution.py:399
  75.7 3.0 %collective-permute-done.3 = f32[1,128]{1,0:T(1,128)S(1)} collective-permute-done((f32[1,128]{1,0:T(1,128)S(1)}, f32[1,128]{1,0:T(1,128)S(1)}, u32[]{:S(2)}, u32[]{:S(2)}) %collective-permute-start.3) | collective-permute-done | bytes 544 | tf_op jit(solution)/shard_map/ppermute | solution.py:399
  78.6 3.2 %collective-permute-start.4 = (f32[1,128]{1,0:T(1,128)S(1)}, f32[1,128]{1,0:T(1,128)S(1)}, u32[]{:S(2)}, u32[]{:S(2)}) collective-permute-start(f32[1,128]{1,0:T(1,128)S(1)} %add.15), channel_id=1, source_target_pairs={{0,4},{1,5},{2,6},{3,7},{4,0},{5,1},{6,2},{7,3},{8,12},{9,13},{10,... | collective-permute-start | bytes 1544 | tf_op jit(solution)/shard_map/ppermute | solution.py:399
  81.8 3.8 %collective-permute-done.4 = f32[1,128]{1,0:T(1,128)S(1)} collective-permute-done((f32[1,128]{1,0:T(1,128)S(1)}, f32[1,128]{1,0:T(1,128)S(1)}, u32[]{:S(2)}, u32[]{:S(2)}) %collective-permute-start.4) | collective-permute-done | bytes 544 | tf_op jit(solution)/shard_map/ppermute | solution.py:399
  85.6 2.8 %collective-permute-start.5 = (f32[1,128]{1,0:T(1,128)S(1)}, f32[1,128]{1,0:T(1,128)S(1)}, u32[]{:S(2)}, u32[]{:S(2)}) collective-permute-start(f32[1,128]{1,0:T(1,128)S(1)} %add.16), channel_id=1, source_target_pairs={{0,8},{1,9},{2,10},{3,11},{4,12},{5,13},{6,14},{7,15},{8,0},{9,1},... | collective-permute-start | bytes 1544 | tf_op jit(solution)/shard_map/ppermute | solution.py:399
  88.4 4.1 %collective-permute-done.5 = f32[1,128]{1,0:T(1,128)S(1)} collective-permute-done((f32[1,128]{1,0:T(1,128)S(1)}, f32[1,128]{1,0:T(1,128)S(1)}, u32[]{:S(2)}, u32[]{:S(2)}) %collective-permute-start.5) | collective-permute-done | bytes 544 | tf_op jit(solution)/shard_map/ppermute | solution.py:399
  92.5 3.8 %all-to-all-done.2 = f32[32,6,4,128]{3,2,1,0:T(4,128)S(1)} async-done(((f32[32,6,4,128]{3,2,1,0:T(4,128)}), f32[32,6,4,128]{3,2,1,0:T(4,128)S(1)}, u32[]{:S(2)}, u32[]{:S(2)}) %all-to-all-start.2) | async-done | bytes 393248 | tf_op jit(solution)/shard_map/all_to_all | solution.py:396
  96.3 1.0 finish.1
  (5 shorter events, 0.0 us)
Async XLA Ops:
  0.6 10.4 %copy-start.5 = (s32[4,64,33]{1,0,2:T(4,128)S(1)}, s32[4,64,33]{1,0,2:T(4,128)}, u32[]{:S(2)}) copy-start(s32[4,64,33]{1,0,2:T(4,128)} %param.14) | copy-start | bytes 101380
  3.0 9.5 %collective-permute-start = (f32[6,32,128]{2,1,0:T(8,128)S(1)}, f32[6,32,128]{2,1,0:T(8,128)S(1)}, u32[]{:S(2)}, u32[]{:S(2)}) collective-permute-start(f32[6,32,128]{2,1,0:T(8,128)S(1)} %get-tuple-element.19.far_own), channel_id=1, source_target_pairs={{0,15},{1,2},{2,1},{3,4},{4,3},{5,6},{6,5},{7,8},{8,7},{9,10},{10,... | collective-permute-start | bytes 294920 | tf_op jit(solution)/shard_map/ppermute | solution.py:386
  8.9 3.6 %copy-start = (bf16[2,256,256]{2,1,0:T(8,128)(2,1)S(1)}, bf16[2,256,256]{2,1,0:T(8,128)(2,1)}, u32[]{:S(2)}) copy-start(bf16[2,256,256]{2,1,0:T(8,128)(2,1)} %constant.21.clone.along_x) | copy-start | bytes 786436
  9.0 3.6 %collective-permute-start.1 = (f32[6,32,128]{2,1,0:T(8,128)S(1)}, f32[6,32,128]{2,1,0:T(8,128)S(1)}, u32[]{:S(2)}, u32[]{:S(2)}) collective-permute-start(f32[6,32,128]{2,1,0:T(8,128)S(1)} %get-tuple-element.20.near_own), channel_id=1, source_target_pairs={{0,1},{1,0},{2,3},{3,2},{4,5},{5,4},{6,7},{7,6},{8,9},{9,8},{10,11... | collective-permute-start | bytes 294920 | tf_op jit(solution)/shard_map/ppermute | solution.py:385
  11.1 0.7 copy-start.4
  11.2 0.7 copy-start.3
  11.9 0.8 copy-start.2
  13.4 14.2 %copy-start.1 = (bf16[2,128,128]{2,1,0:T(8,128)(2,1)S(1)}, bf16[2,128,128]{2,1,0:T(8,128)(2,1)}, u32[]{:S(2)}) copy-start(bf16[2,128,128]{2,1,0:T(8,128)(2,1)} %constant.23.clone.along_z) | copy-start | bytes 196612
  66.0 30.3 %all-to-all-start.2 = ((f32[32,6,4,128]{3,2,1,0:T(4,128)}), f32[32,6,4,128]{3,2,1,0:T(4,128)S(1)}, u32[]{:S(2)}, u32[]{:S(2)}) async-start(f32[32,6,4,128]{3,2,1,0:T(4,128)} %bitcast.17), calls=%async_computation.2 | async-start | bytes 786432 | tf_op jit(solution)/shard_map/all_to_all | solution.py:396
  70.2 3.0 %collective-permute-start.2 = (f32[1,128]{1,0:T(1,128)S(1)}, f32[1,128]{1,0:T(1,128)S(1)}, u32[]{:S(2)}, u32[]{:S(2)}) collective-permute-start(f32[1,128]{1,0:T(1,128)S(1)} %get-tuple-element.35), channel_id=1, source_target_pairs={{0,1},{1,0},{2,3},{3,2},{4,5},{5,4},{6,7},{7,6},{8,9},{9,8},{10,11... | collective-permute-start | bytes 1544 | tf_op jit(solution)/shard_map/ppermute | solution.py:399
  73.2 5.4 %collective-permute-start.3 = (f32[1,128]{1,0:T(1,128)S(1)}, f32[1,128]{1,0:T(1,128)S(1)}, u32[]{:S(2)}, u32[]{:S(2)}) collective-permute-start(f32[1,128]{1,0:T(1,128)S(1)} %add.14), channel_id=1, source_target_pairs={{0,2},{1,3},{2,0},{3,1},{4,6},{5,7},{6,4},{7,5},{8,10},{9,11},{10,... | collective-permute-start | bytes 1544 | tf_op jit(solution)/shard_map/ppermute | solution.py:399
  78.6 6.9 %collective-permute-start.4 = (f32[1,128]{1,0:T(1,128)S(1)}, f32[1,128]{1,0:T(1,128)S(1)}, u32[]{:S(2)}, u32[]{:S(2)}) collective-permute-start(f32[1,128]{1,0:T(1,128)S(1)} %add.15), channel_id=1, source_target_pairs={{0,4},{1,5},{2,6},{3,7},{4,0},{5,1},{6,2},{7,3},{8,12},{9,13},{10,... | collective-permute-start | bytes 1544 | tf_op jit(solution)/shard_map/ppermute | solution.py:399
  85.6 6.9 %collective-permute-start.5 = (f32[1,128]{1,0:T(1,128)S(1)}, f32[1,128]{1,0:T(1,128)S(1)}, u32[]{:S(2)}, u32[]{:S(2)}) collective-permute-start(f32[1,128]{1,0:T(1,128)S(1)} %add.16), channel_id=1, source_target_pairs={{0,8},{1,9},{2,10},{3,11},{4,12},{5,13},{6,14},{7,15},{8,0},{9,1},... | collective-permute-start | bytes 1544 | tf_op jit(solution)/shard_map/ppermute | solution.py:399

commit v8 on v7

--- a/solution.py
+++ b/solution.py
@@ -214,7 +214,7 @@
                 chunks[pl.ds(i * 4 + side * 2 + pair, 16, stride=8 * LIVE), :] = ready[side][16 * pair : 16 * pair + 16]
 
 
-def bins_kernel(me_ref, chunks, map_ref, wide, along_z, _, pieces, rows, block, sem):
+def bins_kernel(me_ref, chunks, map_ref, wide, along_z, old, pieces, rows):
     devices = wide.shape[0]
     place = map_ref[...]
     power = []
@@ -242,11 +242,8 @@
     mine = jnp.broadcast_to(mine, (devices, 128))
     for k in range(LIVE):
         mine = jnp.where(wide[...] == me_ref[0] * SPAN + DEPTH * k, spread(sums, k, lane), mine)
-    for d in range(devices):
-        block[d] = mine[d : d + 1]
-    copy = pltpu.make_async_copy(block, pieces.at[:, SPAN - 1], sem)
-    copy.start()
-    copy.wait()
+    pieces[...] = old[...]
+    pieces[pl.ds(SPAN - 1, devices, stride=SPAN), :] = mine
 
 
 def spread(row, k, lane):
@@ -337,15 +334,10 @@
     devices = wide.shape[0]
     return pl.pallas_call(
         bins_kernel,
-        out_shape=shape(devices, SPAN, 1, 128),
-        in_specs=[spec(SMEM)] + [spec(VMEM)] * 4 + [spec(pl.ANY)],
-        out_specs=spec(pl.ANY),
-        scratch_shapes=[
-            VMEM((128, 128), jnp.float32),
-            VMEM((devices, 1, 128), jnp.float32),
-            pltpu.SemaphoreType.DMA,
-        ],
-        input_output_aliases={5: 0},
+        out_shape=shape(devices * SPAN, 128),
+        in_specs=[spec(SMEM)] + [spec(VMEM)] * 5,
+        out_specs=spec(VMEM),
+        scratch_shapes=[VMEM((128, 128), jnp.float32)],
         compiler_params=pltpu.CompilerParams(vmem_limit_bytes=GRANT),
         name="bins",
     )(me, chunks, place, wide, along_z, pieces)
@@ -390,8 +382,8 @@
     pieces, chunks = sweeps(odd, near_in, far_in, near, far, mid, later, mass, along_x, along_y)
     reps = lax.axis_size("rep")
     chunks = lax.all_to_all(chunks.reshape(ring, 8 * LIVE, 128), "gz", 0, 0, tiled=True)
-    pieces = bins(me, chunks, place, wide, along_z, pieces.reshape(reps, SPAN, 1, 128))
-    pieces = lax.all_to_all(pieces, "rep", 0, 0, tiled=True)
+    pieces = bins(me, chunks, place, wide, along_z, pieces)
+    pieces = lax.all_to_all(pieces.reshape(reps, SPAN, 1, 128), "rep", 0, 0, tiled=True)
     out, sums = pick(item.reshape(-1), pieces.reshape(reps * SPAN, 128))
     got = lax.all_to_all(out.reshape(reps, PER, DEPTH, 128), "rep", 0, 0, tiled=True)
     step = 1

time: 97.9 us -> 97.8 us (level)
  no operation moved by 1% of the time
where the time goes in v8:
time: 97.8 us; the launch traced here: 97.2 us
  blocking collectives  50.1 us (51%)
  starting transfers between devices  22.5 us (23%)
  waiting for transfers between devices  16 us (16%)
  Pallas kernels  6.91 us (7%)
    all_to_all x1, blocking collectives, local(): lax.all_to_all(pieces.reshape(reps, SPAN, 1, 128), 'rep', 0, 0, tiled=True)  35.9 us
    all_to_all x1, blocking collectives, local(): lax.all_to_all(chunks.reshape(ring, 8 * LIVE, 128), 'gz', 0, 0, tiled=True)  14.2 us
    ppermute x4, waiting for transfers between devices, local(): sums = sums + lax.ppermute(sums, 'gz', [(i, i ^ step) for i in range(ring)])  11.9 us
    ppermute x4, starting transfers between devices, local(): sums = sums + lax.ppermute(sums, 'gz', [(i, i ^ step) for i in range(ring)])  10.4 us
    ppermute x1, starting transfers between devices, local(): lax.ppermute(far, 'gz', [(i, (i + 1) % ring if i % 2 else (i - 1) % ring)...  5.92 us
    all_to_all x1, starting transfers between devices, local(): lax.all_to_all(out.reshape(reps, PER, DEPTH, 128), 'rep', 0, 0, tiled=True)  4.17 us
    all_to_all x1, waiting for transfers between devices, local(): lax.all_to_all(out.reshape(reps, PER, DEPTH, 128), 'rep', 0, 0, tiled=True)  3.79 us
    pallas_call x1, Pallas kernels, edges(): pl.pallas_call(edges_kernel, out_shape=[shape(2 * LIVE, ROWS, 128)] * 3 +...  2.36 us
  transfers between devices with their start and end apart: 7, of which 6 were waited for; matrix products, arithmetic and copies ran while one was open for 0% of the time, Pallas kernels for 0%

profile of v8, /device:TPU:2, one launch (start us, length us, event | category | flops | bytes accessed | tf_op | source)
XLA Modules:
  0.0 97.2 jit_solution(16808197287515611825)
XLA Ops:
  0.6 0.0 copy-start.5
  0.6 2.4 %edges.1 = (f32[6,32,128]{2,1,0:T(8,128)S(1)}, f32[6,32,128]{2,1,0:T(8,128)S(1)}, f32[6,32,128]{2,1,0:T(8,128)S(1)}, f32[3,128,128]{2,1,0:T(8,128)S(1)}, f32[128,128]{1,0:T(8,128)S(1)}) custom-call(s32[1]{0:T(128)S(6)} %mul.3.base_ref, s32[1]{0:T(128)} %bitcast.1.odd_ref, s32[192]{0:T(256)} %counts_ref.1, f32[6,128,128]{2,1,0:T(8,128)} %bitcast.33, ...), custom_call_target="tpu_custom_call" | custom-call | tf_op jit(solution)/shard_map/edges/pallas_call | solution.py:290
  3.0 5.9 %collective-permute-start = (f32[6,32,128]{2,1,0:T(8,128)S(1)}, f32[6,32,128]{2,1,0:T(8,128)S(1)}, u32[]{:S(2)}, u32[]{:S(2)}) collective-permute-start(f32[6,32,128]{2,1,0:T(8,128)S(1)} %get-tuple-element.19.far_own), channel_id=1, source_target_pairs={{0,15},{1,2},{2,1},{3,4},{4,3},{5,6},{6,5},{7,8},{8,7},{9,10},{10,... | collective-permute-start | bytes 294920 | tf_op jit(solution)/shard_map/ppermute | solution.py:378
  8.9 0.0 copy-start
  9.0 2.1 %collective-permute-start.1 = (f32[6,32,128]{2,1,0:T(8,128)S(1)}, f32[6,32,128]{2,1,0:T(8,128)S(1)}, u32[]{:S(2)}, u32[]{:S(2)}) collective-permute-start(f32[6,32,128]{2,1,0:T(8,128)S(1)} %get-tuple-element.20.near_own), channel_id=1, source_target_pairs={{0,1},{1,0},{2,3},{3,2},{4,5},{5,4},{6,7},{7,6},{8,9},{9,8},{10,11... | collective-permute-start | bytes 294920 | tf_op jit(solution)/shard_map/ppermute | solution.py:377
  11.0 0.0 copy-done.5
  11.0 0.1 copy.22
  11.1 0.0 copy-start.4
  11.2 0.0 copy-start.3
  11.2 0.6 copy-done.4
  11.8 0.0 copy-done.3
  11.9 0.0 copy-start.2
  11.9 0.3 plan.1
  12.2 0.4 collective-permute-done.far_in
  12.6 0.0 collective-permute-done.1.near_in
  12.6 0.0 copy-done
  12.6 0.0 copy-done.2
  12.6 0.8 sweeps.1
  13.4 0.0 copy-start.1
  13.4 14.2 %all_to_all.15.chunks = f32[16,24,128]{2,1,0:T(8,128)S(1)} all-to-all(f32[16,24,128]{2,1,0:T(8,128)S(1)} %bitcast.28), channel_id=1, replica_groups=mesh['rep'=32,'gz'=16] {'gz'}, dimensions={0} | all-to-all | bytes 393216 | tf_op jit(solution)/shard_map/all_to_all | solution.py:384
  27.6 0.0 copy-done.1
  27.6 1.0 %bins.1 = f32[416,128]{1,0:T(8,128)S(1)} custom-call(s32[1]{0:T(128)} %bitcast.me_ref, f32[16,24,128]{2,1,0:T(8,128)S(1)} %all_to_all.15.chunks, s32[128,128]{1,0:T(8,128)S(1)} %get-tuple-element.31.map_ref, s32[32,128]{1,0:T(8,128)S(1)} %get-tuple-element.32.wide, bf16[2,128,128]{2,1,0:T(8,128)(2,1)S(1)} %copy-done.1, f32[416,128]{1,0:T(8,128)S(1)} %get-tuple-element.33.old), custom_call_target="tpu_custom_call" | custom-call | tf_op jit(solution)/shard_map/bins/pallas_call | solution.py:335
  28.7 35.9 %all_to_all.16 = f32[32,13,1,128]{3,2,1,0:T(1,128)S(1)} all-to-all(f32[32,13,1,128]{3,2,1,0:T(1,128)S(1)} %bitcast.27), channel_id=1, replica_groups=mesh['rep'=32,'gz'=16] {'rep'}, dimensions={0} | all-to-all | bytes 425984 | tf_op jit(solution)/shard_map/all_to_all | solution.py:386
  64.6 1.4 %pick.1 = (f32[192,4,128]{2,1,0:T(4,128)}, f32[1,128]{1,0:T(1,128)S(1)}) custom-call(s32[192]{0:T(256)S(1)} %bitcast.31, f32[416,128]{1,0:T(8,128)S(1)} %bitcast.26), custom_call_target="tpu_custom_call" | custom-call | tf_op jit(solution)/shard_map/pick/pallas_call | solution.py:347
  66.0 4.2 %all-to-all-start.2 = ((f32[32,6,4,128]{3,2,1,0:T(4,128)}), f32[32,6,4,128]{3,2,1,0:T(4,128)S(1)}, u32[]{:S(2)}, u32[]{:S(2)}) async-start(f32[32,6,4,128]{3,2,1,0:T(4,128)} %bitcast.17), calls=%async_computation.2 | async-start | bytes 786432 | tf_op jit(solution)/shard_map/all_to_all | solution.py:388
  70.1 1.9 %collective-permute-start.2 = (f32[1,128]{1,0:T(1,128)S(1)}, f32[1,128]{1,0:T(1,128)S(1)}, u32[]{:S(2)}, u32[]{:S(2)}) collective-permute-start(f32[1,128]{1,0:T(1,128)S(1)} %get-tuple-element.35), channel_id=1, source_target_pairs={{0,1},{1,0},{2,3},{3,2},{4,5},{5,4},{6,7},{7,6},{8,9},{9,8},{10,11... | collective-permute-start | bytes 1544 | tf_op jit(solution)/shard_map/ppermute | solution.py:391
  72.1 1.1 %collective-permute-done.2 = f32[1,128]{1,0:T(1,128)S(1)} collective-permute-done((f32[1,128]{1,0:T(1,128)S(1)}, f32[1,128]{1,0:T(1,128)S(1)}, u32[]{:S(2)}, u32[]{:S(2)}) %collective-permute-start.2) | collective-permute-done | bytes 544 | tf_op jit(solution)/shard_map/ppermute | solution.py:391
  73.2 2.4 %collective-permute-start.3 = (f32[1,128]{1,0:T(1,128)S(1)}, f32[1,128]{1,0:T(1,128)S(1)}, u32[]{:S(2)}, u32[]{:S(2)}) collective-permute-start(f32[1,128]{1,0:T(1,128)S(1)} %add.14), channel_id=1, source_target_pairs={{0,2},{1,3},{2,0},{3,1},{4,6},{5,7},{6,4},{7,5},{8,10},{9,11},{10,... | collective-permute-start | bytes 1544 | tf_op jit(solution)/shard_map/ppermute | solution.py:391
  75.6 3.0 %collective-permute-done.3 = f32[1,128]{1,0:T(1,128)S(1)} collective-permute-done((f32[1,128]{1,0:T(1,128)S(1)}, f32[1,128]{1,0:T(1,128)S(1)}, u32[]{:S(2)}, u32[]{:S(2)}) %collective-permute-start.3) | collective-permute-done | bytes 544 | tf_op jit(solution)/shard_map/ppermute | solution.py:391
  78.6 3.2 %collective-permute-start.4 = (f32[1,128]{1,0:T(1,128)S(1)}, f32[1,128]{1,0:T(1,128)S(1)}, u32[]{:S(2)}, u32[]{:S(2)}) collective-permute-start(f32[1,128]{1,0:T(1,128)S(1)} %add.15), channel_id=1, source_target_pairs={{0,4},{1,5},{2,6},{3,7},{4,0},{5,1},{6,2},{7,3},{8,12},{9,13},{10,... | collective-permute-start | bytes 1544 | tf_op jit(solution)/shard_map/ppermute | solution.py:391
  81.8 3.8 %collective-permute-done.4 = f32[1,128]{1,0:T(1,128)S(1)} collective-permute-done((f32[1,128]{1,0:T(1,128)S(1)}, f32[1,128]{1,0:T(1,128)S(1)}, u32[]{:S(2)}, u32[]{:S(2)}) %collective-permute-start.4) | collective-permute-done | bytes 544 | tf_op jit(solution)/shard_map/ppermute | solution.py:391
  85.5 2.8 %collective-permute-start.5 = (f32[1,128]{1,0:T(1,128)S(1)}, f32[1,128]{1,0:T(1,128)S(1)}, u32[]{:S(2)}, u32[]{:S(2)}) collective-permute-start(f32[1,128]{1,0:T(1,128)S(1)} %add.16), channel_id=1, source_target_pairs={{0,8},{1,9},{2,10},{3,11},{4,12},{5,13},{6,14},{7,15},{8,0},{9,1},... | collective-permute-start | bytes 1544 | tf_op jit(solution)/shard_map/ppermute | solution.py:391
  88.3 4.1 %collective-permute-done.5 = f32[1,128]{1,0:T(1,128)S(1)} collective-permute-done((f32[1,128]{1,0:T(1,128)S(1)}, f32[1,128]{1,0:T(1,128)S(1)}, u32[]{:S(2)}, u32[]{:S(2)}) %collective-permute-start.5) | collective-permute-done | bytes 544 | tf_op jit(solution)/shard_map/ppermute | solution.py:391
  92.4 3.8 %all-to-all-done.2 = f32[32,6,4,128]{3,2,1,0:T(4,128)S(1)} async-done(((f32[32,6,4,128]{3,2,1,0:T(4,128)}), f32[32,6,4,128]{3,2,1,0:T(4,128)S(1)}, u32[]{:S(2)}, u32[]{:S(2)}) %all-to-all-start.2) | async-done | bytes 393248 | tf_op jit(solution)/shard_map/all_to_all | solution.py:388
  96.2 1.0 finish.1
  (5 shorter events, 0.0 us)
Async XLA Ops:
  0.6 10.4 %copy-start.5 = (s32[4,64,33]{1,0,2:T(4,128)S(1)}, s32[4,64,33]{1,0,2:T(4,128)}, u32[]{:S(2)}) copy-start(s32[4,64,33]{1,0,2:T(4,128)} %param.14) | copy-start | bytes 101380
  3.0 9.5 %collective-permute-start = (f32[6,32,128]{2,1,0:T(8,128)S(1)}, f32[6,32,128]{2,1,0:T(8,128)S(1)}, u32[]{:S(2)}, u32[]{:S(2)}) collective-permute-start(f32[6,32,128]{2,1,0:T(8,128)S(1)} %get-tuple-element.19.far_own), channel_id=1, source_target_pairs={{0,15},{1,2},{2,1},{3,4},{4,3},{5,6},{6,5},{7,8},{8,7},{9,10},{10,... | collective-permute-start | bytes 294920 | tf_op jit(solution)/shard_map/ppermute | solution.py:378
  8.9 3.6 %copy-start = (bf16[2,256,256]{2,1,0:T(8,128)(2,1)S(1)}, bf16[2,256,256]{2,1,0:T(8,128)(2,1)}, u32[]{:S(2)}) copy-start(bf16[2,256,256]{2,1,0:T(8,128)(2,1)} %constant.21.clone.along_x) | copy-start | bytes 786436
  9.0 3.6 %collective-permute-start.1 = (f32[6,32,128]{2,1,0:T(8,128)S(1)}, f32[6,32,128]{2,1,0:T(8,128)S(1)}, u32[]{:S(2)}, u32[]{:S(2)}) collective-permute-start(f32[6,32,128]{2,1,0:T(8,128)S(1)} %get-tuple-element.20.near_own), channel_id=1, source_target_pairs={{0,1},{1,0},{2,3},{3,2},{4,5},{5,4},{6,7},{7,6},{8,9},{9,8},{10,11... | collective-permute-start | bytes 294920 | tf_op jit(solution)/shard_map/ppermute | solution.py:377
  11.1 0.7 copy-start.4
  11.2 0.7 copy-start.3
  11.9 0.8 copy-start.2
  13.4 14.2 %copy-start.1 = (bf16[2,128,128]{2,1,0:T(8,128)(2,1)S(1)}, bf16[2,128,128]{2,1,0:T(8,128)(2,1)}, u32[]{:S(2)}) copy-start(bf16[2,128,128]{2,1,0:T(8,128)(2,1)} %constant.23.clone.along_z) | copy-start | bytes 196612
  66.0 30.3 %all-to-all-start.2 = ((f32[32,6,4,128]{3,2,1,0:T(4,128)}), f32[32,6,4,128]{3,2,1,0:T(4,128)S(1)}, u32[]{:S(2)}, u32[]{:S(2)}) async-start(f32[32,6,4,128]{3,2,1,0:T(4,128)} %bitcast.17), calls=%async_computation.2 | async-start | bytes 786432 | tf_op jit(solution)/shard_map/all_to_all | solution.py:388
  70.1 3.0 %collective-permute-start.2 = (f32[1,128]{1,0:T(1,128)S(1)}, f32[1,128]{1,0:T(1,128)S(1)}, u32[]{:S(2)}, u32[]{:S(2)}) collective-permute-start(f32[1,128]{1,0:T(1,128)S(1)} %get-tuple-element.35), channel_id=1, source_target_pairs={{0,1},{1,0},{2,3},{3,2},{4,5},{5,4},{6,7},{7,6},{8,9},{9,8},{10,11... | collective-permute-start | bytes 1544 | tf_op jit(solution)/shard_map/ppermute | solution.py:391
  73.2 5.4 %collective-permute-start.3 = (f32[1,128]{1,0:T(1,128)S(1)}, f32[1,128]{1,0:T(1,128)S(1)}, u32[]{:S(2)}, u32[]{:S(2)}) collective-permute-start(f32[1,128]{1,0:T(1,128)S(1)} %add.14), channel_id=1, source_target_pairs={{0,2},{1,3},{2,0},{3,1},{4,6},{5,7},{6,4},{7,5},{8,10},{9,11},{10,... | collective-permute-start | bytes 1544 | tf_op jit(solution)/shard_map/ppermute | solution.py:391
  78.6 6.9 %collective-permute-start.4 = (f32[1,128]{1,0:T(1,128)S(1)}, f32[1,128]{1,0:T(1,128)S(1)}, u32[]{:S(2)}, u32[]{:S(2)}) collective-permute-start(f32[1,128]{1,0:T(1,128)S(1)} %add.15), channel_id=1, source_target_pairs={{0,4},{1,5},{2,6},{3,7},{4,0},{5,1},{6,2},{7,3},{8,12},{9,13},{10,... | collective-permute-start | bytes 1544 | tf_op jit(solution)/shard_map/ppermute | solution.py:391
  85.5 6.9 %collective-permute-start.5 = (f32[1,128]{1,0:T(1,128)S(1)}, f32[1,128]{1,0:T(1,128)S(1)}, u32[]{:S(2)}, u32[]{:S(2)}) collective-permute-start(f32[1,128]{1,0:T(1,128)S(1)} %add.16), channel_id=1, source_target_pairs={{0,8},{1,9},{2,10},{3,11},{4,12},{5,13},{6,14},{7,15},{8,0},{9,1},... | collective-permute-start | bytes 1544 | tf_op jit(solution)/shard_map/ppermute | solution.py:391
